TPU v7x, 256 devices: a whole 4x4x8 slice. The times are simulated.
256 devices in a mesh: px: 32 (over y, z), py: 8 (over x, core).
Axes of the slice: x: 4, y: 4, z: 8, core: 2. Of those that a mesh axis runs over, the one named last changes fastest.
Arguments:
- solution: float32 [1, 8388608], P(None, ('px', 'py')), may hold values from -6 to 6
- residual: float32 [1, 8388608], P(None, ('px', 'py')), may hold values from -400 to 400
- direction: float32 [1, 8388608], P(None, ('px', 'py')), may hold values from -400 to 400
- offsets: float32 [3, 8388608], P(None, ('px', 'py')), may hold values from 0 to 1
- noise: float32 [8388608], P(('px', 'py')), may hold values from 0.3 to 3
- bin_cells: int32 [3, 65536], P(None, ('px', 'py')), may hold values from 1 to 253, as said below
- lengths: float32 [3], replicated, may hold values from 8 to 14
Outputs:
- new_solution: float32 [1, 8388608], P(None, ('px', 'py'))
- new_residual: float32 [1, 8388608], P(None, ('px', 'py'))
- new_direction: float32 [1, 8388608], P(None, ('px', 'py'))
Inputs may be any that keep to these rules, and one draw needn't show every extreme that they name: `bin_cells`: bin b is held by the device at position b // 256 of px+py (px major); its cell lies in that device's block of grid rows and columns, and its whole 4 x 4 x 4 stencil lies inside the grid.
All inputs are finite; a program needn't handle non-finite values.
Results may differ from a plain program's by a relative error of at most 0.000086.
Values sent between devices are 32-bit elements; how exact they have to be, the bound alone decides.
No kernel may reach another device: no remote copies, remote signals or barrier semaphores. Data moves between devices by JAX's collectives and lax.ppermute only.
A program may use at most 128 MiB of HBM per device.

v0:
```python
import math

import jax
import jax.numpy as jnp
from jax import lax
from jax.sharding import PartitionSpec as P

GRID_X = 128
GRID_Y = 256
GRID_Z = 256
BIN = 128


exact_precision = lax.Precision.HIGHEST


def extended_2(block, sides, width):
    for axis, dim in sides:
        count = lax.axis_size(axis)
        forward = [(i, i + 1) for i in range(count - 1)]
        backward = [(target, source) for source, target in forward]
        low = lax.ppermute(
            lax.slice_in_dim(block, block.shape[dim] - width, None, axis=dim), axis, forward
        )
        high = lax.ppermute(lax.slice_in_dim(block, 0, width, axis=dim), axis, backward)
        block = jnp.concatenate([low, block, high], axis=dim)
    return block


def cubic_weights(fraction):
    first_weight = ((-0.5 * fraction + 1.0) * fraction - 0.5) * fraction
    second_weight = (1.5 * fraction - 2.5) * fraction * fraction + 1.0
    third_weight = ((-1.5 * fraction + 2.0) * fraction + 0.5) * fraction
    fourth_weight = (0.5 * fraction - 0.5) * fraction * fraction
    return jnp.stack([first_weight, second_weight, third_weight, fourth_weight], axis=-1)


def stencil_weights(offsets_binned):
    along_rows = cubic_weights(offsets_binned[0])
    along_columns = cubic_weights(offsets_binned[1])
    along_depth = cubic_weights(offsets_binned[2])
    product = (
        along_rows[:, :, :, None, None]
        * along_columns[:, :, None, :, None]
        * along_depth[:, :, None, None, :]
    )
    return product.reshape(product.shape[0], product.shape[1], 64)


def stencil_steps():
    corner = jnp.arange(64, dtype=jnp.int32)
    return (corner // 16, corner // 4 % 4, corner % 4)


def spectrum_block(
    lengths, first_freq, second_freq, third_freq, first_size, second_size, third_size
):
    shaped_first = lengths[0] * jnp.sin(first_freq * (math.pi / first_size))
    shaped_second = lengths[1] * jnp.sin(second_freq * (math.pi / second_size))
    shaped_third = lengths[2] * jnp.sin(third_freq * (math.pi / third_size))
    denominator = (
        1.0
        + (shaped_first * shaped_first)[:, None, None]
        + (shaped_second * shaped_second)[None, :, None]
        + (shaped_third * shaped_third)[None, None, :]
    )
    return 2.0 * lengths[0] * lengths[1] * lengths[2] / (denominator * denominator)


def block_freqs(position, width):
    return (position * width + jnp.arange(width, dtype=jnp.int32)).astype(jnp.float32)


def dft_tables(count_in, count_out, length, factor):
    index_in = jnp.arange(count_in, dtype=jnp.int32)[:, None]
    index_out = jnp.arange(count_out, dtype=jnp.int32)[None, :]
    phase = index_in * index_out % length
    angle = phase.astype(jnp.float32) * (2.0 * math.pi / length)
    return (jnp.cos(angle) * factor, jnp.sin(angle) * factor)


def transform_axis(values, matrix, axis_number):
    letters = "abcd"
    result = letters[:axis_number] + "e" + letters[axis_number + 1 :]
    formula = letters + "," + letters[axis_number] + "e->" + result
    return jnp.einsum(formula, values, matrix, precision=exact_precision)


def forward_real(values, axis_number, kept, length):
    count = values.shape[axis_number]
    cosine_table, sine_table = dft_tables(count, kept, length, 1.0)
    live = (jnp.arange(kept, dtype=jnp.int32) < length).astype(jnp.float32)[None, :]
    return (
        transform_axis(values, cosine_table * live, axis_number),
        -transform_axis(values, sine_table * live, axis_number),
    )


def forward_complex(complex_pair, axis_number):
    real_part, imag_part = complex_pair
    length = real_part.shape[axis_number]
    cosine_table, sine_table = dft_tables(length, 2 * length, 2 * length, 1.0)
    new_real = transform_axis(real_part, cosine_table, axis_number) + transform_axis(
        imag_part, sine_table, axis_number
    )
    new_imag = transform_axis(imag_part, cosine_table, axis_number) - transform_axis(
        real_part, sine_table, axis_number
    )
    return (new_real, new_imag)


def inverse_complex(complex_pair, axis_number, keep_count):
    real_part, imag_part = complex_pair
    length = real_part.shape[axis_number]
    cosine_table, sine_table = dft_tables(length, keep_count, length, 1.0 / length)
    new_real = transform_axis(real_part, cosine_table, axis_number) - transform_axis(
        imag_part, sine_table, axis_number
    )
    new_imag = transform_axis(real_part, sine_table, axis_number) + transform_axis(
        imag_part, cosine_table, axis_number
    )
    return (new_real, new_imag)


def inverse_real(complex_pair, axis_number, keep_count, length):
    real_part, imag_part = complex_pair
    count = real_part.shape[axis_number]
    cosine_table, sine_table = dft_tables(count, keep_count, length, 1.0 / length)
    slot = jnp.arange(count, dtype=jnp.int32)[:, None]
    slot_weight = (slot < length).astype(jnp.float32)
    return transform_axis(real_part, cosine_table * slot_weight, axis_number) - transform_axis(
        imag_part, sine_table * slot_weight, axis_number
    )


def fold_rims(values, axis_number, interior):
    own_cells = lax.slice_in_dim(values, 3, interior + 3, axis=axis_number)
    low_rim = lax.slice_in_dim(values, 0, 2, axis=axis_number)
    high_rim = lax.slice_in_dim(values, interior + 5, interior + 6, axis=axis_number)
    low_widths = [(0, 0)] * 4
    low_widths[axis_number] = (0, interior - 2)
    high_widths = [(0, 0)] * 4
    high_widths[axis_number] = (interior - 1, 0)
    return own_cells + jnp.pad(low_rim, low_widths) + jnp.pad(high_rim, high_widths)


def on_device(solution, residual, direction, offsets, noise, bin_cells, lengths):
    probes, point_count = direction.shape
    bin_count = bin_cells.shape[1]
    rows_dev = GRID_X // lax.axis_size("px")
    columns_dev = GRID_Y // lax.axis_size("py")
    row_index = lax.axis_index("px")
    column_index = lax.axis_index("py")
    weights = stencil_weights(offsets.reshape(3, bin_count, BIN))
    step_rows, step_columns, step_depth = stencil_steps()
    local_rows = bin_cells[0][:, None] - row_index * rows_dev + step_rows
    local_columns = bin_cells[1][:, None] - column_index * columns_dev + step_columns
    depth_cells = bin_cells[2][:, None] - 1 + step_depth
    patches = jnp.einsum(
        "rnt,ntc->rnc",
        direction.reshape(probes, bin_count, BIN),
        weights,
        precision=exact_precision,
    )
    spread_index = (local_rows * (columns_dev + 3) + local_columns) * GRID_Z + depth_cells
    spread = (
        jnp.zeros((probes, (rows_dev + 3) * (columns_dev + 3) * GRID_Z), jnp.float32)
        .at[:, spread_index]
        .add(patches)
    )
    spread = spread.reshape(probes, rows_dev + 3, columns_dev + 3, GRID_Z)
    bordered = extended_2(spread, (("px", 1), ("py", 2)), 2)
    gridded = fold_rims(fold_rims(bordered, 1, rows_dev), 2, columns_dev)
    depth_length = 2 * GRID_Z - 1
    depth_slots = 2 * GRID_Z
    real_part, imag_part = forward_real(gridded, 3, depth_slots, depth_length)
    spectrum = spectrum_block(
        lengths,
        jnp.arange(2 * GRID_X).astype(jnp.float32),
        block_freqs(row_index, 2 * GRID_Y // lax.axis_size("px")),
        block_freqs(column_index, depth_slots // lax.axis_size("py")),
        2 * GRID_X,
        2 * GRID_Y,
        depth_length,
    )
    real_part, imag_part = forward_complex(
        (
            lax.all_to_all(real_part, "py", split_axis=3, concat_axis=2, tiled=True),
            lax.all_to_all(imag_part, "py", split_axis=3, concat_axis=2, tiled=True),
        ),
        2,
    )
    cycle_real, cycle_imag = forward_complex(
        (
            lax.all_to_all(real_part, "px", split_axis=2, concat_axis=1, tiled=True),
            lax.all_to_all(imag_part, "px", split_axis=2, concat_axis=1, tiled=True),
        ),
        1,
    )
    real_part, imag_part = inverse_complex(
        (cycle_real * spectrum, cycle_imag * spectrum), 1, GRID_X
    )
    real_part, imag_part = inverse_complex(
        (
            lax.all_to_all(real_part, "px", split_axis=1, concat_axis=2, tiled=True),
            lax.all_to_all(imag_part, "px", split_axis=1, concat_axis=2, tiled=True),
        ),
        2,
        GRID_Y,
    )
    covaried = inverse_real(
        (
            lax.all_to_all(real_part, "py", split_axis=2, concat_axis=3, tiled=True),
            lax.all_to_all(imag_part, "py", split_axis=2, concat_axis=3, tiled=True),
        ),
        3,
        GRID_Z,
        depth_length,
    )
    extended = extended_2(covaried, (("px", 1), ("py", 2)), 2)
    gather_index = ((local_rows + 1) * (columns_dev + 4) + local_columns + 1) * GRID_Z + depth_cells
    gathered = extended.reshape(probes, (rows_dev + 4) * (columns_dev + 4) * GRID_Z)[
        :, gather_index
    ]
    interpolated = jnp.einsum("rnc,ntc->rnt", gathered, weights, precision=exact_precision).reshape(
        probes, point_count
    )
    operator_image = interpolated + noise[None, :] * direction
    old_norm = lax.psum(jnp.sum(residual * residual, axis=1), ("px", "py"))
    curvature = lax.psum(jnp.sum(direction * operator_image, axis=1), ("px", "py"))
    step_size = old_norm / curvature
    new_residual = residual - step_size[:, None] * operator_image
    new_norm = lax.psum(jnp.sum(new_residual * new_residual, axis=1), ("px", "py"))
    new_solution = solution + step_size[:, None] * direction
    new_direction = new_residual + (new_norm / old_norm)[:, None] * direction
    return (new_solution, new_residual, new_direction)


def solution(mesh):
    return jax.shard_map(
        on_device,
        mesh=mesh,
        in_specs=(
            P(None, ("px", "py")),
            P(None, ("px", "py")),
            P(None, ("px", "py")),
            P(None, ("px", "py")),
            P(("px", "py")),
            P(None, ("px", "py")),
            P(),
        ),
        out_specs=(P(None, ("px", "py")), P(None, ("px", "py")), P(None, ("px", "py"))),
        check_vma=False,
    )
```

profile of v0, /device:TPU:1, one launch (start us, length us, event | category | flops | bytes accessed | tf_op | source)
XLA Modules:
  0.0 610.4 jit_solution(3539328672558870639)
XLA Ops:
  5.2 3.2 copy-done
  8.4 17.7 %fusion.2 = f32[256,1,64]{2,1,0:T(1,128)S(1)} fusion(f32[256,128,64]{1,0,2:T(8,128)S(1)} %bitcast.192, f32[1,32768]{1,0:T(1,128)S(1)} %copy-done.1), kind=kOutput, calls=%fused_computation.5 | convolution fusion | flops 25165824 | bytes 8585216 | tf_op jit(solution)/shard_map/rnt,ntc->rnc/dot_general | solution.py:159
  26.2 105.5 %scatter_custom_fusion = f32[62720]{0:T(1024)S(1)} fusion(s32[16384]{0:T(1024)S(1)} %reshape.1015, f32[16384]{0:T(1024)S(1)} %reshape.1017, f32[]{:T(128)} %constant.147.clone.1), kind=kCustom, calls=%fused_computation.167 | custom fusion | flops 16384 | bytes 250884 | tf_op jit(solution)/shard_map/scatter-add | solution.py:169
  131.8 4.4 collective-permute-start
  137.7 3.9 collective-permute-done.1
  141.6 4.9 collective-permute-start.2
  146.5 1.9 collective-permute-start.3
  148.4 3.2 collective-permute-done.3
  151.8 2.5 convolution_bitcast_fusion.1
  156.1 4.3 all-to-all-start
  160.5 2.5 fusion.4
  164.8 2.1 all-to-all-done
  166.9 4.4 all-to-all-start.1
  174.1 2.9 fusion.67
  180.2 2.9 fusion.63
  185.3 11.1 %all-to-all-start.3 = ((f32[32,1,4096]{2,1,0:T(1,128)}), f32[32,1,4096]{2,1,0:T(1,128)S(1)}, u32[]{:S(2)}, u32[]{:S(2)}) async-start(f32[32,1,4096]{2,1,0:T(1,128)} %reshape.1078), calls=%async_computation.3 | async-start | bytes 1048576 | tf_op jit(solution)/shard_map/all_to_all | solution.py:196
  197.1 2.9 fusion.65
  200.0 3.8 fusion.69
  206.1 4.4 all-to-all-done.3
  210.4 8.4 %all-to-all-start.2 = ((f32[32,1,4096]{2,1,0:T(1,128)}), f32[32,1,4096]{2,1,0:T(1,128)S(1)}, u32[]{:S(2)}, u32[]{:S(2)}) async-start(f32[32,1,4096]{2,1,0:T(1,128)} %reshape.1076), calls=%async_computation.2 | async-start | bytes 1048576 | tf_op jit(solution)/shard_map/all_to_all | solution.py:195
  223.0 1.9 reduce.5
  227.7 2.5 fusion.124
  230.2 1.9 all-to-all-done.2
  232.1 1.9 reduce.6
  247.2 8.1 %all-to-all-start.5 = ((f32[32,1,4096]{2,1,0:T(1,128)}), f32[32,1,4096]{2,1,0:T(1,128)}, u32[]{:S(2)}, u32[]{:S(2)}) async-start(f32[32,1,4096]{2,1,0:T(1,128)} %reshape.1082), calls=%async_computation.5 | async-start | bytes 1048576 | tf_op jit(solution)/shard_map/all_to_all | solution.py:206
  260.3 7.9 %all-to-all-done.5 = f32[32,1,4096]{2,1,0:T(1,128)} async-done(((f32[32,1,4096]{2,1,0:T(1,128)}), f32[32,1,4096]{2,1,0:T(1,128)}, u32[]{:S(2)}, u32[]{:S(2)}) %all-to-all-start.5) | async-done | bytes 524320 | tf_op jit(solution)/shard_map/all_to_all | solution.py:206
  268.2 8.8 %all-to-all-start.4 = ((f32[32,1,4096]{2,1,0:T(1,128)}), f32[32,1,4096]{2,1,0:T(1,128)S(1)}, u32[]{:S(2)}, u32[]{:S(2)}) async-start(f32[32,1,4096]{2,1,0:T(1,128)} %reshape.1080), calls=%async_computation.4 | async-start | bytes 1048576 | tf_op jit(solution)/shard_map/all_to_all | solution.py:205
  277.0 2.9 reduce.8
  280.8 3.3 fusion.47
  284.1 3.3 fusion.50
  287.4 2.4 all-to-all-done.4
  292.5 2.6 fusion.49
  295.1 3.0 fusion.48
  299.6 9.7 %all-to-all-start.7 = ((f32[8,1,8192]{2,1,0:T(1,128)}), f32[8,1,8192]{2,1,0:T(1,128)S(1)}, u32[]{:S(2)}, u32[]{:S(2)}) async-start(f32[8,1,8192]{2,1,0:T(1,128)} %reshape.1086), calls=%async_computation.7 | async-start | bytes 524288 | tf_op jit(solution)/shard_map/all_to_all | solution.py:214
  310.7 5.0 all-to-all-done.7
  315.7 4.4 all-to-all-start.6
  322.3 4.3 all-to-all-done.6
  328.7 2.5 fusion.17
  331.2 2.5 fusion.5
  333.8 3.7 collective-permute-start.4
  338.8 3.7 collective-permute-done.5
  342.5 4.6 collective-permute-start.6
  347.1 1.9 collective-permute-start.7
  349.9 2.2 collective-permute-done.7
  352.2 90.7 %gather_fusion = f32[16384]{0:T(1024)S(1)} fusion(f32[73728]{0:T(1024)S(1)} %reshape.1001, s32[16384]{0:T(1024)S(1)} %broadcast_clamp_fusion), kind=kCustom, calls=%fused_computation | custom fusion | bytes 196608 | tf_op jit(solution)/shard_map/gather | solution.py:222
  443.1 15.5 %multiply_reduce_fusion.1 = (f32[]{:T(128)}, f32[1,32768]{1,0:T(1,128)S(1)}) fusion(f32[1,32768]{1,0:T(1,128)S(1)} %copy-done.1, f32[1,32768]{1,0:T(1,128)S(1)} %bitcast.257, f32[256,64,1]{1,2,0:T(1,128)S(1)} %bitcast.236, f32[256,128,64]{1,0,2:T(8,128)} %bitcast.193), kind=kOutput, calls=%fused_computation.151 | convolution fusion | flops 25296896 | bytes 8847364 | tf_op jit(solution)/shard_map/rnc,ntc->rnt/dot_general | solution.py:225
  458.5 74.6 %all-reduce.2 = (f32[1]{0:T(128)}, f32[1]{0:T(128)}) all-reduce(f32[1]{0:T(128)} %bitcast, f32[1]{0:T(128)} %bitcast.103), channel_id=1, replica_groups=mesh['px'=32,'py'=8] {'px','py'}, use_global_device_ids=true, to_apply=%region_1.2 | all-reduce | flops 2 | bytes 16 | tf_op jit(solution)/shard_map/psum | solution.py:229
  535.3 72.7 %psum.23 = f32[1]{0:T(128)} all-reduce(f32[1]{0:T(128)} %bitcast.105), channel_id=1, replica_groups=mesh['px'=32,'py'=8] {'px','py'}, use_global_device_ids=true, to_apply=%region_6.7 | all-reduce | flops 1 | bytes 8 | tf_op jit(solution)/shard_map/psum | solution.py:233
  (134 shorter events, 59.0 us)
Async XLA Ops:
  3.8 4.6 copy-start.1
  5.2 3.2 copy-start
  5.2 146.5 %copy-start.10 = (pred[4]{0:T(512)(128)(4,1)S(1)}, pred[4]{0:T(512)(128)(4,1)}, u32[]{:S(2)}) copy-start(pred[4]{0:T(512)(128)(4,1)} %constant.176.clone.1) | copy-start | bytes 16
  5.2 146.6 %copy-start.11 = (pred[32]{0:T(512)(128)(4,1)S(1)}, pred[32]{0:T(512)(128)(4,1)}, u32[]{:S(2)}) copy-start(pred[32]{0:T(512)(128)(4,1)} %constant.177.clone.1) | copy-start | bytes 100
  131.8 5.8 collective-permute-start
  136.2 5.4 collective-permute-start.1
  141.6 6.9 %collective-permute-start.2 = (f32[1,11,2,256]{3,2,1,0:T(2,128)S(1)}, f32[1,11,2,256]{3,2,1,0:T(2,128)S(1)}, u32[]{:S(2)}, u32[]{:S(2)}) collective-permute-start(f32[1,11,2,256]{3,2,1,0:T(2,128)S(1)} %get-tuple-element.10), channel_id=1, source_target_pairs={{0,1},{1,2},{2,3},{3,4},{4,5},{5,6},{6,7},{8,9},{9,10},{10,11},{11... | collective-permute-start | bytes 67592 | tf_op jit(solution)/shard_map/ppermute | solution.py:22
  146.5 5.1 collective-permute-start.3
  156.1 10.8 %all-to-all-start = ((f32[8,1,8192]{2,1,0:T(1,128)}), f32[8,1,8192]{2,1,0:T(1,128)S(1)}, u32[]{:S(2)}, u32[]{:S(2)}) async-start(f32[8,1,8192]{2,1,0:T(1,128)} %reshape.1072), calls=%async_computation | async-start | bytes 524288 | tf_op jit(solution)/shard_map/all_to_all | solution.py:188
  166.9 10.9 %all-to-all-start.1 = ((f32[8,1,8192]{2,1,0:T(1,128)}), f32[8,1,8192]{2,1,0:T(1,128)S(1)}, u32[]{:S(2)}, u32[]{:S(2)}) async-start(f32[8,1,8192]{2,1,0:T(1,128)} %reshape.1074), calls=%async_computation.1 | async-start | bytes 524288 | tf_op jit(solution)/shard_map/all_to_all | solution.py:189
  173.6 22.8 %copy-start.9 = (f32[3]{0:T(128)S(1)}, f32[3]{0:T(128)}, u32[]{:S(2)}) copy-start(f32[3]{0:T(128)} %param.13) | copy-start | bytes 40
  180.1 5.2 copy-start.5
  185.3 25.1 %all-to-all-start.3 = ((f32[32,1,4096]{2,1,0:T(1,128)}), f32[32,1,4096]{2,1,0:T(1,128)S(1)}, u32[]{:S(2)}, u32[]{:S(2)}) async-start(f32[32,1,4096]{2,1,0:T(1,128)} %reshape.1078), calls=%async_computation.3 | async-start | bytes 1048576 | tf_op jit(solution)/shard_map/all_to_all | solution.py:196
  210.4 21.7 %all-to-all-start.2 = ((f32[32,1,4096]{2,1,0:T(1,128)}), f32[32,1,4096]{2,1,0:T(1,128)S(1)}, u32[]{:S(2)}, u32[]{:S(2)}) async-start(f32[32,1,4096]{2,1,0:T(1,128)} %reshape.1076), calls=%async_computation.2 | async-start | bytes 1048576 | tf_op jit(solution)/shard_map/all_to_all | solution.py:195
  247.2 21.0 %all-to-all-start.5 = ((f32[32,1,4096]{2,1,0:T(1,128)}), f32[32,1,4096]{2,1,0:T(1,128)}, u32[]{:S(2)}, u32[]{:S(2)}) async-start(f32[32,1,4096]{2,1,0:T(1,128)} %reshape.1082), calls=%async_computation.5 | async-start | bytes 1048576 | tf_op jit(solution)/shard_map/all_to_all | solution.py:206
  268.2 21.5 %all-to-all-start.4 = ((f32[32,1,4096]{2,1,0:T(1,128)}), f32[32,1,4096]{2,1,0:T(1,128)S(1)}, u32[]{:S(2)}, u32[]{:S(2)}) async-start(f32[32,1,4096]{2,1,0:T(1,128)} %reshape.1080), calls=%async_computation.4 | async-start | bytes 1048576 | tf_op jit(solution)/shard_map/all_to_all | solution.py:205
  287.4 10.7 %copy-start.6 = (f32[256,256]{0,1:S(1)}, f32[256,256]{0,1}, u32[]{:S(2)}) copy-start(f32[256,256]{0,1} %fusion.47) | copy-start | bytes 786436
  287.4 21.9 %copy-start.4 = (f32[256,256]{0,1:S(1)}, f32[256,256]{0,1}, u32[]{:S(2)}) copy-start(f32[256,256]{0,1} %fusion.50) | copy-start | bytes 786436
  298.3 50.7 %copy-start.3 = (f32[1,32768]{1,0:T(1,128)S(1)}, f32[1,32768]{1,0:T(1,128)}, u32[]{:S(2)}) copy-start(f32[1,32768]{1,0:T(1,128)} %param.8) | copy-start | bytes 393220
  299.6 16.2 %all-to-all-start.7 = ((f32[8,1,8192]{2,1,0:T(1,128)}), f32[8,1,8192]{2,1,0:T(1,128)S(1)}, u32[]{:S(2)}, u32[]{:S(2)}) async-start(f32[8,1,8192]{2,1,0:T(1,128)} %reshape.1086), calls=%async_computation.7 | async-start | bytes 524288 | tf_op jit(solution)/shard_map/all_to_all | solution.py:214
  315.7 10.9 %all-to-all-start.6 = ((f32[8,1,8192]{2,1,0:T(1,128)}), f32[8,1,8192]{2,1,0:T(1,128)S(1)}, u32[]{:S(2)}, u32[]{:S(2)}) async-start(f32[8,1,8192]{2,1,0:T(1,128)} %reshape.1084), calls=%async_computation.6 | async-start | bytes 524288 | tf_op jit(solution)/shard_map/all_to_all | solution.py:213
  333.8 5.0 collective-permute-start.4
  337.5 5.0 collective-permute-start.5
  342.5 7.4 %collective-permute-start.6 = (f32[1,8,2,256]{3,2,1,0:T(2,128)S(1)}, f32[1,8,2,256]{3,2,1,0:T(2,128)S(1)}, u32[]{:S(2)}, u32[]{:S(2)}) collective-permute-start(f32[1,8,2,256]{3,2,1,0:T(2,128)S(1)} %get-tuple-element.14), channel_id=1, source_target_pairs={{0,1},{1,2},{2,3},{3,4},{4,5},{5,6},{6,7},{8,9},{9,10},{10,11},{11... | collective-permute-start | bytes 49160 | tf_op jit(solution)/shard_map/ppermute | solution.py:22
  347.1 5.1 collective-permute-start.7
  352.2 90.8 %copy-start.7 = (f32[32768]{0:T(1024)S(1)}, f32[32768]{0:T(1024)}, u32[]{:S(2)}) copy-start(f32[32768]{0:T(1024)} %param.11) | copy-start | bytes 393220
  442.9 166.4 %copy-start.8 = (f32[1,32768]{1,0:T(1,128)S(1)}, f32[1,32768]{1,0:T(1,128)}, u32[]{:S(2)}) copy-start(f32[1,32768]{1,0:T(1,128)} %param.7) | copy-start | bytes 393220
  535.3 74.9 %copy-start.2 = (f32[1,32768]{1,0:T(1,128)}, f32[1,32768]{1,0:T(1,128)S(1)}, u32[]{:S(2)}) copy-start(f32[1,32768]{1,0:T(1,128)S(1)} %get-tuple-element.6) | copy-start | bytes 393220
where the time goes:
time: 621 us; the launch traced here: 610 us
  blocking collectives  147 us (24%)
  other arithmetic  130 us (21%)
  local copies, waits for them, and re-layouts  121 us (19%)
  starting transfers between devices  82.9 us (13%)
  matrix products  81 us (13%)
  waiting for transfers between devices  41.9 us (7%)
  between operations  6.45 us (1%)
    scatter-add x1, other arithmetic, on_device(): spread = jnp.zeros((probes, (rows_dev + 3) * (columns_dev + 3) * GRID_Z),...  105 us
    gather x1, local copies, waits for them, and re-layouts, on_device(): extended.reshape(probes, (rows_dev + 4) * (columns_dev + 4) * GRID_Z)  90.7 us
    psum x1, blocking collectives, on_device(): old_norm = lax.psum(jnp.sum(residual * residual, axis=1), ('px', 'py'))  74.6 us
    psum x1, blocking collectives, on_device(): lax.psum(jnp.sum(new_residual * new_residual, axis=1), ('px', 'py'))  72.7 us
    unnamed x16, matrix products  37.8 us
    unnamed x42, local copies, waits for them, and re-layouts  19 us
    dot_general x1, matrix products, on_device(): jnp.einsum('rnt,ntc->rnc', direction.reshape(probes, bin_count, BIN), wei...  17.7 us
    ppermute x4, starting transfers between devices, extended_2(): lax.ppermute(lax.slice_in_dim(block, block.shape[dim] - width, None, axis...  17.5 us
  transfers between devices with their start and end apart: 16, of which 13 were waited for; matrix products, arithmetic and copies ran while one was open for 8% of the time, Pallas kernels for 0%

commit v1 on v0

v1 whole, which is shorter than its diff:
```python
import math

import jax
import jax.numpy as jnp
import ml_dtypes
import numpy as np
from jax import lax
from jax.experimental import pallas as pl
from jax.experimental.pallas import tpu as pltpu
from jax.sharding import PartitionSpec as P

GRID_X, GRID_Y, GRID_Z = 128, 256, 256
BIN = 128
N_PX, N_PY = 32, 8
DEVICES = N_PX * N_PY
ROWS, COLUMNS = GRID_X // N_PX, GRID_Y // N_PY
SPAN_X, SPAN_Y = ROWS + 3, COLUMNS + 3
CELLS = 256
M_X, M_Y, M_Z = 2 * GRID_X, 2 * GRID_Y, 2 * GRID_Z - 1
BINS = 256
GROUP = 32
GROUPS = BINS // GROUP
PAIRS = GROUP * 16
BLOCK_X, BLOCK_Y = M_X // ROWS, M_Y // COLUMNS
CHUNKS = 3
PER_CHUNK = (BLOCK_X // 2 + 1) // CHUNKS
CHUNK = PER_CHUNK * BLOCK_Y

f32, bf16 = jnp.float32, jnp.bfloat16


def halves(table):
    table = np.asarray(table, np.float64)
    high = table.astype(np.float32).astype(ml_dtypes.bfloat16)
    low = (table - high.astype(np.float64)).astype(np.float32).astype(ml_dtypes.bfloat16)
    return high, low


def depth_tables():
    freq = np.arange(GRID_Z)[:, None]
    depth = np.arange(GRID_Z)[None, :]
    angle = 2 * np.pi * (freq * depth % M_Z) / M_Z
    forward = np.concatenate([np.cos(angle), -np.sin(angle)], 0)
    twice = np.where(freq == 0, 1.0, 2.0) / M_Z
    inverse = np.concatenate([np.cos(angle) * twice, -np.sin(angle) * twice], 0).T
    return halves(forward) + halves(inverse)


def plane_tables():
    kx = np.arange(BLOCK_X // 2 + 1)
    ky = np.arange(BLOCK_Y)
    source = np.arange(DEVICES)
    px, py = source // N_PY, source % N_PY
    phase = (kx[:, None, None] * px / BLOCK_X + ky[None, :, None] * py / BLOCK_Y) * 2 * np.pi
    phase = phase.reshape(CHUNKS, CHUNK, DEVICES)
    blocks = np.concatenate([np.cos(phase), np.sin(phase)], 1)
    lane = np.arange(CELLS)
    live = lane < SPAN_X * SPAN_Y
    a, e = lane // SPAN_Y - 1, lane % SPAN_Y - 1
    twist = 2 * np.pi * (kx[:, None, None] * a / M_X + ky[None, :, None] * e / M_Y)
    twist = twist.reshape(-1, CELLS)
    out = np.arange(ROWS * COLUMNS)
    high_x, high_y = out // COLUMNS, out % COLUMNS
    inner = 2 * np.pi * (a[:, None] * high_x[None, :] / ROWS + e[:, None] * high_y[None, :] / COLUMNS)
    c, s = np.cos(inner) * live[:, None], np.sin(inner) * live[:, None]
    inner_forward = np.block([[c, -s], [s, c]])
    inner_inverse = np.block([[c.T, s.T], [-s.T, c.T]])
    full_x = BLOCK_X * high_x[None, :]
    full_y = BLOCK_Y * high_y[None, :]
    sine_x = [np.sin(np.pi * (sign * kx[:, None] + full_x) / M_X) ** 2 for sign in (1, -1)]
    sine_y = [np.sin(np.pi * (sign * ky[:, None] + full_y) / M_Y) ** 2 for sign in (1, -1)]
    scale = 1.0 / (M_X * M_Y)
    weight = np.where((kx == 0) | (kx == BLOCK_X // 2), 0.0, scale)[:, None] * np.ones((1, ROWS * COLUMNS))
    return dict(
        blocks=halves(blocks),
        blocks_back=halves(blocks.transpose(0, 2, 1)),
        inner=halves(inner_forward),
        inner_back=halves(inner_inverse),
        twist=(np.cos(twist).astype(np.float32), (-np.sin(twist)).astype(np.float32)),
        sine_x=[t.astype(np.float32) for t in sine_x],
        sine_y=[t.astype(np.float32) for t in sine_y],
        weight=weight.astype(np.float32),
    )


def split(values):
    high = values.astype(bf16)
    return high, (values - high.astype(f32)).astype(bf16)


def dot(a, b):
    return jnp.dot(a, b, preferred_element_type=f32)


def dot_nt(a, b):
    return lax.dot_general(a, b, (((1,), (1,)), ((), ())), preferred_element_type=f32)


def dot3(a, b, mul=dot):
    return mul(a[0], b[0]) + mul(a[0], b[1]) + mul(a[1], b[0])


def cubic_weights(t):
    return (
        ((-0.5 * t + 1.0) * t - 0.5) * t,
        (1.5 * t - 2.5) * t * t + 1.0,
        ((-1.5 * t + 2.0) * t + 0.5) * t,
        (0.5 * t - 0.5) * t * t,
    )


def one_hot(hit):
    return jnp.where(hit, 1.0, 0.0).astype(bf16)


def iota(shape, dim):
    return lax.broadcasted_iota(jnp.int32, shape, dim)


def stencil_cells(base):
    shift = iota((GROUP, CELLS), 1) - base
    return jnp.concatenate([one_hot(shift == a * SPAN_Y + e) for a in range(4) for e in range(4)], 0)


def same_bin(shape):
    return ((iota(shape, 0) ^ iota(shape, 1)) & (GROUP - 1)) == 0


def group_slice(g, size=GROUP):
    return pl.ds(pl.multiple_of(g * size, size), size)


def spread_kernel(direction, offsets, places, depth_row, forward_hi, forward_lo, out, q_hi, q_lo):
    def group(g, _):
        bins = group_slice(g)
        wx = cubic_weights(offsets[0, bins, :])
        wy = cubic_weights(offsets[1, bins, :])
        wz = cubic_weights(offsets[2, bins, :])
        d = direction[bins, :]
        wx = [w * d for w in wx]
        columns = split(jnp.concatenate([x * y for x in wx for y in wy], 0))
        depths = split(jnp.concatenate(wz, 0))
        patches = dot3(depths, columns, dot_nt)
        patches = split(jnp.where(same_bin((4 * GROUP, PAIRS)), patches, 0.0))
        cells = stencil_cells(places[bins, 0:1])
        placed = split(dot(patches[0], cells) + dot(patches[1], cells))
        rows = group_slice(g, 4 * GROUP)
        q_hi[rows, :] = placed[0]
        q_lo[rows, :] = placed[1]
        return 0

    lax.fori_loop(0, GROUPS, group, 0)
    at_depth = one_hot(iota((GRID_Z, 4 * BINS), 0) == depth_row[...])
    gridded = split(dot(at_depth, q_hi[...]) + dot(at_depth, q_lo[...]))
    transformed = dot3((forward_hi[...], forward_lo[...]), gridded)
    for part in range(2):
        for half in range(2):
            out[pl.ds(2 * part + half, GRID_Z, stride=4), :] = transformed[
                part * GRID_Z : (part + 1) * GRID_Z, half * 128 : (half + 1) * 128
            ]


def plane_kernel(
    scalars, received, blocks_hi, blocks_lo, back_hi, back_lo, inner_hi, inner_lo, inback_hi, inback_lo,
    twist_re, twist_im, sx_a, sx_b, sy_a, sy_b, weight_b,
    out, r_hi, r_lo, wide, m_hi, m_lo, narrow, g_hi, g_lo, total,
):
    for j in range(4):
        hi, lo = split(received[pl.ds(j, DEVICES, stride=4), :])
        r_hi[:, 128 * j : 128 * (j + 1)] = hi
        r_lo[:, 128 * j : 128 * (j + 1)] = lo
    total[...] = jnp.zeros_like(total)
    scale_x, scale_y, rest, factor = scalars[0], scalars[1], scalars[2], scalars[3]
    factor_a = factor * (1.0 / (M_X * M_Y))

    def chunk(c, _):
        wide[...] = dot3((blocks_hi[c], blocks_lo[c]), (r_hi[...], r_lo[...]))

        def twisted(j, _):
            top = group_slice(j, BLOCK_Y)
            bottom = pl.ds(pl.multiple_of(CHUNK + j * BLOCK_Y, BLOCK_Y), BLOCK_Y)
            table = pl.ds(pl.multiple_of(c * CHUNK + j * BLOCK_Y, BLOCK_Y), BLOCK_Y)
            tr, ti = twist_re[table, :], twist_im[table, :]
            cre, cim = wide[top, :CELLS], wide[top, CELLS:]
            sre, sim = wide[bottom, :CELLS], wide[bottom, CELLS:]
            ur, ui, vr, vi = cre + sim, cim - sre, cre - sim, cim + sre
            for rows, re, im in (
                (top, ur * tr - ui * ti, ur * ti + ui * tr),
                (bottom, vr * tr + vi * ti, vi * tr - vr * ti),
            ):
                m_hi[rows, :CELLS], m_lo[rows, :CELLS] = split(re)
                m_hi[rows, CELLS:], m_lo[rows, CELLS:] = split(im)
            return 0

        lax.fori_loop(0, PER_CHUNK, twisted, 0, unroll=True)
        narrow[...] = dot3((m_hi[...], m_lo[...]), (inner_hi[...], inner_lo[...]))

        def filtered(j, _):
            top = group_slice(j, BLOCK_Y)
            bottom = pl.ds(pl.multiple_of(CHUNK + j * BLOCK_Y, BLOCK_Y), BLOCK_Y)
            freq = pl.ds(c * PER_CHUNK + j, 1)
            for rows, sx, sy, weight in (
                (top, sx_a, sy_a, factor_a),
                (bottom, sx_b, sy_b, factor * weight_b[freq, :]),
            ):
                denominator = (rest + scale_x * sx[freq, :]) + scale_y * sy[...]
                spectrum = weight / (denominator * denominator)
                for part in range(2):
                    lanes = slice(128 * part, 128 * (part + 1))
                    g_hi[rows, lanes], g_lo[rows, lanes] = split(narrow[rows, lanes] * spectrum)
            return 0

        lax.fori_loop(0, PER_CHUNK, filtered, 0, unroll=True)
        wide[...] = dot3((g_hi[...], g_lo[...]), (inback_hi[...], inback_lo[...]))

        def untwisted(j, _):
            top = group_slice(j, BLOCK_Y)
            bottom = pl.ds(pl.multiple_of(CHUNK + j * BLOCK_Y, BLOCK_Y), BLOCK_Y)
            table = pl.ds(pl.multiple_of(c * CHUNK + j * BLOCK_Y, BLOCK_Y), BLOCK_Y)
            tr, ti = twist_re[table, :], twist_im[table, :]
            zr, zi = wide[top, :CELLS], wide[top, CELLS:]
            yr, yi = wide[bottom, :CELLS], wide[bottom, CELLS:]
            ar, ai = zr * tr + zi * ti, zi * tr - zr * ti
            br, bi = yr * tr - yi * ti, yr * ti + yi * tr
            m_hi[top, :CELLS], m_lo[top, :CELLS] = split(ar + br)
            m_hi[top, CELLS:], m_lo[top, CELLS:] = split(ai + bi)
            m_hi[bottom, :CELLS], m_lo[bottom, :CELLS] = split(bi - ai)
            m_hi[bottom, CELLS:], m_lo[bottom, CELLS:] = split(ar - br)
            return 0

        lax.fori_loop(0, PER_CHUNK, untwisted, 0, unroll=True)
        total[...] += dot3((back_hi[c], back_lo[c]), (m_hi[...], m_lo[...]))
        return 0

    lax.fori_loop(0, CHUNKS, chunk, 0)
    for j in range(4):
        out[pl.ds(j, DEVICES, stride=4), :] = total[:, 128 * j : 128 * (j + 1)]


def gather_kernel(
    received, direction, residual, noise, offsets, places, inverse_hi, inverse_lo,
    image, sums, v_hi, v_lo, e_hi, e_lo,
):
    for part in range(2):
        for half in range(2):
            rows = slice(part * GRID_Z, (part + 1) * GRID_Z)
            lanes = slice(half * 128, (half + 1) * 128)
            v_hi[rows, lanes], v_lo[rows, lanes] = split(received[pl.ds(2 * part + half, GRID_Z, stride=4), :])
    grid_hi, grid_lo = split(dot3((inverse_hi[...], inverse_lo[...]), (v_hi[...], v_lo[...])))
    e_hi[...] = grid_hi
    e_lo[...] = grid_lo

    def group(g, carry):
        bins = group_slice(g)
        shift = iota((GROUP, GRID_Z), 1) - places[bins, 1:2]
        at_depth = jnp.concatenate([one_hot(shift == f - 1) for f in range(4)], 0)
        lines_hi = dot(at_depth, e_hi[...]).astype(bf16)
        lines_lo = dot(at_depth, e_lo[...]).astype(bf16)
        cells = stencil_cells(places[bins, 0:1])
        keep = same_bin((PAIRS, 4 * GROUP))
        read_hi = jnp.where(keep, dot_nt(cells, lines_hi), 0.0).astype(bf16)
        read_lo = jnp.where(keep, dot_nt(cells, lines_lo), 0.0).astype(bf16)
        depths = split(jnp.concatenate(cubic_weights(offsets[2, bins, :]), 0))
        along = dot3((read_hi, read_lo), depths)
        wx = cubic_weights(offsets[0, bins, :])
        wy = cubic_weights(offsets[1, bins, :])
        value = 0.0
        for a in range(4):
            row = 0.0
            for e in range(4):
                start = (4 * a + e) * GROUP
                row = row + wy[e] * along[start : start + GROUP]
            value = value + wx[a] * row
        d, r = direction[bins, :], residual[bins, :]
        value = value + noise[bins, :] * d
        image[bins, :] = value
        return tuple(
            total + (x * y).reshape(GROUP // 8, 8, BIN).sum(0)
            for total, (x, y) in zip(carry, ((r, r), (d, value), (r, value), (value, value)))
        )

    zero = jnp.zeros((8, BIN), f32)
    totals = lax.fori_loop(0, GROUPS, group, (zero,) * 4)
    sums[...] = jnp.concatenate([jnp.broadcast_to(jnp.sum(t, keepdims=True), (1, BIN)) for t in totals], 0)


VMEM = pl.BlockSpec(memory_space=pltpu.VMEM)
SMEM = pl.BlockSpec(memory_space=pltpu.SMEM)


def params():
    return pltpu.CompilerParams(vmem_limit_bytes=40 * 1024 * 1024)


def on_device(solution, residual, direction, offsets, noise, bin_cells, lengths):
    row_index, column_index = lax.axis_index("px"), lax.axis_index("py")
    depth_tabs = depth_tables()
    plane = plane_tables()
    d = direction.reshape(BINS, BIN)
    r = residual.reshape(BINS, BIN)
    offsets = offsets.reshape(3, BINS, BIN)
    base = (bin_cells[0] - row_index * ROWS) * SPAN_Y + (bin_cells[1] - column_index * COLUMNS)
    places = jnp.stack([base, bin_cells[2]], 1)
    depth_row = (
        bin_cells[2].reshape(GROUPS, 1, GROUP) + jnp.arange(-1, 3, dtype=jnp.int32)[None, :, None]
    ).reshape(1, 4 * BINS)

    blocks = pl.pallas_call(
        spread_kernel,
        out_shape=jax.ShapeDtypeStruct((4 * DEVICES, 128), f32),
        in_specs=[VMEM] * 6,
        out_specs=VMEM,
        scratch_shapes=[pltpu.VMEM((4 * BINS, CELLS), bf16)] * 2,
        compiler_params=params(),
        name="spread",
    )(d, offsets, places, depth_row, *depth_tabs[:2])
    received = lax.all_to_all(blocks.reshape(DEVICES, 4, 128), ("px", "py"), 0, 0, tiled=True)

    freq = (row_index * N_PY + column_index).astype(f32)
    depth_part = lengths[2] * jnp.sin(freq * (math.pi / M_Z))
    scalars = jnp.stack(
        [
            lengths[0] * lengths[0],
            lengths[1] * lengths[1],
            1.0 + depth_part * depth_part,
            2.0 * lengths[0] * lengths[1] * lengths[2],
        ]
    )
    tables = (
        *plane["blocks"], *plane["blocks_back"], *plane["inner"], *plane["inner_back"], *plane["twist"],
        *plane["sine_x"], *plane["sine_y"], plane["weight"],
    )
    filtered = pl.pallas_call(
        plane_kernel,
        out_shape=jax.ShapeDtypeStruct((4 * DEVICES, 128), f32),
        in_specs=[SMEM] + [VMEM] * (1 + len(tables)),
        out_specs=VMEM,
        scratch_shapes=[
            pltpu.VMEM((DEVICES, 512), bf16),
            pltpu.VMEM((DEVICES, 512), bf16),
            pltpu.VMEM((2 * CHUNK, 512), f32),
            pltpu.VMEM((2 * CHUNK, 512), bf16),
            pltpu.VMEM((2 * CHUNK, 512), bf16),
            pltpu.VMEM((2 * CHUNK, 256), f32),
            pltpu.VMEM((2 * CHUNK, 256), bf16),
            pltpu.VMEM((2 * CHUNK, 256), bf16),
            pltpu.VMEM((DEVICES, 512), f32),
        ],
        compiler_params=params(),
        name="plane",
    )(scalars, received.reshape(4 * DEVICES, 128), *tables)
    returned = lax.all_to_all(filtered.reshape(DEVICES, 4, 128), ("px", "py"), 0, 0, tiled=True)

    image, sums = pl.pallas_call(
        gather_kernel,
        out_shape=(jax.ShapeDtypeStruct((BINS, BIN), f32), jax.ShapeDtypeStruct((4, 128), f32)),
        in_specs=[VMEM] * 8,
        out_specs=(VMEM, VMEM),
        scratch_shapes=[pltpu.VMEM((2 * GRID_Z, CELLS), bf16)] * 2 + [pltpu.VMEM((GRID_Z, CELLS), bf16)] * 2,
        compiler_params=params(),
        name="interpolate",
    )(returned.reshape(4 * DEVICES, 128), d, r, noise.reshape(BINS, BIN), offsets, places, *depth_tabs[2:])

    everywhere = lax.all_to_all(
        jnp.broadcast_to(sums[:, 0][None, :], (DEVICES, 4)), ("px", "py"), 0, 0, tiled=True
    )
    old_norm, curvature, cross, square = jnp.sum(everywhere, axis=0)
    step = old_norm / curvature
    new_norm = old_norm - 2.0 * step * cross + step * step * square
    image = image.reshape(1, -1)
    new_residual = residual - step * image
    new_solution = solution + step * direction
    new_direction = new_residual + (new_norm / old_norm) * direction
    return new_solution, new_residual, new_direction


def solution(mesh):
    points = P(None, ("px", "py"))
    return jax.shard_map(
        on_device,
        mesh=mesh,
        in_specs=(points, points, points, points, P(("px", "py")), points, P()),
        out_specs=(points, points, points),
        check_vma=False,
    )
```

time: 621 us -> 118 us (0.19); the launches traced: 610 us -> 117 us
  other arithmetic: 130 us -> 1.55 us
  local copies, waits for them, and re-layouts: 121 us -> 10.4 us
  blocking collectives: 147 us -> 44.3 us
  matrix products: 81 us -> 0 us
  starting transfers between devices: 82.9 us -> 15.7 us
  waiting for transfers between devices: 41.9 us -> 14.5 us
  Pallas kernels: 0 us -> 20.5 us
    psum x2 -> x0, blocking collectives: 147 us -> none  [the longest x1 74.6 us: on_device(): old_norm = lax.psum(jnp.sum(residual * residual, axis=1), ('px', 'py'))]
    scatter-add x1 -> x0, other arithmetic: 105 us -> none  [on_device(): spread = jnp.zeros((probes, (rows_dev + 3) * (columns_dev + 3) * GRID_Z),...]
    gather x1 -> x0, local copies, waits for them, and re-layouts: 90.7 us -> none  [on_device(): extended.reshape(probes, (rows_dev + 4) * (columns_dev + 4) * GRID_Z)]
    all_to_all x0 -> x2, blocking collectives: none -> 44.3 us  [the longest x1 26 us: on_device(): lax.all_to_all(filtered.reshape(DEVICES, 4, 128), ('px', 'py'), 0, 0, til...]
    all_to_all x8 -> x1, starting transfers between devices: 59 us -> 15.7 us  [on_device(): lax.all_to_all(blocks.reshape(DEVICES, 4, 128), ('px', 'py'), 0, 0, tiled...]
    dot_general x6 -> x0, matrix products: 43.2 us -> none  [the longest x1 17.7 us: on_device(): jnp.einsum('rnt,ntc->rnc', direction.reshape(probes, bin_count, BIN), wei...]
    unnamed x16 -> x0, matrix products: 37.8 us -> none
    ppermute x8 -> x0, starting transfers between devices: 24 us -> none  [the longest x4 17.5 us: extended_2(): lax.ppermute(lax.slice_in_dim(block, block.shape[dim] - width, None, axis...]
  transfers between devices with their start and end apart: 16 -> 1, of which waited for: 13 -> 1; matrix products, arithmetic and copies ran while one was open for 8% -> 1% of each run, Pallas kernels for 0% -> 0%
where the time goes in v1:
time: 118 us; the launch traced here: 117 us
  blocking collectives  44.3 us (38%)
  Pallas kernels  20.5 us (17%)
  starting transfers between devices  15.7 us (13%)
  waiting for transfers between devices  14.5 us (12%)
  local copies, waits for them, and re-layouts  10.4 us (9%)
  between operations  10.1 us (9%)
  other arithmetic  1.55 us (1%)
    all_to_all x1, blocking collectives, on_device(): lax.all_to_all(filtered.reshape(DEVICES, 4, 128), ('px', 'py'), 0, 0, til...  26 us
    all_to_all x1, blocking collectives, on_device(): lax.all_to_all(jnp.broadcast_to(sums[:, 0][None, :], (DEVICES, 4)), ('px'...  18.3 us
    all_to_all x1, starting transfers between devices, on_device(): lax.all_to_all(blocks.reshape(DEVICES, 4, 128), ('px', 'py'), 0, 0, tiled...  15.7 us
    all_to_all x1, waiting for transfers between devices, on_device(): lax.all_to_all(blocks.reshape(DEVICES, 4, 128), ('px', 'py'), 0, 0, tiled...  14.5 us
    unnamed x51, local copies, waits for them, and re-layouts  8.75 us
    pallas_call x1, Pallas kernels, on_device(): pl.pallas_call(plane_kernel, out_shape=jax.ShapeDtypeStruct((4 * DEVICES,...  7.85 us
    pallas_call x1, Pallas kernels, on_device(): pl.pallas_call(gather_kernel, out_shape=(jax.ShapeDtypeStruct((BINS, BIN)...  6.34 us
    pallas_call x1, Pallas kernels, on_device(): pl.pallas_call(spread_kernel, out_shape=jax.ShapeDtypeStruct((4 * DEVICES...  6.27 us
  transfers between devices with their start and end apart: 1, of which 1 were waited for; matrix products, arithmetic and copies ran while one was open for 1% of the time, Pallas kernels for 0%

profile of v1, /device:TPU:1, one launch (start us, length us, event | category | flops | bytes accessed | tf_op | source)
XLA Modules:
  0.0 117.0 jit_solution(2617982686953415470)
XLA Ops:
  0.6 0.0 copy-start.24
  0.7 0.7 copy-done.24
  1.4 0.1 add.60
  1.4 0.1 broadcast_add_fusion
  1.5 0.1 add.65.depth_row
  1.6 0.1 copy.35.places
  1.8 0.0 copy-start
  1.8 0.0 copy-start.14
  1.8 0.0 copy-start.15
  1.8 1.1 copy.45
  2.9 0.0 copy-done
  2.9 0.0 copy-done.14
  3.0 0.1 copy-done.15
  3.0 6.3 %spread.1 = f32[1024,128]{1,0:T(8,128)} custom-call(f32[256,128]{1,0:T(8,128)S(1)} %bitcast.29, f32[3,256,128]{2,1,0:T(8,128)S(1)} %bitcast.24, s32[256,2]{1,0:T(8,128)S(1)} %copy.35.places, s32[1,1024]{1,0:T(1,128)S(1)} %add.65.depth_row, bf16[512,256]{1,0:T(8,128)(2,1)S(1)} %copy-done.15, bf16[512,256]{1,0:T(8,128)(2,1)S(1)} %copy-done.14), custom_call_target="tpu_custom_call" | custom-call | tf_op jit(solution)/shard_map/spread/pallas_call | solution.py:308
  9.3 0.0 copy-start.21
  9.3 15.7 %all-to-all-start = ((f32[256,4,128]{2,1,0:T(4,128)}), f32[256,4,128]{2,1,0:T(4,128)S(1)}, u32[]{:S(2)}, u32[]{:S(2)}) async-start(f32[256,4,128]{2,1,0:T(4,128)} %bitcast.7), calls=%async_computation | async-start | bytes 1048576 | tf_op jit(solution)/shard_map/all_to_all | solution.py:317
  25.0 0.0 copy-start.18
  25.0 0.0 copy-start.17
  25.1 0.0 copy-done.23
  25.1 0.6 fusion.1
  30.9 0.1 pad_maximum_fusion.scalars
  31.0 14.5 %all-to-all-done = f32[256,4,128]{2,1,0:T(4,128)S(1)} async-done(((f32[256,4,128]{2,1,0:T(4,128)}), f32[256,4,128]{2,1,0:T(4,128)S(1)}, u32[]{:S(2)}, u32[]{:S(2)}) %all-to-all-start) | async-done | bytes 524320 | tf_op jit(solution)/shard_map/all_to_all | solution.py:317
  45.5 0.0 copy-done.2
  45.5 0.0 copy-done.3
  45.5 0.0 copy-done.4
  45.5 0.0 copy-done.1
  45.6 0.0 copy-start.5
  45.6 1.0 copy-done.5
  46.6 1.0 copy-done.6
  47.7 0.9 copy-done.10
  48.6 0.9 copy-done.11
  49.6 0.9 copy-done.12
  50.5 0.9 copy-done.13
  51.5 7.8 %plane.1 = f32[1024,128]{1,0:T(8,128)S(1)} custom-call(f32[4]{0:T(128)S(1)} %pad_maximum_fusion.scalars, f32[1024,128]{1,0:T(8,128)S(1)} %bitcast.26, bf16[3,352,256]{2,1,0:T(8,128)(2,1)S(1)} %copy-done.6, bf16[3,352,256]{2,1,0:T(8,128)(2,1)S(1)} %copy-done.5, bf16[3,256,352]{2,1,0:T(8,128)(2,1)S(1)} %copy-done.2, bf16[3,256,352]{2,1,0:T(8,128)(2,1)S(1)} %copy-done.1, ...), custom_call_target="tpu_custom_call" | custom-call | tf_op jit(solution)/shard_map/plane/pallas_call | solution.py:333
  59.3 0.0 copy-start.7
  59.3 0.0 copy-start.8
  59.4 0.0 copy-start.9
  59.4 0.0 copy-start.16
  59.4 26.0 %all_to_all.16 = f32[256,4,128]{2,1,0:T(4,128)S(1)} all-to-all(f32[256,4,128]{2,1,0:T(4,128)S(1)} %bitcast.27), channel_id=1, replica_groups=mesh['px'=32,'py'=8] {'px','py'}, dimensions={0} | all-to-all | bytes 1048576 | tf_op jit(solution)/shard_map/all_to_all | solution.py:352
  85.4 6.3 %interpolate.1 = (f32[256,128]{1,0:T(8,128)S(1)}, f32[4,128]{1,0:T(4,128)S(1)}) custom-call(f32[1024,128]{1,0:T(8,128)S(1)} %bitcast.28, f32[256,128]{1,0:T(8,128)S(1)} %bitcast.30, f32[256,128]{1,0:T(8,128)S(1)} %bitcast.31, f32[256,128]{1,0:T(8,128)S(1)} %bitcast.32, f32[3,256,128]{2,1,0:T(8,128)S(1)} %bitcast.25, s32[256,2]{1,0:T(8,128)S(1)} %copy.35.places, ...), custom_call_target="tpu_custom_call" | custom-call | tf_op jit(solution)/shard_map/interpolate/pallas_call | solution.py:354
  91.7 0.1 slice_reduce_fusion
  91.9 0.1 broadcast_in_dim.9
  91.9 18.3 %all_to_all.17 = f32[256,1,4]{2,1,0:T(1,128)S(1)} all-to-all(f32[256,1,4]{2,1,0:T(1,128)S(1)} %broadcast_in_dim.9), channel_id=1, replica_groups=mesh['px'=32,'py'=8] {'px','py'}, dimensions={0} | all-to-all | bytes 8192 | tf_op jit(solution)/shard_map/all_to_all | solution.py:364
  110.2 0.3 reduce_sum.9
  110.5 0.6 fusion
  115.0 0.0 copy-start.22
  115.1 0.9 copy-done.22
  115.9 1.1 multiply_add_fusion
  (25 shorter events, 0.1 us)
Async XLA Ops:
  0.6 0.7 copy-start.24
  1.8 1.2 %copy-start = (f32[1,32768]{1,0:T(1,128)S(1)}, f32[1,32768]{1,0:T(1,128)}, u32[]{:S(2)}) copy-start(f32[1,32768]{1,0:T(1,128)} %param.28) | copy-start | bytes 393220
  1.8 1.2 %copy-start.14 = (bf16[512,256]{1,0:T(8,128)(2,1)S(1)}, bf16[512,256]{1,0:T(8,128)(2,1)}, u32[]{:S(2)}) copy-start(bf16[512,256]{1,0:T(8,128)(2,1)} %constant.68.clone.forward_lo) | copy-start | bytes 786436
  1.8 1.2 %copy-start.15 = (bf16[512,256]{1,0:T(8,128)(2,1)S(1)}, bf16[512,256]{1,0:T(8,128)(2,1)}, u32[]{:S(2)}) copy-start(bf16[512,256]{1,0:T(8,128)(2,1)} %constant.67.clone.forward_hi) | copy-start | bytes 786436
  3.0 42.5 %copy-start.2 = (bf16[3,256,352]{2,1,0:T(8,128)(2,1)S(1)}, bf16[3,256,352]{2,1,0:T(8,128)(2,1)}, u32[]{:S(2)}) copy-start(bf16[3,256,352]{2,1,0:T(8,128)(2,1)} %constant.71.clone.back_hi) | copy-start | bytes 1622020
  3.0 42.5 %copy-start.3 = (f32[528,256]{1,0:T(8,128)S(1)}, f32[528,256]{1,0:T(8,128)}, u32[]{:S(2)}) copy-start(f32[528,256]{1,0:T(8,128)} %constant.78.clone.twist_im) | copy-start | bytes 1622020
  3.0 42.5 %copy-start.4 = (f32[528,256]{1,0:T(8,128)S(1)}, f32[528,256]{1,0:T(8,128)}, u32[]{:S(2)}) copy-start(f32[528,256]{1,0:T(8,128)} %constant.77.clone.twist_re) | copy-start | bytes 1622020
  9.3 36.2 %copy-start.1 = (bf16[3,256,352]{2,1,0:T(8,128)(2,1)S(1)}, bf16[3,256,352]{2,1,0:T(8,128)(2,1)}, u32[]{:S(2)}) copy-start(bf16[3,256,352]{2,1,0:T(8,128)(2,1)} %constant.72.clone.back_lo) | copy-start | bytes 1622020
  9.3 15.8 %copy-start.23 = (f32[3]{0:T(128)S(1)}, f32[3]{0:T(128)}, u32[]{:S(2)}) copy-start(f32[3]{0:T(128)} %param.32) | copy-start | bytes 40
  9.3 36.2 %copy-start.19 = (f32[33,128]{1,0:T(8,128)S(1)}, f32[33,128]{1,0:T(8,128)}, u32[]{:S(2)}) copy-start(f32[33,128]{1,0:T(8,128)} %constant.79.clone.sx_a) | copy-start | bytes 50692
  9.3 36.2 %copy-start.20 = (f32[16,128]{1,0:T(8,128)S(1)}, f32[16,128]{1,0:T(8,128)}, u32[]{:S(2)}) copy-start(f32[16,128]{1,0:T(8,128)} %constant.82.clone.sy_b) | copy-start | bytes 24580
  9.3 36.2 %copy-start.21 = (f32[16,128]{1,0:T(8,128)S(1)}, f32[16,128]{1,0:T(8,128)}, u32[]{:S(2)}) copy-start(f32[16,128]{1,0:T(8,128)} %constant.81.clone.sy_a) | copy-start | bytes 24580
  9.3 36.2 %all-to-all-start = ((f32[256,4,128]{2,1,0:T(4,128)}), f32[256,4,128]{2,1,0:T(4,128)S(1)}, u32[]{:S(2)}, u32[]{:S(2)}) async-start(f32[256,4,128]{2,1,0:T(4,128)} %bitcast.7), calls=%async_computation | async-start | bytes 1048576 | tf_op jit(solution)/shard_map/all_to_all | solution.py:317
  25.0 20.5 %copy-start.18 = (f32[33,128]{1,0:T(8,128)S(1)}, f32[33,128]{1,0:T(8,128)}, u32[]{:S(2)}) copy-start(f32[33,128]{1,0:T(8,128)} %constant.80.clone.sx_b) | copy-start | bytes 50692
  25.0 20.5 %copy-start.17 = (f32[33,128]{1,0:T(8,128)S(1)}, f32[33,128]{1,0:T(8,128)}, u32[]{:S(2)}) copy-start(f32[33,128]{1,0:T(8,128)} %constant.83.clone.weight_b) | copy-start | bytes 50692
  45.6 1.1 copy-start.5
  46.6 1.0 copy-start.6
  47.7 0.9 copy-start.10
  48.6 0.9 copy-start.11
  49.6 0.9 copy-start.12
  50.5 0.9 copy-start.13
  59.3 26.1 %copy-start.7 = (f32[1,32768]{1,0:T(1,128)S(1)}, f32[1,32768]{1,0:T(1,128)}, u32[]{:S(2)}) copy-start(f32[1,32768]{1,0:T(1,128)} %param.27) | copy-start | bytes 393220
  59.3 26.0 %copy-start.8 = (bf16[256,512]{1,0:T(8,128)(2,1)S(1)}, bf16[256,512]{1,0:T(8,128)(2,1)}, u32[]{:S(2)}) copy-start(bf16[256,512]{1,0:T(8,128)(2,1)} %constant.85.clone.inverse_lo) | copy-start | bytes 786436
  59.4 26.0 %copy-start.9 = (bf16[256,512]{1,0:T(8,128)(2,1)S(1)}, bf16[256,512]{1,0:T(8,128)(2,1)}, u32[]{:S(2)}) copy-start(bf16[256,512]{1,0:T(8,128)(2,1)} %constant.84.clone.inverse_hi) | copy-start | bytes 786436
  59.4 26.0 %copy-start.16 = (f32[32768]{0:T(1024)S(1)}, f32[32768]{0:T(1024)}, u32[]{:S(2)}) copy-start(f32[32768]{0:T(1024)} %param.30) | copy-start | bytes 393220
  115.0 0.9 copy-start.22

commit v2 on v1

--- a/solution.py
+++ b/solution.py
@@ -1,5 +1,3 @@
-import math
-
 import jax
 import jax.numpy as jnp
 import ml_dtypes
@@ -80,6 +78,7 @@
         sine_x=[t.astype(np.float32) for t in sine_x],
         sine_y=[t.astype(np.float32) for t in sine_y],
         weight=weight.astype(np.float32),
+        depth_sine=(np.sin(np.pi * np.arange(GRID_Z) / M_Z) ** 2).astype(np.float32),
     )
 
 
@@ -130,7 +129,12 @@
     return pl.ds(pl.multiple_of(g * size, size), size)
 
 
-def spread_kernel(direction, offsets, places, depth_row, forward_hi, forward_lo, out, q_hi, q_lo):
+def block_base(cells):
+    first_row, first_column = lax.axis_index("px") * ROWS, lax.axis_index("py") * COLUMNS
+    return (cells[:, 0:1] - first_row) * SPAN_Y + (cells[:, 1:2] - first_column)
+
+
+def spread_kernel(direction, offsets, cells_down, cells_across, forward_hi, forward_lo, out, q_hi, q_lo):
     def group(g, _):
         bins = group_slice(g)
         wx = cubic_weights(offsets[0, bins, :])
@@ -142,15 +146,17 @@
         depths = split(jnp.concatenate(wz, 0))
         patches = dot3(depths, columns, dot_nt)
         patches = split(jnp.where(same_bin((4 * GROUP, PAIRS)), patches, 0.0))
-        cells = stencil_cells(places[bins, 0:1])
+        cells = stencil_cells(block_base(cells_down[bins, :]))
         placed = split(dot(patches[0], cells) + dot(patches[1], cells))
-        rows = group_slice(g, 4 * GROUP)
-        q_hi[rows, :] = placed[0]
-        q_lo[rows, :] = placed[1]
+        for f in range(4):
+            rows = pl.ds(pl.multiple_of(f * BINS + g * GROUP, GROUP), GROUP)
+            q_hi[rows, :] = placed[0][f * GROUP : (f + 1) * GROUP]
+            q_lo[rows, :] = placed[1][f * GROUP : (f + 1) * GROUP]
         return 0
 
     lax.fori_loop(0, GROUPS, group, 0)
-    at_depth = one_hot(iota((GRID_Z, 4 * BINS), 0) == depth_row[...])
+    shift = iota((GRID_Z, BINS), 0) - cells_across[2:3, :]
+    at_depth = jnp.concatenate([one_hot(shift == f - 1) for f in range(4)], 1)
     gridded = split(dot(at_depth, q_hi[...]) + dot(at_depth, q_lo[...]))
     transformed = dot3((forward_hi[...], forward_lo[...]), gridded)
     for part in range(2):
@@ -161,7 +167,7 @@
 
 
 def plane_kernel(
-    scalars, received, blocks_hi, blocks_lo, back_hi, back_lo, inner_hi, inner_lo, inback_hi, inback_lo,
+    lengths, depth_sine, received, blocks_hi, blocks_lo, back_hi, back_lo, inner_hi, inner_lo, inback_hi, inback_lo,
     twist_re, twist_im, sx_a, sx_b, sy_a, sy_b, weight_b,
     out, r_hi, r_lo, wide, m_hi, m_lo, narrow, g_hi, g_lo, total,
 ):
@@ -170,7 +176,9 @@
         r_hi[:, 128 * j : 128 * (j + 1)] = hi
         r_lo[:, 128 * j : 128 * (j + 1)] = lo
     total[...] = jnp.zeros_like(total)
-    scale_x, scale_y, rest, factor = scalars[0], scalars[1], scalars[2], scalars[3]
+    scale_x, scale_y = lengths[0] * lengths[0], lengths[1] * lengths[1]
+    rest = 1.0 + lengths[2] * lengths[2] * depth_sine[lax.axis_index("px") * N_PY + lax.axis_index("py")]
+    factor = 2.0 * lengths[0] * lengths[1] * lengths[2]
     factor_a = factor * (1.0 / (M_X * M_Y))
 
     def chunk(c, _):
@@ -238,7 +246,7 @@
 
 
 def gather_kernel(
-    received, direction, residual, noise, offsets, places, inverse_hi, inverse_lo,
+    received, direction, residual, noise, offsets, cells_down, inverse_hi, inverse_lo,
     image, sums, v_hi, v_lo, e_hi, e_lo,
 ):
     for part in range(2):
@@ -252,11 +260,11 @@
 
     def group(g, carry):
         bins = group_slice(g)
-        shift = iota((GROUP, GRID_Z), 1) - places[bins, 1:2]
+        shift = iota((GROUP, GRID_Z), 1) - cells_down[bins, 2:3]
         at_depth = jnp.concatenate([one_hot(shift == f - 1) for f in range(4)], 0)
         lines_hi = dot(at_depth, e_hi[...]).astype(bf16)
         lines_lo = dot(at_depth, e_lo[...]).astype(bf16)
-        cells = stencil_cells(places[bins, 0:1])
+        cells = stencil_cells(block_base(cells_down[bins, :]))
         keep = same_bin((PAIRS, 4 * GROUP))
         read_hi = jnp.where(keep, dot_nt(cells, lines_hi), 0.0).astype(bf16)
         read_lo = jnp.where(keep, dot_nt(cells, lines_lo), 0.0).astype(bf16)
@@ -281,7 +289,23 @@
 
     zero = jnp.zeros((8, BIN), f32)
     totals = lax.fori_loop(0, GROUPS, group, (zero,) * 4)
-    sums[...] = jnp.concatenate([jnp.broadcast_to(jnp.sum(t, keepdims=True), (1, BIN)) for t in totals], 0)
+    lane = iota((1, BIN), 1)
+    row = jnp.zeros((1, BIN), f32)
+    for j, part in enumerate(totals):
+        row = jnp.where(lane == j, jnp.sum(part, keepdims=True), row)
+    sums[...] = jnp.broadcast_to(row, (DEVICES, BIN))
+
+
+def step_kernel(sums, iterate, residual, direction, image, new_iterate, new_residual, new_direction):
+    row = jnp.sum(sums[...], axis=0, keepdims=True)
+    old_norm, curvature, cross, square = (row[:, j : j + 1] for j in range(4))
+    step = old_norm / curvature
+    new_norm = old_norm - 2.0 * step * cross + step * step * square
+    d = direction[...]
+    r = residual[...] - step * image[...]
+    new_iterate[...] = iterate[...] + step * d
+    new_residual[...] = r
+    new_direction[...] = r + (new_norm / old_norm) * d
 
 
 VMEM = pl.BlockSpec(memory_space=pltpu.VMEM)
@@ -289,21 +313,15 @@
 
 
 def params():
-    return pltpu.CompilerParams(vmem_limit_bytes=40 * 1024 * 1024)
+    return pltpu.CompilerParams(vmem_limit_bytes=16 * 1024 * 1024)
 
 
 def on_device(solution, residual, direction, offsets, noise, bin_cells, lengths):
-    row_index, column_index = lax.axis_index("px"), lax.axis_index("py")
     depth_tabs = depth_tables()
     plane = plane_tables()
-    d = direction.reshape(BINS, BIN)
-    r = residual.reshape(BINS, BIN)
+    d, r = direction.reshape(BINS, BIN), residual.reshape(BINS, BIN)
     offsets = offsets.reshape(3, BINS, BIN)
-    base = (bin_cells[0] - row_index * ROWS) * SPAN_Y + (bin_cells[1] - column_index * COLUMNS)
-    places = jnp.stack([base, bin_cells[2]], 1)
-    depth_row = (
-        bin_cells[2].reshape(GROUPS, 1, GROUP) + jnp.arange(-1, 3, dtype=jnp.int32)[None, :, None]
-    ).reshape(1, 4 * BINS)
+    cells_down = bin_cells.T
 
     blocks = pl.pallas_call(
         spread_kernel,
@@ -313,19 +331,9 @@
         scratch_shapes=[pltpu.VMEM((4 * BINS, CELLS), bf16)] * 2,
         compiler_params=params(),
         name="spread",
-    )(d, offsets, places, depth_row, *depth_tabs[:2])
+    )(d, offsets, cells_down, bin_cells, *depth_tabs[:2])
     received = lax.all_to_all(blocks.reshape(DEVICES, 4, 128), ("px", "py"), 0, 0, tiled=True)
 
-    freq = (row_index * N_PY + column_index).astype(f32)
-    depth_part = lengths[2] * jnp.sin(freq * (math.pi / M_Z))
-    scalars = jnp.stack(
-        [
-            lengths[0] * lengths[0],
-            lengths[1] * lengths[1],
-            1.0 + depth_part * depth_part,
-            2.0 * lengths[0] * lengths[1] * lengths[2],
-        ]
-    )
     tables = (
         *plane["blocks"], *plane["blocks_back"], *plane["inner"], *plane["inner_back"], *plane["twist"],
         *plane["sine_x"], *plane["sine_y"], plane["weight"],
@@ -333,7 +341,7 @@
     filtered = pl.pallas_call(
         plane_kernel,
         out_shape=jax.ShapeDtypeStruct((4 * DEVICES, 128), f32),
-        in_specs=[SMEM] + [VMEM] * (1 + len(tables)),
+        in_specs=[SMEM] * 2 + [VMEM] * (1 + len(tables)),
         out_specs=VMEM,
         scratch_shapes=[
             pltpu.VMEM((DEVICES, 512), bf16),
@@ -348,30 +356,29 @@
         ],
         compiler_params=params(),
         name="plane",
-    )(scalars, received.reshape(4 * DEVICES, 128), *tables)
+    )(lengths, plane["depth_sine"], received.reshape(4 * DEVICES, 128), *tables)
     returned = lax.all_to_all(filtered.reshape(DEVICES, 4, 128), ("px", "py"), 0, 0, tiled=True)
 
     image, sums = pl.pallas_call(
         gather_kernel,
-        out_shape=(jax.ShapeDtypeStruct((BINS, BIN), f32), jax.ShapeDtypeStruct((4, 128), f32)),
+        out_shape=(jax.ShapeDtypeStruct((BINS, BIN), f32), jax.ShapeDtypeStruct((DEVICES, BIN), f32)),
         in_specs=[VMEM] * 8,
         out_specs=(VMEM, VMEM),
         scratch_shapes=[pltpu.VMEM((2 * GRID_Z, CELLS), bf16)] * 2 + [pltpu.VMEM((GRID_Z, CELLS), bf16)] * 2,
         compiler_params=params(),
         name="interpolate",
-    )(returned.reshape(4 * DEVICES, 128), d, r, noise.reshape(BINS, BIN), offsets, places, *depth_tabs[2:])
-
-    everywhere = lax.all_to_all(
-        jnp.broadcast_to(sums[:, 0][None, :], (DEVICES, 4)), ("px", "py"), 0, 0, tiled=True
-    )
-    old_norm, curvature, cross, square = jnp.sum(everywhere, axis=0)
-    step = old_norm / curvature
-    new_norm = old_norm - 2.0 * step * cross + step * step * square
-    image = image.reshape(1, -1)
-    new_residual = residual - step * image
-    new_solution = solution + step * direction
-    new_direction = new_residual + (new_norm / old_norm) * direction
-    return new_solution, new_residual, new_direction
+    )(returned.reshape(4 * DEVICES, 128), d, r, noise.reshape(BINS, BIN), offsets, cells_down, *depth_tabs[2:])
+
+    everywhere = lax.all_to_all(sums.reshape(DEVICES, 1, BIN), ("px", "py"), 0, 0, tiled=True)
+    outs = pl.pallas_call(
+        step_kernel,
+        out_shape=(jax.ShapeDtypeStruct((BINS, BIN), f32),) * 3,
+        in_specs=[VMEM] * 5,
+        out_specs=(VMEM,) * 3,
+        compiler_params=params(),
+        name="step",
+    )(everywhere.reshape(DEVICES, BIN), solution.reshape(BINS, BIN), r, d, image)
+    return tuple(out.reshape(1, -1) for out in outs)
 
 
 def solution(mesh):

time: 118 us -> 110 us (0.932)
  blocking collectives: 44.3 us -> 80.3 us
  starting transfers between devices: 15.7 us -> 0 us
  waiting for transfers between devices: 14.5 us -> 0 us
  between operations: 10.1 us -> 0.9 us
  local copies, waits for them, and re-layouts: 10.4 us -> 8.14 us
  other arithmetic: 1.55 us -> 0 us
    all_to_all x1 -> x2, blocking collectives: 18.3 us -> 54.3 us  [the longest x1 36 us: on_device(): lax.all_to_all(blocks.reshape(DEVICES, 4, 128), ('px', 'py'), 0, 0, tiled...]
    all_to_all x1 -> x0, starting transfers between devices: 15.7 us -> none  [on_device(): lax.all_to_all(blocks.reshape(DEVICES, 4, 128), ('px', 'py'), 0, 0, tiled...]
    all_to_all x1 -> x0, waiting for transfers between devices: 14.5 us -> none  [on_device(): lax.all_to_all(blocks.reshape(DEVICES, 4, 128), ('px', 'py'), 0, 0, tiled...]
    unnamed x51 -> x54, local copies, waits for them, and re-layouts: 8.75 us -> 8.14 us
  transfers between devices with their start and end apart: 1 -> 0, of which waited for: 1 -> 0; matrix products, arithmetic and copies ran while one was open for 1% -> 0% of each run, Pallas kernels for 0% -> 0%
where the time goes in v2:
time: 110 us
  blocking collectives  80.3 us (73%)
  Pallas kernels  20.7 us (19%)
  local copies, waits for them, and re-layouts  8.14 us (7%)
    all_to_all x1, blocking collectives, on_device(): lax.all_to_all(blocks.reshape(DEVICES, 4, 128), ('px', 'py'), 0, 0, tiled...  36 us
    all_to_all x1, blocking collectives, on_device(): lax.all_to_all(filtered.reshape(DEVICES, 4, 128), ('px', 'py'), 0, 0, til...  26 us
    all_to_all x1, blocking collectives, on_device(): lax.all_to_all(sums.reshape(DEVICES, 1, BIN), ('px', 'py'), 0, 0, tiled=T...  18.3 us
    unnamed x54, local copies, waits for them, and re-layouts  8.14 us
    pallas_call x1, Pallas kernels, on_device(): pl.pallas_call(plane_kernel, out_shape=jax.ShapeDtypeStruct((4 * DEVICES,...  7.93 us
    pallas_call x1, Pallas kernels, on_device(): pl.pallas_call(gather_kernel, out_shape=(jax.ShapeDtypeStruct((BINS, BIN)...  6.36 us
    pallas_call x1, Pallas kernels, on_device(): pl.pallas_call(spread_kernel, out_shape=jax.ShapeDtypeStruct((4 * DEVICES...  5.48 us

profile of v2, /device:TPU:1, one launch (start us, length us, event | category | flops | bytes accessed | tf_op | source)
XLA Modules:
  0.0 110.0 jit_solution(11647655001852672827)
XLA Ops:
  0.6 0.0 copy-start.10
  0.6 0.9 copy.31
  1.5 0.0 copy-start
  1.5 0.0 copy-start.5
  1.5 0.0 copy-start.6
  1.5 1.2 %copy.35 = f32[1,3,256,128]{3,2,1,0:T(8,128)S(1)} copy(f32[1,3,256,128]{3,1,2,0:T(4,128)} %bitcast.37) | data formatting | bytes 786432
  2.7 0.0 copy-done
  2.7 0.0 copy-start.14
  2.7 0.9 copy-done.14
  3.7 0.9 copy-done.15
  4.6 0.7 copy-done.21
  5.3 5.5 %spread.1 = f32[1024,128]{1,0:T(8,128)S(1)} custom-call(f32[256,128]{1,0:T(8,128)S(1)} %bitcast.26, f32[3,256,128]{2,1,0:T(8,128)S(1)} %bitcast.20, s32[256,3]{1,0:T(8,128)S(1)} %bitcast.29, s32[3,256]{1,0:T(4,128)S(1)} %copy-done.21, bf16[512,256]{1,0:T(8,128)(2,1)S(1)} %copy-done.15, bf16[512,256]{1,0:T(8,128)(2,1)S(1)} %copy-done.14), custom_call_target="tpu_custom_call" | custom-call | tf_op jit(solution)/shard_map/spread/pallas_call | solution.py:326
  10.8 0.0 copy-start.1
  10.8 0.0 copy-start.18
  10.8 0.0 copy-start.19
  10.8 0.0 copy-start.20
  10.9 0.0 copy-start.22
  10.9 0.0 copy-start.23
  10.9 36.0 %all_to_all.15 = f32[256,4,128]{2,1,0:T(4,128)S(1)} all-to-all(f32[256,4,128]{2,1,0:T(4,128)S(1)} %bitcast.22), channel_id=1, replica_groups=mesh['px'=32,'py'=8] {'px','py'}, dimensions={0} | all-to-all | bytes 1048576 | tf_op jit(solution)/shard_map/all_to_all | solution.py:335
  46.8 0.0 copy-done.10
  46.9 0.0 copy-done.5
  46.9 0.0 copy-done.6
  46.9 0.0 copy-done.2
  46.9 0.0 copy-done.3
  46.9 0.0 copy-done.4
  46.9 0.0 copy-done.1
  46.9 0.0 copy-done.18
  46.9 0.0 copy-done.19
  46.9 0.0 copy-done.20
  46.9 0.0 copy-done.22
  46.9 0.0 copy-done.23
  47.0 0.6 copy-done.24
  47.5 0.0 copy-done.25
  47.5 0.9 copy-done.11
  48.5 0.9 copy-done.12
  49.4 0.9 copy-done.13
  50.4 7.9 %plane.1 = f32[1024,128]{1,0:T(8,128)S(1)} custom-call(f32[3]{0:T(128)S(1)} %copy-done.25, f32[256]{0:T(256)S(1)} %copy-done.24, f32[1024,128]{1,0:T(8,128)S(1)} %bitcast.24, bf16[3,352,256]{2,1,0:T(8,128)(2,1)S(1)} %copy-done.6, bf16[3,352,256]{2,1,0:T(8,128)(2,1)S(1)} %copy-done.5, bf16[3,256,352]{2,1,0:T(8,128)(2,1)S(1)} %copy-done.2, ...), custom_call_target="tpu_custom_call" | custom-call | tf_op jit(solution)/shard_map/plane/pallas_call | solution.py:341
  58.3 0.0 copy-start.7
  58.3 0.0 copy-start.8
  58.3 0.0 copy-start.9
  58.4 0.0 copy-start.17
  58.4 26.0 %all_to_all.16 = f32[256,4,128]{2,1,0:T(4,128)S(1)} all-to-all(f32[256,4,128]{2,1,0:T(4,128)S(1)} %bitcast.25), channel_id=1, replica_groups=mesh['px'=32,'py'=8] {'px','py'}, dimensions={0} | all-to-all | bytes 1048576 | tf_op jit(solution)/shard_map/all_to_all | solution.py:360
  84.4 0.0 copy-done.7
  84.4 0.0 copy-done.8
  84.4 6.4 %interpolate.1 = (f32[256,128]{1,0:T(8,128)S(1)}, f32[256,128]{1,0:T(8,128)S(1)}) custom-call(f32[1024,128]{1,0:T(8,128)S(1)} %bitcast.23, f32[256,128]{1,0:T(8,128)S(1)} %bitcast.27, f32[256,128]{1,0:T(8,128)S(1)} %bitcast.32, f32[256,128]{1,0:T(8,128)S(1)} %bitcast.36, f32[3,256,128]{2,1,0:T(8,128)S(1)} %bitcast.21, s32[256,3]{1,0:T(8,128)S(1)} %bitcast.30, ...), custom_call_target="tpu_custom_call" | custom-call | tf_op jit(solution)/shard_map/interpolate/pallas_call | solution.py:362
  90.8 0.0 copy-start.16
  90.8 18.3 %all_to_all.17 = f32[256,1,128]{2,1,0:T(1,128)S(1)} all-to-all(f32[256,1,128]{2,1,0:T(1,128)S(1)} %bitcast.35), channel_id=1, replica_groups=mesh['px'=32,'py'=8] {'px','py'}, dimensions={0} | all-to-all | bytes 262144 | tf_op jit(solution)/shard_map/all_to_all | solution.py:372
  109.1 0.9 step.1
  (13 shorter events, 0.0 us)
Async XLA Ops:
  0.6 46.2 %copy-start.10 = (bf16[256,512]{1,0:T(8,128)(2,1)S(1)}, bf16[256,512]{1,0:T(8,128)(2,1)}, u32[]{:S(2)}) copy-start(bf16[256,512]{1,0:T(8,128)(2,1)} %constant.50.clone.inback_lo) | copy-start | bytes 786436
  1.5 1.2 %copy-start = (f32[1,32768]{1,0:T(1,128)S(1)}, f32[1,32768]{1,0:T(1,128)}, u32[]{:S(2)}) copy-start(f32[1,32768]{1,0:T(1,128)} %param.29) | copy-start | bytes 393220
  1.5 45.3 %copy-start.5 = (bf16[3,352,256]{2,1,0:T(8,128)(2,1)S(1)}, bf16[3,352,256]{2,1,0:T(8,128)(2,1)}, u32[]{:S(2)}) copy-start(bf16[3,352,256]{2,1,0:T(8,128)(2,1)} %constant.44.clone.blocks_lo) | copy-start | bytes 1622020
  1.5 45.3 %copy-start.6 = (bf16[3,352,256]{2,1,0:T(8,128)(2,1)S(1)}, bf16[3,352,256]{2,1,0:T(8,128)(2,1)}, u32[]{:S(2)}) copy-start(bf16[3,352,256]{2,1,0:T(8,128)(2,1)} %constant.43.clone.blocks_hi) | copy-start | bytes 1622020
  2.7 1.0 copy-start.14
  3.7 0.9 copy-start.15
  4.6 0.7 copy-start.21
  5.3 41.6 %copy-start.2 = (bf16[3,256,352]{2,1,0:T(8,128)(2,1)S(1)}, bf16[3,256,352]{2,1,0:T(8,128)(2,1)}, u32[]{:S(2)}) copy-start(bf16[3,256,352]{2,1,0:T(8,128)(2,1)} %constant.45.clone.back_hi) | copy-start | bytes 1622020
  5.3 41.6 %copy-start.3 = (f32[528,256]{1,0:T(8,128)S(1)}, f32[528,256]{1,0:T(8,128)}, u32[]{:S(2)}) copy-start(f32[528,256]{1,0:T(8,128)} %constant.52.clone.twist_im) | copy-start | bytes 1622020
  5.3 41.6 %copy-start.4 = (f32[528,256]{1,0:T(8,128)S(1)}, f32[528,256]{1,0:T(8,128)}, u32[]{:S(2)}) copy-start(f32[528,256]{1,0:T(8,128)} %constant.51.clone.twist_re) | copy-start | bytes 1622020
  10.8 36.1 %copy-start.1 = (bf16[3,256,352]{2,1,0:T(8,128)(2,1)S(1)}, bf16[3,256,352]{2,1,0:T(8,128)(2,1)}, u32[]{:S(2)}) copy-start(bf16[3,256,352]{2,1,0:T(8,128)(2,1)} %constant.46.clone.back_lo) | copy-start | bytes 1622020
  10.8 36.1 %copy-start.18 = (f32[33,128]{1,0:T(8,128)S(1)}, f32[33,128]{1,0:T(8,128)}, u32[]{:S(2)}) copy-start(f32[33,128]{1,0:T(8,128)} %constant.57.clone.weight_b) | copy-start | bytes 50692
  10.8 36.1 %copy-start.19 = (f32[33,128]{1,0:T(8,128)S(1)}, f32[33,128]{1,0:T(8,128)}, u32[]{:S(2)}) copy-start(f32[33,128]{1,0:T(8,128)} %constant.54.clone.sx_b) | copy-start | bytes 50692
  10.8 36.1 %copy-start.20 = (f32[33,128]{1,0:T(8,128)S(1)}, f32[33,128]{1,0:T(8,128)}, u32[]{:S(2)}) copy-start(f32[33,128]{1,0:T(8,128)} %constant.53.clone.sx_a) | copy-start | bytes 50692
  10.9 36.1 %copy-start.22 = (f32[16,128]{1,0:T(8,128)S(1)}, f32[16,128]{1,0:T(8,128)}, u32[]{:S(2)}) copy-start(f32[16,128]{1,0:T(8,128)} %constant.56.clone.sy_b) | copy-start | bytes 24580
  10.9 36.1 %copy-start.23 = (f32[16,128]{1,0:T(8,128)S(1)}, f32[16,128]{1,0:T(8,128)}, u32[]{:S(2)}) copy-start(f32[16,128]{1,0:T(8,128)} %constant.55.clone.sy_a) | copy-start | bytes 24580
  46.8 0.7 copy-start.24
  46.8 0.7 copy-start.25
  47.5 1.0 copy-start.11
  48.5 0.9 copy-start.12
  49.4 0.9 copy-start.13
  58.3 26.1 %copy-start.7 = (f32[1,32768]{1,0:T(1,128)S(1)}, f32[1,32768]{1,0:T(1,128)}, u32[]{:S(2)}) copy-start(f32[1,32768]{1,0:T(1,128)} %param.28) | copy-start | bytes 393220
  58.3 26.0 %copy-start.8 = (bf16[256,512]{1,0:T(8,128)(2,1)S(1)}, bf16[256,512]{1,0:T(8,128)(2,1)}, u32[]{:S(2)}) copy-start(bf16[256,512]{1,0:T(8,128)(2,1)} %constant.59.clone.inverse_lo) | copy-start | bytes 786436
  58.3 26.0 %copy-start.9 = (bf16[256,512]{1,0:T(8,128)(2,1)S(1)}, bf16[256,512]{1,0:T(8,128)(2,1)}, u32[]{:S(2)}) copy-start(bf16[256,512]{1,0:T(8,128)(2,1)} %constant.58.clone.inverse_hi) | copy-start | bytes 786436
  58.4 26.0 %copy-start.17 = (f32[32768]{0:T(1024)S(1)}, f32[32768]{0:T(1024)}, u32[]{:S(2)}) copy-start(f32[32768]{0:T(1024)} %param.31) | copy-start | bytes 393220
  90.8 18.3 %copy-start.16 = (f32[1,32768]{1,0:T(1,128)S(1)}, f32[1,32768]{1,0:T(1,128)}, u32[]{:S(2)}) copy-start(f32[1,32768]{1,0:T(1,128)} %param.27) | copy-start | bytes 393220

commit v3 on v2

v3 whole, which is shorter than its diff:
```python
import jax
import jax.numpy as jnp
import ml_dtypes
import numpy as np
from jax import lax
from jax.experimental import pallas as pl
from jax.experimental.pallas import tpu as pltpu
from jax.sharding import PartitionSpec as P

GRID_X, GRID_Y, GRID_Z = 128, 256, 256
BIN = 128
N_PX, N_PY = 32, 8
DEVICES = N_PX * N_PY
ROWS, COLUMNS = GRID_X // N_PX, GRID_Y // N_PY
SPAN_X, SPAN_Y = ROWS + 3, COLUMNS + 3
CELLS = 256
M_X, M_Y, M_Z = 2 * GRID_X, 2 * GRID_Y, 2 * GRID_Z - 1
BINS = 256
SPREAD_GROUP, READ_GROUP = 32, 64
BLOCK_X, BLOCK_Y = M_X // ROWS, M_Y // COLUMNS
CHUNKS = 3
PER_CHUNK = (BLOCK_X // 2 + 1) // CHUNKS
CHUNK = PER_CHUNK * BLOCK_Y
BACK = 384
SMALL_ROWS = 208

f32, bf16 = jnp.float32, jnp.bfloat16


def halves(table):
    table = np.asarray(table, np.float64)
    high = table.astype(np.float32).astype(ml_dtypes.bfloat16)
    low = (table - high.astype(np.float64)).astype(np.float32).astype(ml_dtypes.bfloat16)
    return np.concatenate([high, low], -1)


def depth_tables():
    freq = np.arange(GRID_Z)[:, None]
    depth = np.arange(GRID_Z)[None, :]
    angle = 2 * np.pi * (freq * depth % M_Z) / M_Z
    forward = np.concatenate([np.cos(angle), -np.sin(angle)], 0)
    doubled = np.where(freq == 0, 1.0, 2.0) / M_Z
    inverse = np.concatenate([np.cos(angle) * doubled, -np.sin(angle) * doubled], 0).T
    return halves(forward), halves(inverse)


def plane_tables():
    kx = np.arange(BLOCK_X // 2 + 1)
    ky = np.arange(BLOCK_Y)
    source = np.arange(DEVICES)
    px, py = source // N_PY, source % N_PY
    phase = (kx[:, None, None] * px / BLOCK_X + ky[None, :, None] * py / BLOCK_Y) * 2 * np.pi
    phase = phase.reshape(CHUNKS, CHUNK, DEVICES)
    blocks = np.concatenate([np.cos(phase), np.sin(phase)], 1)
    back = np.pad(blocks.transpose(0, 2, 1), ((0, 0), (0, 0), (0, BACK - 2 * CHUNK)))
    lane = np.arange(CELLS)
    live = lane < SPAN_X * SPAN_Y
    a, e = lane // SPAN_Y - 1, lane % SPAN_Y - 1
    twist_x = 2 * np.pi * kx[:, None] * a / M_X
    twist_y = 2 * np.pi * ky[:, None] * e / M_Y
    out = np.arange(ROWS * COLUMNS)
    high_x, high_y = out // COLUMNS, out % COLUMNS
    inner = 2 * np.pi * (a[:, None] * high_x[None, :] / ROWS + e[:, None] * high_y[None, :] / COLUMNS)
    c, s = np.cos(inner) * live[:, None], np.sin(inner) * live[:, None]
    full_x = BLOCK_X * high_x[None, :]
    full_y = BLOCK_Y * high_y[None, :]
    sine_x = [np.sin(np.pi * (sign * kx[:, None] + full_x) / M_X) ** 2 for sign in (1, -1)]
    sine_y = [np.sin(np.pi * (sign * ky[:, None] + full_y) / M_Y) ** 2 for sign in (1, -1)]
    scale = 1.0 / (M_X * M_Y)
    weight = np.where((kx == 0) | (kx == BLOCK_X // 2), 0.0, scale)[:, None] * np.ones((1, ROWS * COLUMNS))
    depth_sine = np.sin(np.pi * np.arange(GRID_Z) / M_Z) ** 2
    rows = [np.zeros((SMALL_ROWS, CELLS))]
    rows[0][0:16], rows[0][16:32] = np.cos(twist_y), -np.sin(twist_y)
    rows[0][32:48] = np.concatenate(sine_y, 1)
    rows[0][48:81], rows[0][88:121] = np.cos(twist_x), -np.sin(twist_x)
    rows[0][128:161] = np.concatenate(sine_x, 1)
    rows[0][168:201, :128] = weight
    rows[0][201] = depth_sine
    return (
        halves(blocks),
        halves(back),
        halves(np.block([[c, -s], [s, c]])),
        halves(np.block([[c.T, s.T], [-s.T, c.T]])),
        rows[0].astype(np.float32),
    )


def split(values):
    high = values.astype(bf16)
    return high, (values - high.astype(f32)).astype(bf16)


def dot(a, b):
    return jnp.dot(a, b, preferred_element_type=f32)


def dot_nt(a, b):
    return lax.dot_general(a, b, (((1,), (1,)), ((), ())), preferred_element_type=f32)


def dot3(a, b, mul=dot):
    side = 1 if mul is dot_nt else 0
    return mul(jnp.concatenate([a[0], a[0], a[1]], 1), jnp.concatenate([b[0], b[1], b[0]], side))


def cubic_weights(t):
    return (
        ((-0.5 * t + 1.0) * t - 0.5) * t,
        (1.5 * t - 2.5) * t * t + 1.0,
        ((-1.5 * t + 2.0) * t + 0.5) * t,
        (0.5 * t - 0.5) * t * t,
    )


def one_hot(hit):
    return jnp.where(hit, 1.0, 0.0).astype(bf16)


def iota(shape, dim):
    return lax.broadcasted_iota(jnp.int32, shape, dim)


def stencil_cells(base):
    shift = iota(base.shape, 1) - base
    return jnp.concatenate([one_hot(shift == a * SPAN_Y + e) for a in range(4) for e in range(4)], 0)


def same_bin(shape, group):
    return ((iota(shape, 0) ^ iota(shape, 1)) & (group - 1)) == 0


def group_slice(g, size):
    return pl.ds(pl.multiple_of(g * size, size), size)


def twice(lanes):
    return jnp.concatenate([lanes, lanes], 1)


def spread_kernel(
    direction_hbm, offsets_hbm, cells_hbm, forward_hbm,
    out, offsets, base, depth,
    direction, cells, forward, q_hi, q_lo, sems,
):
    group = SPREAD_GROUP
    copies = [
        pltpu.make_async_copy(cells_hbm, cells, sems.at[0]),
        pltpu.make_async_copy(direction_hbm, direction, sems.at[1]),
        *(pltpu.make_async_copy(offsets_hbm.at[:, d, :], offsets.at[d], sems.at[2 + d]) for d in range(3)),
        pltpu.make_async_copy(forward_hbm, forward, sems.at[5]),
    ]
    for copy in copies:
        copy.start()
    copies[0].wait()
    first = (cells[0:1, :] - lax.axis_index("px") * ROWS) * SPAN_Y + cells[1:2, :] - lax.axis_index("py") * COLUMNS
    packed = (first + 256 * cells[2:3, :]).astype(f32)
    own = iota((BINS, BINS), 0) == iota((BINS, BINS), 1)
    packed = jnp.sum(jnp.where(own, packed, 0.0), axis=1, keepdims=True).astype(jnp.int32)
    base[...] = jnp.broadcast_to(packed & 255, (BINS, 128))
    depth[...] = jnp.broadcast_to(packed >> 8, (BINS, 128))
    for copy in copies[1:5]:
        copy.wait()

    def step(g, _):
        bins = group_slice(g, group)
        wx = cubic_weights(offsets[0, bins, :])
        wy = cubic_weights(offsets[1, bins, :])
        wz = cubic_weights(offsets[2, bins, :])
        d = direction[bins, :]
        wx = [w * d for w in wx]
        columns = split(jnp.concatenate([x * y for x in wx for y in wy], 0))
        depths = split(jnp.concatenate(wz, 0))
        patches = dot3(depths, columns, dot_nt)
        patches = split(jnp.where(same_bin(patches.shape, group), patches, 0.0))
        placed = split(dot(jnp.concatenate(patches, 1), jnp.concatenate([stencil_cells(twice(base[bins, :]))] * 2, 0)))
        for f in range(4):
            rows = pl.ds(pl.multiple_of(f * BINS + g * group, group), group)
            q_hi[rows, :] = placed[0][f * group : (f + 1) * group]
            q_lo[rows, :] = placed[1][f * group : (f + 1) * group]
        return 0

    lax.fori_loop(0, BINS // group, step, 0, unroll=4)
    shift = iota((GRID_Z, BINS), 0) - cells[2:3, :]
    at_depth = jnp.concatenate([one_hot(shift == f - 1) for f in range(4)], 1)
    gridded = split(dot(twice(at_depth), jnp.concatenate([q_hi[...], q_lo[...]], 0)))
    copies[5].wait()
    transformed = dot3((forward[:, :GRID_Z], forward[:, GRID_Z:]), gridded)
    for part in range(2):
        for half in range(2):
            out[pl.ds(2 * part + half, GRID_Z, stride=4), :] = transformed[
                part * GRID_Z : (part + 1) * GRID_Z, half * 128 : (half + 1) * 128
            ]


def plane_kernel(
    lengths, received, blocks, back, inner, inner_back, small, out, r_hi, r_lo, wide, m_hi, m_lo, narrow, g_hi, g_lo
):
    for j in range(4):
        lanes = slice(128 * j, 128 * (j + 1))
        r_hi[:, lanes], r_lo[:, lanes] = split(received[pl.ds(j, DEVICES, stride=4), :])
    scale_x, scale_y = lengths[0] * lengths[0], lengths[1] * lengths[1]
    frequency = lax.axis_index("px") * N_PY + lax.axis_index("py")
    sine = jnp.sum(jnp.where(iota((1, GRID_Z), 1) == frequency, small[201:202, :], 0.0), axis=1, keepdims=True)
    rest = 1.0 + lengths[2] * lengths[2] * sine
    factor = 2.0 * lengths[0] * lengths[1] * lengths[2]
    ty_re, ty_im = small[0:16, :], small[16:32, :]
    rest_y = [rest + scale_y * small[32:48, 128 * part : 128 * (part + 1)] for part in range(2)]
    total = 0.0
    for c in range(CHUNKS):
        left = (blocks[c, :, :DEVICES], blocks[c, :, DEVICES:])
        wide[c] = dot3(left, (r_hi[...], r_lo[...]))
        spans = []
        for j in range(PER_CHUNK):
            kx = c * PER_CHUNK + j
            top = slice(j * BLOCK_Y, (j + 1) * BLOCK_Y)
            bottom = slice(CHUNK + j * BLOCK_Y, CHUNK + (j + 1) * BLOCK_Y)
            tx_re, tx_im = small[48 + kx : 49 + kx, :], small[88 + kx : 89 + kx, :]
            spans.append((kx, top, bottom, tx_re * ty_re - tx_im * ty_im, tx_re * ty_im + tx_im * ty_re))
        for kx, top, bottom, tr, ti in spans:
            cre, cim = wide[c, top, :CELLS], wide[c, top, CELLS:]
            sre, sim = wide[c, bottom, :CELLS], wide[c, bottom, CELLS:]
            ur, ui, vr, vi = cre + sim, cim - sre, cre - sim, cim + sre
            for rows, re, im in (
                (top, ur * tr - ui * ti, ur * ti + ui * tr),
                (bottom, vr * tr + vi * ti, vi * tr - vr * ti),
            ):
                m_hi[c, rows, :CELLS], m_lo[c, rows, :CELLS] = split(re)
                m_hi[c, rows, CELLS:], m_lo[c, rows, CELLS:] = split(im)
        narrow[c] = dot3((m_hi[c], m_lo[c]), (inner[:, :CELLS], inner[:, CELLS:]))
        for kx, top, bottom, tr, ti in spans:
            for part, rows in enumerate((top, bottom)):
                lanes = slice(128 * part, 128 * (part + 1))
                denominator = rest_y[part] + scale_x * small[128 + kx : 129 + kx, lanes]
                weight = factor * (1.0 / (M_X * M_Y)) if part == 0 else factor * small[168 + kx : 169 + kx, :128]
                spectrum = twice(weight / (denominator * denominator))
                g_hi[c, rows, :], g_lo[c, rows, :] = split(narrow[c, rows, :] * spectrum)
        wide[c] = dot3((g_hi[c], g_lo[c]), (inner_back[:, : 2 * CELLS], inner_back[:, 2 * CELLS :]))
        for kx, top, bottom, tr, ti in spans:
            zr, zi = wide[c, top, :CELLS], wide[c, top, CELLS:]
            yr, yi = wide[c, bottom, :CELLS], wide[c, bottom, CELLS:]
            ar, ai = zr * tr + zi * ti, zi * tr - zr * ti
            br, bi = yr * tr - yi * ti, yr * ti + yi * tr
            for rows, re, im in ((top, ar + br, ai + bi), (bottom, bi - ai, ar - br)):
                m_hi[c, rows, :CELLS], m_lo[c, rows, :CELLS] = split(re)
                m_hi[c, rows, CELLS:], m_lo[c, rows, CELLS:] = split(im)
        left = (back[c, :, : 2 * CHUNK], back[c, :, BACK : BACK + 2 * CHUNK])
        total = total + dot3(left, (m_hi[c], m_lo[c]))
    for j in range(4):
        out[pl.ds(j, DEVICES, stride=4), :] = total[:, 128 * j : 128 * (j + 1)]


def gather_kernel(received, direction, residual, noise, offsets, base, depth, inverse, image, sums, v_hi, v_lo):
    group = READ_GROUP
    for part in range(2):
        for half in range(2):
            rows = slice(part * GRID_Z, (part + 1) * GRID_Z)
            lanes = slice(half * 128, (half + 1) * 128)
            v_hi[rows, lanes], v_lo[rows, lanes] = split(received[pl.ds(2 * part + half, GRID_Z, stride=4), :])
    grid = split(dot3((inverse[:, : 2 * GRID_Z], inverse[:, 2 * GRID_Z :]), (v_hi[...], v_lo[...])))
    v_hi[:GRID_Z, :], v_lo[:GRID_Z, :] = grid

    def step(g, carry):
        bins = group_slice(g, group)
        shift = iota((group, GRID_Z), 1) - twice(depth[bins, :])
        at_depth = jnp.concatenate([one_hot(shift == f - 1) for f in range(4)], 0)
        lines_hi = dot(at_depth, v_hi[:GRID_Z, :]).astype(bf16)
        lines_lo = dot(at_depth, v_lo[:GRID_Z, :]).astype(bf16)
        cells = stencil_cells(twice(base[bins, :]))
        keep = same_bin((16 * group, 4 * group), group)
        read_hi = jnp.where(keep, dot_nt(cells, lines_hi), 0.0).astype(bf16)
        read_lo = jnp.where(keep, dot_nt(cells, lines_lo), 0.0).astype(bf16)
        depths = split(jnp.concatenate(cubic_weights(offsets[2, bins, :]), 0))
        along = dot3((read_hi, read_lo), depths)
        wx = cubic_weights(offsets[0, bins, :])
        wy = cubic_weights(offsets[1, bins, :])
        value = 0.0
        for a in range(4):
            row = 0.0
            for e in range(4):
                start = (4 * a + e) * group
                row = row + wy[e] * along[start : start + group]
            value = value + wx[a] * row
        d, r = direction[bins, :], residual[bins, :]
        value = value + noise[bins, :] * d
        image[bins, :] = value
        return tuple(
            total + (x * y).reshape(group // 8, 8, BIN).sum(0)
            for total, (x, y) in zip(carry, ((r, r), (d, value), (r, value), (value, value)))
        )

    zero = jnp.zeros((8, BIN), f32)
    totals = lax.fori_loop(0, BINS // group, step, (zero,) * 4, unroll=2)
    lane = iota((1, BIN), 1)
    row = jnp.zeros((1, BIN), f32)
    for j, part in enumerate(totals):
        row = jnp.where(lane == j, jnp.sum(part, keepdims=True), row)
    sums[...] = jnp.broadcast_to(row, (DEVICES, BIN))


def step_kernel(sums, iterate, residual, direction, image, new_iterate, new_residual, new_direction):
    row = jnp.sum(sums[...], axis=0, keepdims=True)
    old_norm, curvature, cross, square = (row[:, j : j + 1] for j in range(4))
    step = old_norm / curvature
    new_norm = old_norm - 2.0 * step * cross + step * step * square
    d = direction[...]
    r = residual[...] - step * image[...]
    new_iterate[...] = iterate[...] + step * d
    new_residual[...] = r
    new_direction[...] = r + (new_norm / old_norm) * d


VMEM = pl.BlockSpec(memory_space=pltpu.VMEM)
HBM = pl.BlockSpec(memory_space=pltpu.HBM)
SMEM = pl.BlockSpec(memory_space=pltpu.SMEM)


def params():
    return pltpu.CompilerParams(vmem_limit_bytes=16 * 1024 * 1024)


def on_device(solution, residual, direction, offsets, noise, bin_cells, lengths):
    forward, inverse = depth_tables()
    d, r = direction.reshape(BINS, BIN), residual.reshape(BINS, BIN)
    point = jax.ShapeDtypeStruct((BINS, BIN), f32)
    index = jax.ShapeDtypeStruct((BINS, BIN), jnp.int32)
    block = jax.ShapeDtypeStruct((4 * DEVICES, 128), f32)

    blocks, by_bin, base, depth = pl.pallas_call(
        spread_kernel,
        out_shape=(block, jax.ShapeDtypeStruct((3, BINS, BIN), f32), index, index),
        in_specs=[HBM] * 4,
        out_specs=(VMEM,) * 4,
        scratch_shapes=[
            pltpu.VMEM((BINS, BIN), f32),
            pltpu.VMEM((3, BINS), jnp.int32),
            pltpu.VMEM(forward.shape, bf16),
            pltpu.VMEM((4 * BINS, CELLS), bf16),
            pltpu.VMEM((4 * BINS, CELLS), bf16),
            pltpu.SemaphoreType.DMA((6,)),
        ],
        compiler_params=params(),
        name="spread",
    )(d, offsets.reshape(3, BINS, BIN).transpose(1, 0, 2), bin_cells, forward)
    received = lax.all_to_all(blocks.reshape(DEVICES, 4, 128), ("px", "py"), 0, 0, tiled=True)

    filtered = pl.pallas_call(
        plane_kernel,
        out_shape=block,
        in_specs=[SMEM] + [VMEM] * 6,
        out_specs=VMEM,
        scratch_shapes=[
            pltpu.VMEM((DEVICES, 512), bf16),
            pltpu.VMEM((DEVICES, 512), bf16),
            pltpu.VMEM((CHUNKS, 2 * CHUNK, 512), f32),
            pltpu.VMEM((CHUNKS, 2 * CHUNK, 512), bf16),
            pltpu.VMEM((CHUNKS, 2 * CHUNK, 512), bf16),
            pltpu.VMEM((CHUNKS, 2 * CHUNK, 256), f32),
            pltpu.VMEM((CHUNKS, 2 * CHUNK, 256), bf16),
            pltpu.VMEM((CHUNKS, 2 * CHUNK, 256), bf16),
        ],
        compiler_params=params(),
        name="plane",
    )(lengths, received.reshape(4 * DEVICES, 128), *plane_tables())
    returned = lax.all_to_all(filtered.reshape(DEVICES, 4, 128), ("px", "py"), 0, 0, tiled=True)

    image, sums = pl.pallas_call(
        gather_kernel,
        out_shape=(point, jax.ShapeDtypeStruct((DEVICES, BIN), f32)),
        in_specs=[VMEM] * 8,
        out_specs=(VMEM, VMEM),
        scratch_shapes=[pltpu.VMEM((2 * GRID_Z, CELLS), bf16)] * 2,
        compiler_params=params(),
        name="interpolate",
    )(returned.reshape(4 * DEVICES, 128), d, r, noise.reshape(BINS, BIN), by_bin, base, depth, inverse)

    everywhere = lax.all_to_all(sums.reshape(DEVICES, 1, BIN), ("px", "py"), 0, 0, tiled=True)
    outs = pl.pallas_call(
        step_kernel,
        out_shape=(point,) * 3,
        in_specs=[VMEM] * 5,
        out_specs=(VMEM,) * 3,
        compiler_params=params(),
        name="step",
    )(everywhere.reshape(DEVICES, BIN), solution.reshape(BINS, BIN), r, d, image)
    return tuple(out.reshape(1, -1) for out in outs)


def solution(mesh):
    points = P(None, ("px", "py"))
    return jax.shard_map(
        on_device,
        mesh=mesh,
        in_specs=(points, points, points, points, P(("px", "py")), points, P()),
        out_specs=(points, points, points),
        check_vma=False,
    )
```

time: 110 us -> 104 us (0.945)
  Pallas kernels: 20.7 us -> 16.6 us
  local copies, waits for them, and re-layouts: 8.14 us -> 5.97 us
    pallas_call x4, Pallas kernels: 20.7 us -> 16.6 us  [the longest x1 7 us: on_device(): pl.pallas_call(plane_kernel, out_shape=block, in_specs=[SMEM] + [VMEM] *...]
    unnamed x54 -> x30, local copies, waits for them, and re-layouts: 8.14 us -> 5.97 us
where the time goes in v3:
time: 104 us
  blocking collectives  80.3 us (77%)
  Pallas kernels  16.6 us (16%)
  local copies, waits for them, and re-layouts  5.97 us (6%)
    all_to_all x1, blocking collectives, on_device(): lax.all_to_all(blocks.reshape(DEVICES, 4, 128), ('px', 'py'), 0, 0, tiled...  36 us
    all_to_all x1, blocking collectives, on_device(): lax.all_to_all(filtered.reshape(DEVICES, 4, 128), ('px', 'py'), 0, 0, til...  26 us
    all_to_all x1, blocking collectives, on_device(): lax.all_to_all(sums.reshape(DEVICES, 1, BIN), ('px', 'py'), 0, 0, tiled=T...  18.3 us
    pallas_call x1, Pallas kernels, on_device(): pl.pallas_call(plane_kernel, out_shape=block, in_specs=[SMEM] + [VMEM] *...  7 us
    unnamed x30, local copies, waits for them, and re-layouts  5.97 us
    pallas_call x1, Pallas kernels, on_device(): pl.pallas_call(spread_kernel, out_shape=(block, jax.ShapeDtypeStruct((3,...  4.55 us
    pallas_call x1, Pallas kernels, on_device(): pl.pallas_call(gather_kernel, out_shape=(point, jax.ShapeDtypeStruct((DEV...  4.09 us

profile of v3, /device:TPU:1, one launch (start us, length us, event | category | flops | bytes accessed | tf_op | source)
XLA Modules:
  0.0 103.5 jit_solution(12354782502450074871)
XLA Ops:
  0.6 0.0 copy-start
  0.6 0.0 copy-start.1
  0.7 1.0 copy-done.1
  1.6 0.0 copy-start.7
  1.6 1.0 %copy-done.7 = f32[3,32768]{1,0:T(4,128)S(1)} copy-done((f32[3,32768]{1,0:T(4,128)S(1)}, f32[3,32768]{1,0:T(4,128)}, u32[]{:S(2)}) %copy-start.7) | copy-done | bytes 393240
  2.7 0.0 copy-start.8
  2.7 1.0 %copy-done.8 = bf16[512,512]{1,0:T(8,128)(2,1)S(1)} copy-done((bf16[512,512]{1,0:T(8,128)(2,1)S(1)}, bf16[512,512]{1,0:T(8,128)(2,1)}, u32[]{:S(2)}) %copy-start.8) | copy-done | bytes 524312
  3.7 0.0 copy-start.13
  3.7 0.7 copy-done.13
  4.4 0.0 copy-start.4
  4.4 0.0 copy-start.5
  4.4 0.0 copy-start.14
  4.4 4.5 %spread.1 = (f32[1024,128]{1,0:T(8,128)S(1)}, f32[3,256,128]{2,1,0:T(8,128)S(1)}, s32[256,128]{1,0:T(8,128)S(1)}, s32[256,128]{1,0:T(8,128)S(1)}) custom-call(f32[256,128]{1,0:T(8,128)S(1)} %bitcast.21, f32[256,3,128]{2,1,0:T(4,128)S(1)} %bitcast.27, s32[3,256]{1,0:T(4,128)S(1)} %copy-done.13, bf16[512,512]{1,0:T(8,128)(2,1)S(1)} %copy-done.8), custom_call_target="tpu_custom_call" | custom-call | tf_op jit(solution)/shard_map/spread/pallas_call | solution.py:328
  9.0 36.0 %all_to_all.15 = f32[256,4,128]{2,1,0:T(4,128)S(1)} all-to-all(f32[256,4,128]{2,1,0:T(4,128)S(1)} %bitcast.28), channel_id=1, replica_groups=mesh['px'=32,'py'=8] {'px','py'}, dimensions={0} | all-to-all | bytes 1048576 | tf_op jit(solution)/shard_map/all_to_all | solution.py:344
  44.9 0.0 copy-done
  44.9 0.0 copy-done.4
  44.9 0.0 copy-done.5
  45.0 0.0 copy-done.14
  45.0 0.0 copy-start.3
  45.0 1.2 %copy-done.3 = bf16[3,352,512]{2,1,0:T(8,128)(2,1)S(1)} copy-done((bf16[3,352,512]{2,1,0:T(8,128)(2,1)S(1)}, bf16[3,352,512]{2,1,0:T(8,128)(2,1)}, u32[]{:S(2)}) %copy-start.3) | copy-done | bytes 1081368
  46.2 0.0 copy-start.10
  46.2 0.9 copy-done.10
  47.1 0.0 copy-start.2
  47.1 0.0 copy-start.6
  47.1 0.0 copy-start.11
  47.1 7.0 %plane.1 = f32[1024,128]{1,0:T(8,128)S(1)} custom-call(f32[3]{0:T(128)S(1)} %copy-done.14, f32[1024,128]{1,0:T(8,128)S(1)} %bitcast.18, bf16[3,352,512]{2,1,0:T(8,128)(2,1)S(1)} %copy-done.3, bf16[3,256,768]{2,1,0:T(8,128)(2,1)S(1)} %copy-done, bf16[512,512]{1,0:T(8,128)(2,1)S(1)} %copy-done.5, bf16[256,1024]{1,0:T(8,128)(2,1)S(1)} %copy-done.4, ...), custom_call_target="tpu_custom_call" | custom-call | tf_op jit(solution)/shard_map/plane/pallas_call | solution.py:346
  54.1 0.0 copy-start.9
  54.2 26.0 %all_to_all.16 = f32[256,4,128]{2,1,0:T(4,128)S(1)} all-to-all(f32[256,4,128]{2,1,0:T(4,128)S(1)} %bitcast.19), channel_id=1, replica_groups=mesh['px'=32,'py'=8] {'px','py'}, dimensions={0} | all-to-all | bytes 1048576 | tf_op jit(solution)/shard_map/all_to_all | solution.py:364
  80.2 0.0 copy-done.2
  80.2 0.0 copy-done.6
  80.2 0.0 copy-done.11
  80.2 0.0 copy-done.9
  80.2 0.0 copy-start.12
  80.2 4.1 %interpolate.1 = (f32[256,128]{1,0:T(8,128)S(1)}, f32[256,128]{1,0:T(8,128)S(1)}) custom-call(f32[1024,128]{1,0:T(8,128)S(1)} %bitcast.20, f32[256,128]{1,0:T(8,128)S(1)} %bitcast.22, f32[256,128]{1,0:T(8,128)S(1)} %bitcast.24, f32[256,128]{1,0:T(8,128)S(1)} %bitcast.29, f32[3,256,128]{2,1,0:T(8,128)S(1)} %get-tuple-element.13.offsets, ...), custom_call_target="tpu_custom_call" | custom-call | tf_op jit(solution)/shard_map/interpolate/pallas_call | solution.py:366
  84.3 18.3 %all_to_all.17 = f32[256,1,128]{2,1,0:T(1,128)S(1)} all-to-all(f32[256,1,128]{2,1,0:T(1,128)S(1)} %bitcast.31), channel_id=1, replica_groups=mesh['px'=32,'py'=8] {'px','py'}, dimensions={0} | all-to-all | bytes 262144 | tf_op jit(solution)/shard_map/all_to_all | solution.py:376
  102.6 0.0 copy-done.12
  102.6 0.9 step.1
Async XLA Ops:
  0.6 44.3 %copy-start = (bf16[3,256,768]{2,1,0:T(8,128)(2,1)S(1)}, bf16[3,256,768]{2,1,0:T(8,128)(2,1)}, u32[]{:S(2)}) copy-start(bf16[3,256,768]{2,1,0:T(8,128)(2,1)} %constant.16.clone.back) | copy-start | bytes 3538948
  0.6 1.0 copy-start.1
  1.6 1.0 %copy-start.7 = (f32[3,32768]{1,0:T(4,128)S(1)}, f32[3,32768]{1,0:T(4,128)}, u32[]{:S(2)}) copy-start(f32[3,32768]{1,0:T(4,128)} %param.17) | copy-start | bytes 1179652
  2.7 1.0 %copy-start.8 = (bf16[512,512]{1,0:T(8,128)(2,1)S(1)}, bf16[512,512]{1,0:T(8,128)(2,1)}, u32[]{:S(2)}) copy-start(bf16[512,512]{1,0:T(8,128)(2,1)} %constant.14.clone.forward_hbm) | copy-start | bytes 1572868
  3.7 0.7 copy-start.13
  4.4 40.5 %copy-start.4 = (bf16[256,1024]{1,0:T(8,128)(2,1)S(1)}, bf16[256,1024]{1,0:T(8,128)(2,1)}, u32[]{:S(2)}) copy-start(bf16[256,1024]{1,0:T(8,128)(2,1)} %constant.18.clone.inner_back) | copy-start | bytes 1572868
  4.4 40.5 %copy-start.5 = (bf16[512,512]{1,0:T(8,128)(2,1)S(1)}, bf16[512,512]{1,0:T(8,128)(2,1)}, u32[]{:S(2)}) copy-start(bf16[512,512]{1,0:T(8,128)(2,1)} %constant.17.clone.inner) | copy-start | bytes 1572868
  4.4 40.5 %copy-start.14 = (f32[3]{0:T(128)S(1)}, f32[3]{0:T(128)}, u32[]{:S(2)}) copy-start(f32[3]{0:T(128)} %lengths.1) | copy-start | bytes 40
  45.0 1.2 %copy-start.3 = (bf16[3,352,512]{2,1,0:T(8,128)(2,1)S(1)}, bf16[3,352,512]{2,1,0:T(8,128)(2,1)}, u32[]{:S(2)}) copy-start(bf16[3,352,512]{2,1,0:T(8,128)(2,1)} %constant.15.clone.blocks) | copy-start | bytes 3244036
  46.2 0.9 copy-start.10
  47.1 33.0 %copy-start.2 = (f32[1,32768]{1,0:T(1,128)S(1)}, f32[1,32768]{1,0:T(1,128)}, u32[]{:S(2)}) copy-start(f32[1,32768]{1,0:T(1,128)} %param.16) | copy-start | bytes 393220
  47.1 33.0 %copy-start.6 = (f32[1,32768]{1,0:T(1,128)S(1)}, f32[1,32768]{1,0:T(1,128)}, u32[]{:S(2)}) copy-start(f32[1,32768]{1,0:T(1,128)} %param.15) | copy-start | bytes 393220
  47.1 33.0 %copy-start.11 = (f32[32768]{0:T(1024)S(1)}, f32[32768]{0:T(1024)}, u32[]{:S(2)}) copy-start(f32[32768]{0:T(1024)} %param.18) | copy-start | bytes 393220
  54.1 26.0 %copy-start.9 = (bf16[256,1024]{1,0:T(8,128)(2,1)S(1)}, bf16[256,1024]{1,0:T(8,128)(2,1)}, u32[]{:S(2)}) copy-start(bf16[256,1024]{1,0:T(8,128)(2,1)} %constant.20.clone.inverse) | copy-start | bytes 1572868
  80.2 22.4 %copy-start.12 = (f32[1,32768]{1,0:T(1,128)S(1)}, f32[1,32768]{1,0:T(1,128)}, u32[]{:S(2)}) copy-start(f32[1,32768]{1,0:T(1,128)} %param.14) | copy-start | bytes 393220

commit v4 on v3

--- a/solution.py
+++ b/solution.py
@@ -23,6 +23,7 @@
 CHUNK = PER_CHUNK * BLOCK_Y
 BACK = 384
 SMALL_ROWS = 208
+TABLES = 5
 
 f32, bf16 = jnp.float32, jnp.bfloat16
 
@@ -138,16 +139,17 @@
 
 
 def spread_kernel(
-    direction_hbm, offsets_hbm, cells_hbm, forward_hbm,
-    out, offsets, base, depth,
-    direction, cells, forward, q_hi, q_lo, sems,
+    direction_hbm, offsets_hbm, cells_hbm, forward_hbm, *refs
 ):
+    tables_hbm, (out, offsets, base, depth), tables = refs[:TABLES], refs[TABLES : TABLES + 4], refs[TABLES + 4 : 2 * TABLES + 4]
+    direction, cells, forward, q_hi, q_lo, sems = refs[2 * TABLES + 4 :]
     group = SPREAD_GROUP
     copies = [
         pltpu.make_async_copy(cells_hbm, cells, sems.at[0]),
         pltpu.make_async_copy(direction_hbm, direction, sems.at[1]),
         *(pltpu.make_async_copy(offsets_hbm.at[:, d, :], offsets.at[d], sems.at[2 + d]) for d in range(3)),
         pltpu.make_async_copy(forward_hbm, forward, sems.at[5]),
+        *(pltpu.make_async_copy(tables_hbm[t], tables[t], sems.at[6 + t]) for t in range(TABLES)),
     ]
     for copy in copies:
         copy.start()
@@ -190,6 +192,8 @@
             out[pl.ds(2 * part + half, GRID_Z, stride=4), :] = transformed[
                 part * GRID_Z : (part + 1) * GRID_Z, half * 128 : (half + 1) * 128
             ]
+    for copy in copies[6:]:
+        copy.wait()
 
 
 def plane_kernel(
@@ -325,22 +329,29 @@
     index = jax.ShapeDtypeStruct((BINS, BIN), jnp.int32)
     block = jax.ShapeDtypeStruct((4 * DEVICES, 128), f32)
 
-    blocks, by_bin, base, depth = pl.pallas_call(
+    tables = plane_tables()
+    by_tile = offsets.reshape(3, BINS, BIN).transpose(1, 0, 2)
+    operands = [pltpu.with_memory_space_constraint(x, pltpu.HBM) for x in (d, by_tile, bin_cells, forward, *tables)]
+
+    blocks, by_bin, base, depth, *tables = pl.pallas_call(
         spread_kernel,
-        out_shape=(block, jax.ShapeDtypeStruct((3, BINS, BIN), f32), index, index),
-        in_specs=[HBM] * 4,
-        out_specs=(VMEM,) * 4,
+        out_shape=(
+            block, jax.ShapeDtypeStruct((3, BINS, BIN), f32), index, index,
+            *(jax.ShapeDtypeStruct(t.shape, t.dtype) for t in tables),
+        ),
+        in_specs=[HBM] * len(operands),
+        out_specs=(VMEM,) * (4 + TABLES),
         scratch_shapes=[
             pltpu.VMEM((BINS, BIN), f32),
             pltpu.VMEM((3, BINS), jnp.int32),
             pltpu.VMEM(forward.shape, bf16),
             pltpu.VMEM((4 * BINS, CELLS), bf16),
             pltpu.VMEM((4 * BINS, CELLS), bf16),
-            pltpu.SemaphoreType.DMA((6,)),
+            pltpu.SemaphoreType.DMA((6 + TABLES,)),
         ],
         compiler_params=params(),
         name="spread",
-    )(d, offsets.reshape(3, BINS, BIN).transpose(1, 0, 2), bin_cells, forward)
+    )(*operands)
     received = lax.all_to_all(blocks.reshape(DEVICES, 4, 128), ("px", "py"), 0, 0, tiled=True)
 
     filtered = pl.pallas_call(
@@ -360,7 +371,7 @@
         ],
         compiler_params=params(),
         name="plane",
-    )(lengths, received.reshape(4 * DEVICES, 128), *plane_tables())
+    )(lengths, received.reshape(4 * DEVICES, 128), *tables)
     returned = lax.all_to_all(filtered.reshape(DEVICES, 4, 128), ("px", "py"), 0, 0, tiled=True)
 
     image, sums = pl.pallas_call(

time: 104 us -> 98.2 us (0.944)
  local copies, waits for them, and re-layouts: 5.97 us -> 0.03 us
    unnamed x30 -> x12, local copies, waits for them, and re-layouts: 5.97 us -> 0.03 us
where the time goes in v4:
time: 98.2 us; the launch traced here: 98 us
  blocking collectives  80.3 us (82%)
  Pallas kernels  17 us (17%)
    all_to_all x1, blocking collectives, on_device(): lax.all_to_all(blocks.reshape(DEVICES, 4, 128), ('px', 'py'), 0, 0, tiled...  36 us
    all_to_all x1, blocking collectives, on_device(): lax.all_to_all(filtered.reshape(DEVICES, 4, 128), ('px', 'py'), 0, 0, til...  26 us
    all_to_all x1, blocking collectives, on_device(): lax.all_to_all(sums.reshape(DEVICES, 1, BIN), ('px', 'py'), 0, 0, tiled=T...  18.3 us
    pallas_call x1, Pallas kernels, on_device(): pl.pallas_call(plane_kernel, out_shape=block, in_specs=[SMEM] + [VMEM] *...  6.9 us
    pallas_call x1, Pallas kernels, on_device(): pl.pallas_call(spread_kernel, out_shape=(block, jax.ShapeDtypeStruct((3,...  5.1 us
    pallas_call x1, Pallas kernels, on_device(): pl.pallas_call(gather_kernel, out_shape=(point, jax.ShapeDtypeStruct((DEV...  4.08 us

profile of v4, /device:TPU:1, one launch (start us, length us, event | category | flops | bytes accessed | tf_op | source)
XLA Modules:
  0.0 98.0 jit_solution(1092496513478975183)
XLA Ops:
  0.6 0.0 copy-start.5
  0.6 5.1 %spread.1 = (f32[1024,128]{1,0:T(8,128)S(1)}, f32[3,256,128]{2,1,0:T(8,128)S(1)}, s32[256,128]{1,0:T(8,128)S(1)}, s32[256,128]{1,0:T(8,128)S(1)}, bf16[3,352,512...) custom-call(f32[256,128]{1,0:T(8,128)} %bitcast.21, ...), custom_call_target="tpu_custom_call" | custom-call | tf_op jit(solution)/shard_map/spread/pallas_call | solution.py:336
  5.8 36.0 %all_to_all.15 = f32[256,4,128]{2,1,0:T(4,128)S(1)} all-to-all(f32[256,4,128]{2,1,0:T(4,128)S(1)} %bitcast.27), channel_id=1, replica_groups=mesh['px'=32,'py'=8] {'px','py'}, dimensions={0} | all-to-all | bytes 1048576 | tf_op jit(solution)/shard_map/all_to_all | solution.py:355
  41.7 0.0 copy-done.5
  41.7 0.0 copy-start
  41.7 0.0 copy-start.1
  41.7 0.0 copy-start.3
  41.7 6.9 %plane.1 = f32[1024,128]{1,0:T(8,128)S(1)} custom-call(f32[3]{0:T(128)S(1)} %copy-done.5, f32[1024,128]{1,0:T(8,128)S(1)} %bitcast.18, bf16[3,352,512]{2,1,0:T(8,128)(2,1)S(1)} %get-tuple-element.18.blocks, bf16[3,256,768]{2,1,0:T(8,128)(2,1)S(1)} %get-tuple-element.19.back, bf16[512,512]{1,0:T(8,128)(2,1)S(1)} %get-tuple-element.20.inner, ...), custom_call_target="tpu_custom_call" | custom-call | tf_op jit(solution)/shard_map/plane/pallas_call | solution.py:357
  48.6 0.0 copy-start.2
  48.6 26.0 %all_to_all.16 = f32[256,4,128]{2,1,0:T(4,128)S(1)} all-to-all(f32[256,4,128]{2,1,0:T(4,128)S(1)} %bitcast.19), channel_id=1, replica_groups=mesh['px'=32,'py'=8] {'px','py'}, dimensions={0} | all-to-all | bytes 1048576 | tf_op jit(solution)/shard_map/all_to_all | solution.py:375
  74.7 0.0 copy-done
  74.7 0.0 copy-done.1
  74.7 0.0 copy-done.3
  74.7 0.0 copy-done.2
  74.7 0.0 copy-start.4
  74.7 4.1 %interpolate.1 = (f32[256,128]{1,0:T(8,128)S(1)}, f32[256,128]{1,0:T(8,128)S(1)}) custom-call(f32[1024,128]{1,0:T(8,128)S(1)} %bitcast.20, f32[256,128]{1,0:T(8,128)S(1)} %bitcast.22, f32[256,128]{1,0:T(8,128)S(1)} %bitcast.24, f32[256,128]{1,0:T(8,128)S(1)} %bitcast.28, f32[3,256,128]{2,1,0:T(8,128)S(1)} %get-tuple-element.23.offsets, ...), custom_call_target="tpu_custom_call" | custom-call | tf_op jit(solution)/shard_map/interpolate/pallas_call | solution.py:377
  78.8 18.3 %all_to_all.17 = f32[256,1,128]{2,1,0:T(1,128)S(1)} all-to-all(f32[256,1,128]{2,1,0:T(1,128)S(1)} %bitcast.30), channel_id=1, replica_groups=mesh['px'=32,'py'=8] {'px','py'}, dimensions={0} | all-to-all | bytes 262144 | tf_op jit(solution)/shard_map/all_to_all | solution.py:387
  97.1 0.0 copy-done.4
  97.1 0.9 step.1
Async XLA Ops:
  0.6 41.1 %copy-start.5 = (f32[3]{0:T(128)S(1)}, f32[3]{0:T(128)}, u32[]{:S(2)}) copy-start(f32[3]{0:T(128)} %lengths.1) | copy-start | bytes 40
  41.7 32.9 %copy-start = (f32[1,32768]{1,0:T(1,128)S(1)}, f32[1,32768]{1,0:T(1,128)}, u32[]{:S(2)}) copy-start(f32[1,32768]{1,0:T(1,128)} %param.16) | copy-start | bytes 393220
  41.7 32.9 %copy-start.1 = (f32[1,32768]{1,0:T(1,128)S(1)}, f32[1,32768]{1,0:T(1,128)}, u32[]{:S(2)}) copy-start(f32[1,32768]{1,0:T(1,128)} %param.15) | copy-start | bytes 393220
  41.7 32.9 %copy-start.3 = (f32[32768]{0:T(1024)S(1)}, f32[32768]{0:T(1024)}, u32[]{:S(2)}) copy-start(f32[32768]{0:T(1024)} %param.18) | copy-start | bytes 393220
  48.6 26.0 %copy-start.2 = (bf16[256,1024]{1,0:T(8,128)(2,1)S(1)}, bf16[256,1024]{1,0:T(8,128)(2,1)}, u32[]{:S(2)}) copy-start(bf16[256,1024]{1,0:T(8,128)(2,1)} %constant.20.clone.inverse) | copy-start | bytes 1572868
  74.7 22.4 %copy-start.4 = (f32[1,32768]{1,0:T(1,128)S(1)}, f32[1,32768]{1,0:T(1,128)}, u32[]{:S(2)}) copy-start(f32[1,32768]{1,0:T(1,128)} %param.14) | copy-start | bytes 393220

commit v5 on v4

--- a/solution.py
+++ b/solution.py
@@ -16,7 +16,7 @@
 CELLS = 256
 M_X, M_Y, M_Z = 2 * GRID_X, 2 * GRID_Y, 2 * GRID_Z - 1
 BINS = 256
-SPREAD_GROUP, READ_GROUP = 32, 64
+SPREAD_GROUP, READ_GROUP = 32, 32
 BLOCK_X, BLOCK_Y = M_X // ROWS, M_Y // COLUMNS
 CHUNKS = 3
 PER_CHUNK = (BLOCK_X // 2 + 1) // CHUNKS
@@ -99,9 +99,13 @@
     return lax.dot_general(a, b, (((1,), (1,)), ((), ())), preferred_element_type=f32)
 
 
-def dot3(a, b, mul=dot):
-    side = 1 if mul is dot_nt else 0
-    return mul(jnp.concatenate([a[0], a[0], a[1]], 1), jnp.concatenate([b[0], b[1], b[0]], side))
+def dot3(a, b):
+    return dot(jnp.concatenate([a[0], a[0], a[1]], 1), jnp.concatenate([b[0], b[1], b[0]], 0))
+
+
+def interleave(parts):
+    while parts:
+        parts = [part for part in parts if next(part, 0) is None]
 
 
 def cubic_weights(t):
@@ -131,7 +135,7 @@
 
 
 def group_slice(g, size):
-    return pl.ds(pl.multiple_of(g * size, size), size)
+    return slice(g * size, (g + 1) * size)
 
 
 def twice(lanes):
@@ -163,28 +167,46 @@
     for copy in copies[1:5]:
         copy.wait()
 
-    def step(g, _):
+    def multiplied(g):
         bins = group_slice(g, group)
         wx = cubic_weights(offsets[0, bins, :])
         wy = cubic_weights(offsets[1, bins, :])
         wz = cubic_weights(offsets[2, bins, :])
         d = direction[bins, :]
         wx = [w * d for w in wx]
-        columns = split(jnp.concatenate([x * y for x in wx for y in wy], 0))
-        depths = split(jnp.concatenate(wz, 0))
-        patches = dot3(depths, columns, dot_nt)
-        patches = split(jnp.where(same_bin(patches.shape, group), patches, 0.0))
-        placed = split(dot(jnp.concatenate(patches, 1), jnp.concatenate([stencil_cells(twice(base[bins, :]))] * 2, 0)))
+        columns = jnp.concatenate(split(jnp.concatenate([x * y for x in wx for y in wy], 0)), 1)
+        depths = twice(jnp.concatenate(split(jnp.concatenate(wz, 0)), 0))
+        yield
+        patches = dot_nt(depths, columns)
+        yield
+        patches = patches[: 4 * group] + patches[4 * group :]
+        patches = jnp.concatenate(split(jnp.where(same_bin(patches.shape, group), patches, 0.0)), 0)
+        cells = stencil_cells(twice(base[bins, :]))
+        yield
+        placed = dot(patches, cells)
+        yield
+        placed = split(placed[: 4 * group] + placed[4 * group :])
         for f in range(4):
-            rows = pl.ds(pl.multiple_of(f * BINS + g * group, group), group)
+            rows = slice((4 * (g // 2) + f) * 2 * group + g % 2 * group, (4 * (g // 2) + f) * 2 * group + (g % 2 + 1) * group)
             q_hi[rows, :] = placed[0][f * group : (f + 1) * group]
             q_lo[rows, :] = placed[1][f * group : (f + 1) * group]
-        return 0
-
-    lax.fori_loop(0, BINS // group, step, 0, unroll=4)
-    shift = iota((GRID_Z, BINS), 0) - cells[2:3, :]
-    at_depth = jnp.concatenate([one_hot(shift == f - 1) for f in range(4)], 1)
-    gridded = split(dot(twice(at_depth), jnp.concatenate([q_hi[...], q_lo[...]], 0)))
+
+    def pair(p, found):
+        parts = [multiplied(2 * p), multiplied(2 * p + 1)]
+        while parts:
+            parts = [part for part in parts if next(part, 0) is None]
+            yield
+        own = cells[2:3, 2 * p * group : 2 * (p + 1) * group]
+        own = jnp.concatenate([own + f - 1 for f in range(4)], 1)
+        at_depth = one_hot(iota((GRID_Z, 8 * group), 0) == own)
+        yield
+        rows = slice(8 * p * group, 8 * (p + 1) * group)
+        found.append(dot(twice(at_depth), jnp.concatenate([q_hi[rows, :], q_lo[rows, :]], 0)))
+        yield
+
+    found = []
+    interleave([pair(p, found) for p in range(BINS // group // 2)])
+    gridded = split(sum(found))
     copies[5].wait()
     transformed = dot3((forward[:, :GRID_Z], forward[:, GRID_Z:]), gridded)
     for part in range(2):
@@ -209,10 +231,10 @@
     factor = 2.0 * lengths[0] * lengths[1] * lengths[2]
     ty_re, ty_im = small[0:16, :], small[16:32, :]
     rest_y = [rest + scale_y * small[32:48, 128 * part : 128 * (part + 1)] for part in range(2)]
-    total = 0.0
-    for c in range(CHUNKS):
+    def chunk(c):
         left = (blocks[c, :, :DEVICES], blocks[c, :, DEVICES:])
         wide[c] = dot3(left, (r_hi[...], r_lo[...]))
+        yield
         spans = []
         for j in range(PER_CHUNK):
             kx = c * PER_CHUNK + j
@@ -230,7 +252,9 @@
             ):
                 m_hi[c, rows, :CELLS], m_lo[c, rows, :CELLS] = split(re)
                 m_hi[c, rows, CELLS:], m_lo[c, rows, CELLS:] = split(im)
+        yield
         narrow[c] = dot3((m_hi[c], m_lo[c]), (inner[:, :CELLS], inner[:, CELLS:]))
+        yield
         for kx, top, bottom, tr, ti in spans:
             for part, rows in enumerate((top, bottom)):
                 lanes = slice(128 * part, 128 * (part + 1))
@@ -238,7 +262,9 @@
                 weight = factor * (1.0 / (M_X * M_Y)) if part == 0 else factor * small[168 + kx : 169 + kx, :128]
                 spectrum = twice(weight / (denominator * denominator))
                 g_hi[c, rows, :], g_lo[c, rows, :] = split(narrow[c, rows, :] * spectrum)
+        yield
         wide[c] = dot3((g_hi[c], g_lo[c]), (inner_back[:, : 2 * CELLS], inner_back[:, 2 * CELLS :]))
+        yield
         for kx, top, bottom, tr, ti in spans:
             zr, zi = wide[c, top, :CELLS], wide[c, top, CELLS:]
             yr, yi = wide[c, bottom, :CELLS], wide[c, bottom, CELLS:]
@@ -247,8 +273,12 @@
             for rows, re, im in ((top, ar + br, ai + bi), (bottom, bi - ai, ar - br)):
                 m_hi[c, rows, :CELLS], m_lo[c, rows, :CELLS] = split(re)
                 m_hi[c, rows, CELLS:], m_lo[c, rows, CELLS:] = split(im)
+        yield
         left = (back[c, :, : 2 * CHUNK], back[c, :, BACK : BACK + 2 * CHUNK])
-        total = total + dot3(left, (m_hi[c], m_lo[c]))
+        totals.append(dot3(left, (m_hi[c], m_lo[c])))
+    totals = []
+    interleave([chunk(c) for c in range(CHUNKS)])
+    total = sum(totals)
     for j in range(4):
         out[pl.ds(j, DEVICES, stride=4), :] = total[:, 128 * j : 128 * (j + 1)]
 
@@ -263,18 +293,24 @@
     grid = split(dot3((inverse[:, : 2 * GRID_Z], inverse[:, 2 * GRID_Z :]), (v_hi[...], v_lo[...])))
     v_hi[:GRID_Z, :], v_lo[:GRID_Z, :] = grid
 
-    def step(g, carry):
+    def step(g, found):
         bins = group_slice(g, group)
         shift = iota((group, GRID_Z), 1) - twice(depth[bins, :])
         at_depth = jnp.concatenate([one_hot(shift == f - 1) for f in range(4)], 0)
-        lines_hi = dot(at_depth, v_hi[:GRID_Z, :]).astype(bf16)
-        lines_lo = dot(at_depth, v_lo[:GRID_Z, :]).astype(bf16)
+        yield
+        lines = [dot(at_depth, v[:GRID_Z, :]).astype(bf16) for v in (v_hi, v_lo)]
+        lines = jnp.concatenate(lines, 0)
         cells = stencil_cells(twice(base[bins, :]))
-        keep = same_bin((16 * group, 4 * group), group)
-        read_hi = jnp.where(keep, dot_nt(cells, lines_hi), 0.0).astype(bf16)
-        read_lo = jnp.where(keep, dot_nt(cells, lines_lo), 0.0).astype(bf16)
-        depths = split(jnp.concatenate(cubic_weights(offsets[2, bins, :]), 0))
-        along = dot3((read_hi, read_lo), depths)
+        yield
+        read = dot_nt(cells, lines)
+        yield
+        read = jnp.where(same_bin(read.shape, group), read, 0.0).astype(bf16)
+        depths = jnp.concatenate(split(jnp.concatenate(cubic_weights(offsets[2, bins, :]), 0)), 1)
+        depths = jnp.concatenate([depths, depths], 0)
+        yield
+        along = dot(read, depths)
+        yield
+        along = along[:, :BIN] + along[:, BIN:]
         wx = cubic_weights(offsets[0, bins, :])
         wy = cubic_weights(offsets[1, bins, :])
         value = 0.0
@@ -287,13 +323,11 @@
         d, r = direction[bins, :], residual[bins, :]
         value = value + noise[bins, :] * d
         image[bins, :] = value
-        return tuple(
-            total + (x * y).reshape(group // 8, 8, BIN).sum(0)
-            for total, (x, y) in zip(carry, ((r, r), (d, value), (r, value), (value, value)))
-        )
-
-    zero = jnp.zeros((8, BIN), f32)
-    totals = lax.fori_loop(0, BINS // group, step, (zero,) * 4, unroll=2)
+        found.append([(x * y).reshape(group // 8, 8, BIN).sum(0) for x, y in ((r, r), (d, value), (r, value), (value, value))])
+
+    found = []
+    interleave([step(g, found) for g in range(BINS // group)])
+    totals = [sum(parts) for parts in zip(*found)]
     lane = iota((1, BIN), 1)
     row = jnp.zeros((1, BIN), f32)
     for j, part in enumerate(totals):

time: 98.2 us -> 93 us (0.947)
  Pallas kernels: 17 us -> 11.8 us
    pallas_call x1, Pallas kernels: 6.9 us -> 4.59 us  [on_device(): pl.pallas_call(plane_kernel, out_shape=block, in_specs=[SMEM] + [VMEM] *...]
    pallas_call x1, Pallas kernels: 4.08 us -> 2.5 us  [on_device(): pl.pallas_call(gather_kernel, out_shape=(point, jax.ShapeDtypeStruct((DEV...]
    pallas_call x1, Pallas kernels: 5.1 us -> 3.82 us  [on_device(): pl.pallas_call(spread_kernel, out_shape=(block, jax.ShapeDtypeStruct((3,...]
where the time goes in v5:
time: 93 us; the launch traced here: 92.8 us
  blocking collectives  80.3 us (86%)
  Pallas kernels  11.8 us (13%)
    all_to_all x1, blocking collectives, on_device(): lax.all_to_all(blocks.reshape(DEVICES, 4, 128), ('px', 'py'), 0, 0, tiled...  36 us
    all_to_all x1, blocking collectives, on_device(): lax.all_to_all(filtered.reshape(DEVICES, 4, 128), ('px', 'py'), 0, 0, til...  26 us
    all_to_all x1, blocking collectives, on_device(): lax.all_to_all(sums.reshape(DEVICES, 1, BIN), ('px', 'py'), 0, 0, tiled=T...  18.3 us
    pallas_call x1, Pallas kernels, on_device(): pl.pallas_call(plane_kernel, out_shape=block, in_specs=[SMEM] + [VMEM] *...  4.59 us
    pallas_call x1, Pallas kernels, on_device(): pl.pallas_call(spread_kernel, out_shape=(block, jax.ShapeDtypeStruct((3,...  3.82 us
    pallas_call x1, Pallas kernels, on_device(): pl.pallas_call(gather_kernel, out_shape=(point, jax.ShapeDtypeStruct((DEV...  2.5 us

profile of v5, /device:TPU:1, one launch (start us, length us, event | category | flops | bytes accessed | tf_op | source)
XLA Modules:
  0.0 92.8 jit_solution(17208818409475154642)
XLA Ops:
  0.6 0.0 copy-start.5
  0.6 3.8 %spread.1 = (f32[1024,128]{1,0:T(8,128)S(1)}, f32[3,256,128]{2,1,0:T(8,128)S(1)}, s32[256,128]{1,0:T(8,128)S(1)}, s32[256,128]{1,0:T(8,128)S(1)}, bf16[3,352,512...) custom-call(f32[256,128]{1,0:T(8,128)} %bitcast.21, ...), custom_call_target="tpu_custom_call" | custom-call | tf_op jit(solution)/shard_map/spread/pallas_call | solution.py:370
  4.5 36.0 %all_to_all.15 = f32[256,4,128]{2,1,0:T(4,128)S(1)} all-to-all(f32[256,4,128]{2,1,0:T(4,128)S(1)} %bitcast.27), channel_id=1, replica_groups=mesh['px'=32,'py'=8] {'px','py'}, dimensions={0} | all-to-all | bytes 1048576 | tf_op jit(solution)/shard_map/all_to_all | solution.py:389
  40.4 0.0 copy-done.5
  40.4 0.0 copy-start
  40.4 0.0 copy-start.1
  40.4 0.0 copy-start.3
  40.5 4.6 %plane.1 = f32[1024,128]{1,0:T(8,128)S(1)} custom-call(f32[3]{0:T(128)S(1)} %copy-done.5, f32[1024,128]{1,0:T(8,128)S(1)} %bitcast.18, bf16[3,352,512]{2,1,0:T(8,128)(2,1)S(1)} %get-tuple-element.18.blocks, bf16[3,256,768]{2,1,0:T(8,128)(2,1)S(1)} %get-tuple-element.19.back, bf16[512,512]{1,0:T(8,128)(2,1)S(1)} %get-tuple-element.20.inner, ...), custom_call_target="tpu_custom_call" | custom-call | tf_op jit(solution)/shard_map/plane/pallas_call | solution.py:391
  45.0 0.0 copy-start.2
  45.1 26.0 %all_to_all.16 = f32[256,4,128]{2,1,0:T(4,128)S(1)} all-to-all(f32[256,4,128]{2,1,0:T(4,128)S(1)} %bitcast.19), channel_id=1, replica_groups=mesh['px'=32,'py'=8] {'px','py'}, dimensions={0} | all-to-all | bytes 1048576 | tf_op jit(solution)/shard_map/all_to_all | solution.py:409
  71.1 0.0 copy-done
  71.1 0.0 copy-done.1
  71.1 0.0 copy-done.3
  71.1 0.0 copy-done.2
  71.1 0.0 copy-start.4
  71.1 2.5 %interpolate.1 = (f32[256,128]{1,0:T(8,128)S(1)}, f32[256,128]{1,0:T(8,128)S(1)}) custom-call(f32[1024,128]{1,0:T(8,128)S(1)} %bitcast.20, f32[256,128]{1,0:T(8,128)S(1)} %bitcast.22, f32[256,128]{1,0:T(8,128)S(1)} %bitcast.24, f32[256,128]{1,0:T(8,128)S(1)} %bitcast.28, f32[3,256,128]{2,1,0:T(8,128)S(1)} %get-tuple-element.23.offsets, ...), custom_call_target="tpu_custom_call" | custom-call | tf_op jit(solution)/shard_map/interpolate/pallas_call | solution.py:411
  73.6 18.3 %all_to_all.17 = f32[256,1,128]{2,1,0:T(1,128)S(1)} all-to-all(f32[256,1,128]{2,1,0:T(1,128)S(1)} %bitcast.30), channel_id=1, replica_groups=mesh['px'=32,'py'=8] {'px','py'}, dimensions={0} | all-to-all | bytes 262144 | tf_op jit(solution)/shard_map/all_to_all | solution.py:421
  91.9 0.0 copy-done.4
  91.9 0.9 step.1
Async XLA Ops:
  0.6 39.8 %copy-start.5 = (f32[3]{0:T(128)S(1)}, f32[3]{0:T(128)}, u32[]{:S(2)}) copy-start(f32[3]{0:T(128)} %lengths.1) | copy-start | bytes 40
  40.4 30.6 %copy-start = (f32[1,32768]{1,0:T(1,128)S(1)}, f32[1,32768]{1,0:T(1,128)}, u32[]{:S(2)}) copy-start(f32[1,32768]{1,0:T(1,128)} %param.16) | copy-start | bytes 393220
  40.4 30.6 %copy-start.1 = (f32[1,32768]{1,0:T(1,128)S(1)}, f32[1,32768]{1,0:T(1,128)}, u32[]{:S(2)}) copy-start(f32[1,32768]{1,0:T(1,128)} %param.15) | copy-start | bytes 393220
  40.4 30.6 %copy-start.3 = (f32[32768]{0:T(1024)S(1)}, f32[32768]{0:T(1024)}, u32[]{:S(2)}) copy-start(f32[32768]{0:T(1024)} %param.18) | copy-start | bytes 393220
  45.0 26.0 %copy-start.2 = (bf16[256,1024]{1,0:T(8,128)(2,1)S(1)}, bf16[256,1024]{1,0:T(8,128)(2,1)}, u32[]{:S(2)}) copy-start(bf16[256,1024]{1,0:T(8,128)(2,1)} %constant.20.clone.inverse) | copy-start | bytes 1572868
  71.1 20.8 %copy-start.4 = (f32[1,32768]{1,0:T(1,128)S(1)}, f32[1,32768]{1,0:T(1,128)}, u32[]{:S(2)}) copy-start(f32[1,32768]{1,0:T(1,128)} %param.14) | copy-start | bytes 393220

commit v6 on v5

--- a/solution.py
+++ b/solution.py
@@ -13,17 +13,12 @@
 DEVICES = N_PX * N_PY
 ROWS, COLUMNS = GRID_X // N_PX, GRID_Y // N_PY
 SPAN_X, SPAN_Y = ROWS + 3, COLUMNS + 3
-CELLS = 256
+CELLS, OWN, RIM = 256, 128, 64
 M_X, M_Y, M_Z = 2 * GRID_X, 2 * GRID_Y, 2 * GRID_Z - 1
 BINS = 256
 SPREAD_GROUP, READ_GROUP = 32, 32
-BLOCK_X, BLOCK_Y = M_X // ROWS, M_Y // COLUMNS
-CHUNKS = 3
-PER_CHUNK = (BLOCK_X // 2 + 1) // CHUNKS
-CHUNK = PER_CHUNK * BLOCK_Y
-BACK = 384
-SMALL_ROWS = 208
-TABLES = 5
+TABLES = 7
+SLOTS = (1, 2, 3, 4, 5, 6, 0)
 
 f32, bf16 = jnp.float32, jnp.bfloat16
 
@@ -45,44 +40,35 @@
     return halves(forward), halves(inverse)
 
 
+def cas(product, length):
+    angle = 2 * np.pi * (product % length) / length
+    return np.cos(angle) + np.sin(angle)
+
+
 def plane_tables():
-    kx = np.arange(BLOCK_X // 2 + 1)
-    ky = np.arange(BLOCK_Y)
-    source = np.arange(DEVICES)
-    px, py = source // N_PY, source % N_PY
-    phase = (kx[:, None, None] * px / BLOCK_X + ky[None, :, None] * py / BLOCK_Y) * 2 * np.pi
-    phase = phase.reshape(CHUNKS, CHUNK, DEVICES)
-    blocks = np.concatenate([np.cos(phase), np.sin(phase)], 1)
-    back = np.pad(blocks.transpose(0, 2, 1), ((0, 0), (0, 0), (0, BACK - 2 * CHUNK)))
-    lane = np.arange(CELLS)
-    live = lane < SPAN_X * SPAN_Y
-    a, e = lane // SPAN_Y - 1, lane % SPAN_Y - 1
-    twist_x = 2 * np.pi * kx[:, None] * a / M_X
-    twist_y = 2 * np.pi * ky[:, None] * e / M_Y
-    out = np.arange(ROWS * COLUMNS)
-    high_x, high_y = out // COLUMNS, out % COLUMNS
-    inner = 2 * np.pi * (a[:, None] * high_x[None, :] / ROWS + e[:, None] * high_y[None, :] / COLUMNS)
-    c, s = np.cos(inner) * live[:, None], np.sin(inner) * live[:, None]
-    full_x = BLOCK_X * high_x[None, :]
-    full_y = BLOCK_Y * high_y[None, :]
-    sine_x = [np.sin(np.pi * (sign * kx[:, None] + full_x) / M_X) ** 2 for sign in (1, -1)]
-    sine_y = [np.sin(np.pi * (sign * ky[:, None] + full_y) / M_Y) ** 2 for sign in (1, -1)]
-    scale = 1.0 / (M_X * M_Y)
-    weight = np.where((kx == 0) | (kx == BLOCK_X // 2), 0.0, scale)[:, None] * np.ones((1, ROWS * COLUMNS))
-    depth_sine = np.sin(np.pi * np.arange(GRID_Z) / M_Z) ** 2
-    rows = [np.zeros((SMALL_ROWS, CELLS))]
-    rows[0][0:16], rows[0][16:32] = np.cos(twist_y), -np.sin(twist_y)
-    rows[0][32:48] = np.concatenate(sine_y, 1)
-    rows[0][48:81], rows[0][88:121] = np.cos(twist_x), -np.sin(twist_x)
-    rows[0][128:161] = np.concatenate(sine_x, 1)
-    rows[0][168:201, :128] = weight
-    rows[0][201] = depth_sine
+    kx, ky = np.arange(M_X), np.arange(M_Y)
+    px = np.arange(N_PX)
+    x = np.concatenate([ROWS * px + slot - 1 for slot in SLOTS])
+    along_x = np.zeros((M_X, DEVICES))
+    along_x[:, : len(x)] = cas(kx[:, None] * x[None, :], M_X)
+    along_y = cas(np.arange(GRID_Y)[:, None] * ky[None, :], M_Y)
+    sine_x = np.sin(np.pi * kx / M_X) ** 2
+    sines = np.zeros((8, M_Y), np.float32)
+    sines[0] = np.sin(np.pi * ky / M_Y) ** 2
+    sines[1, :GRID_Z] = np.sin(np.pi * np.arange(GRID_Z) / M_Z) ** 2
+    rim = np.zeros((OWN, CELLS), np.float32)
+    for row in range(SPAN_X):
+        start = {0: OWN + 96, 5: OWN, 6: OWN + 32}.get(row, (row - 1) * COLUMNS)
+        for q, column in enumerate((COLUMNS - 1, 0, 1)):
+            rim[RIM + 3 * row + q, start + column] = 1.0
     return (
-        halves(blocks),
-        halves(back),
-        halves(np.block([[c, -s], [s, c]])),
-        halves(np.block([[c.T, s.T], [-s.T, c.T]])),
-        rows[0].astype(np.float32),
+        halves(along_x),
+        halves(along_x.T),
+        halves(along_y),
+        halves(along_y.T),
+        np.repeat(sine_x[:, None], 128, 1).astype(np.float32),
+        sines,
+        rim.astype(ml_dtypes.bfloat16),
     )
 
 
@@ -125,8 +111,20 @@
     return lax.broadcasted_iota(jnp.int32, shape, dim)
 
 
+def cell_index():
+    lane = iota((1, CELLS), 1)
+    place, part = lane & 127, (lane & 127) >> 5
+    row = jnp.where(lane < OWN, part + 1, jnp.where(part == 3, 0, part + 5))
+    rim = place - RIM
+    rim_row = (rim * 11) >> 5
+    q = rim - 3 * rim_row
+    rim_column = jnp.where(q == 0, 0, q + COLUMNS)
+    rim_cell = jnp.where(rim < 3 * SPAN_X, rim_row * SPAN_Y + rim_column, -(1 << 20))
+    return jnp.where((lane >= OWN) & (part == 2), rim_cell, row * SPAN_Y + (lane & 31) + 1)
+
+
 def stencil_cells(base):
-    shift = iota(base.shape, 1) - base
+    shift = cell_index() - base
     return jnp.concatenate([one_hot(shift == a * SPAN_Y + e) for a in range(4) for e in range(4)], 0)
 
 
@@ -218,69 +216,93 @@
         copy.wait()
 
 
+def moved(values, rows):
+    return pltpu.roll(values, rows % DEVICES, 0)
+
+
+def turned(values, lanes):
+    return pltpu.roll(values, lanes % 128, 1) if lanes % 128 else values
+
+
+def by_quarter(pieces):
+    quarter = iota(pieces[0].shape, 1) >> 5
+    result = 0.0
+    for q, piece in enumerate(pieces):
+        if piece is not None:
+            result = jnp.where(quarter == q, piece, result)
+    return result
+
+
 def plane_kernel(
-    lengths, received, blocks, back, inner, inner_back, small, out, r_hi, r_lo, wide, m_hi, m_lo, narrow, g_hi, g_lo
+    lengths, received, along_x, back_x, along_y, back_y, sine_x, sines, rim, out, tiles, x_hi, x_lo, spectrum
 ):
-    for j in range(4):
-        lanes = slice(128 * j, 128 * (j + 1))
-        r_hi[:, lanes], r_lo[:, lanes] = split(received[pl.ds(j, DEVICES, stride=4), :])
-    scale_x, scale_y = lengths[0] * lengths[0], lengths[1] * lengths[1]
-    frequency = lax.axis_index("px") * N_PY + lax.axis_index("py")
-    sine = jnp.sum(jnp.where(iota((1, GRID_Z), 1) == frequency, small[201:202, :], 0.0), axis=1, keepdims=True)
-    rest = 1.0 + lengths[2] * lengths[2] * sine
-    factor = 2.0 * lengths[0] * lengths[1] * lengths[2]
-    ty_re, ty_im = small[0:16, :], small[16:32, :]
-    rest_y = [rest + scale_y * small[32:48, 128 * part : 128 * (part + 1)] for part in range(2)]
-    def chunk(c):
-        left = (blocks[c, :, :DEVICES], blocks[c, :, DEVICES:])
-        wide[c] = dot3(left, (r_hi[...], r_lo[...]))
-        yield
-        spans = []
-        for j in range(PER_CHUNK):
-            kx = c * PER_CHUNK + j
-            top = slice(j * BLOCK_Y, (j + 1) * BLOCK_Y)
-            bottom = slice(CHUNK + j * BLOCK_Y, CHUNK + (j + 1) * BLOCK_Y)
-            tx_re, tx_im = small[48 + kx : 49 + kx, :], small[88 + kx : 89 + kx, :]
-            spans.append((kx, top, bottom, tx_re * ty_re - tx_im * ty_im, tx_re * ty_im + tx_im * ty_re))
-        for kx, top, bottom, tr, ti in spans:
-            cre, cim = wide[c, top, :CELLS], wide[c, top, CELLS:]
-            sre, sim = wide[c, bottom, :CELLS], wide[c, bottom, CELLS:]
-            ur, ui, vr, vi = cre + sim, cim - sre, cre - sim, cim + sre
-            for rows, re, im in (
-                (top, ur * tr - ui * ti, ur * ti + ui * tr),
-                (bottom, vr * tr + vi * ti, vi * tr - vr * ti),
-            ):
-                m_hi[c, rows, :CELLS], m_lo[c, rows, :CELLS] = split(re)
-                m_hi[c, rows, CELLS:], m_lo[c, rows, CELLS:] = split(im)
-        yield
-        narrow[c] = dot3((m_hi[c], m_lo[c]), (inner[:, :CELLS], inner[:, CELLS:]))
-        yield
-        for kx, top, bottom, tr, ti in spans:
-            for part, rows in enumerate((top, bottom)):
-                lanes = slice(128 * part, 128 * (part + 1))
-                denominator = rest_y[part] + scale_x * small[128 + kx : 129 + kx, lanes]
-                weight = factor * (1.0 / (M_X * M_Y)) if part == 0 else factor * small[168 + kx : 169 + kx, :128]
-                spectrum = twice(weight / (denominator * denominator))
-                g_hi[c, rows, :], g_lo[c, rows, :] = split(narrow[c, rows, :] * spectrum)
-        yield
-        wide[c] = dot3((g_hi[c], g_lo[c]), (inner_back[:, : 2 * CELLS], inner_back[:, 2 * CELLS :]))
-        yield
-        for kx, top, bottom, tr, ti in spans:
-            zr, zi = wide[c, top, :CELLS], wide[c, top, CELLS:]
-            yr, yi = wide[c, bottom, :CELLS], wide[c, bottom, CELLS:]
-            ar, ai = zr * tr + zi * ti, zi * tr - zr * ti
-            br, bi = yr * tr - yi * ti, yr * ti + yi * tr
-            for rows, re, im in ((top, ar + br, ai + bi), (bottom, bi - ai, ar - br)):
-                m_hi[c, rows, :CELLS], m_lo[c, rows, :CELLS] = split(re)
-                m_hi[c, rows, CELLS:], m_lo[c, rows, CELLS:] = split(im)
-        yield
-        left = (back[c, :, : 2 * CHUNK], back[c, :, BACK : BACK + 2 * CHUNK])
-        totals.append(dot3(left, (m_hi[c], m_lo[c])))
-    totals = []
-    interleave([chunk(c) for c in range(CHUNKS)])
-    total = sum(totals)
-    for j in range(4):
-        out[pl.ds(j, DEVICES, stride=4), :] = total[:, 128 * j : 128 * (j + 1)]
+    last_column = (iota((DEVICES, CELLS), 1) & 31) == COLUMNS - 1
+    quarter = iota((DEVICES, OWN), 1) >> 5
+    place = ((0, 0), (0, 1), (0, 2), (0, 3), (1, 0), (1, 1), (1, 3))
+
+    def filtering():
+        yield
+        scale_x, scale_y = lengths[0] * lengths[0], lengths[1] * lengths[1]
+        frequency = lax.axis_index("px") * N_PY + lax.axis_index("py")
+        sine = jnp.where(iota((1, GRID_Z), 1) == frequency, sines[1:2, :GRID_Z], 0.0)
+        rest = 1.0 + lengths[2] * lengths[2] * jnp.sum(sine, axis=1, keepdims=True)
+        factor = 2.0 / (M_X * M_Y) * lengths[0] * lengths[1] * lengths[2]
+        rows = rest + scale_x * sine_x[...]
+        for j in range(M_Y // 128):
+            lanes = slice(128 * j, 128 * (j + 1))
+            denominator = rows + scale_y * sines[0:1, lanes]
+            spectrum[:, lanes] = factor / (denominator * denominator)
+
+    def plane(part):
+        own, rest = (received[pl.ds(2 * part + half, DEVICES, stride=4), :] for half in range(2))
+        rims = dot(jnp.concatenate(split(rest), 0), rim[...])
+        yield
+        columns = rims[:DEVICES] + rims[DEVICES:]
+        columns = jnp.where(last_column, moved(columns, -1), moved(columns, 1))
+        tiles[part, 0] = own + columns[:, :OWN]
+        tiles[part, 1] = jnp.where(quarter == 2, 0.0, rest) + columns[:, OWN:]
+        loaded = [[tiles[part, tile, pl.ds(py, N_PX, stride=N_PY), :] for py in range(N_PY)] for tile in range(2)]
+        for slot, (tile, q) in enumerate(place):
+            rows = slice(slot * N_PX, (slot + 1) * N_PX)
+            for half in range(2):
+                lanes = slice(128 * half, 128 * (half + 1))
+                values = by_quarter([turned(loaded[tile][4 * half + p], 32 * (p - q)) for p in range(4)])
+                x_hi[part, rows, lanes], x_lo[part, rows, lanes] = split(values)
+        empty = slice(len(place) * N_PX, DEVICES)
+        x_hi[part, empty, :] = jnp.zeros((N_PX, GRID_Y), bf16)
+        x_lo[part, empty, :] = jnp.zeros((N_PX, GRID_Y), bf16)
+        yield
+        values = dot3((along_x[:, :DEVICES], along_x[:, DEVICES:]), (x_hi[part], x_lo[part]))
+        yield
+        values = split(values)
+        yield
+        values = dot3(values, (along_y[:, :M_Y], along_y[:, M_Y:]))
+        yield
+        values = split(values * spectrum[...])
+        yield
+        values = dot3(values, (back_y[:, :GRID_Y], back_y[:, GRID_Y:]))
+        yield
+        values = split(values)
+        yield
+        values = dot3((back_x[:, :M_X], back_x[:, M_X:]), values)
+        yield
+        for py in range(N_PY):
+            lanes = slice(128 * (py // 4), 128 * (py // 4 + 1))
+            pieces = [[None] * 4, [None] * 4]
+            for slot, (tile, q) in enumerate(place):
+                pieces[tile][q] = turned(values[slot * N_PX : (slot + 1) * N_PX, lanes], 32 * (q - py % 4))
+            for tile in range(2):
+                tiles[part, tile, pl.ds(py, N_PX, stride=N_PY), :] = by_quarter(pieces[tile])
+        own, rest = tiles[part, 0], tiles[part, 1]
+        out[pl.ds(2 * part, DEVICES, stride=4), :] = own
+        region = jnp.concatenate([own, rest], 1)
+        region = jnp.concatenate(split(jnp.where(last_column, moved(region, 1), moved(region, -1))), 0)
+        yield
+        rims = dot_nt(region, rim[...])
+        yield
+        out[pl.ds(2 * part + 1, DEVICES, stride=4), :] = rest + rims[:DEVICES] + rims[DEVICES:]
+
+    interleave([plane(0), plane(1), filtering()])
 
 
 def gather_kernel(received, direction, residual, noise, offsets, base, depth, inverse, image, sums, v_hi, v_lo):
@@ -354,6 +376,23 @@
 
 def params():
     return pltpu.CompilerParams(vmem_limit_bytes=16 * 1024 * 1024)
+
+
+def filter_plane(lengths, received, tables):
+    return pl.pallas_call(
+        plane_kernel,
+        out_shape=jax.ShapeDtypeStruct((4 * DEVICES, 128), f32),
+        in_specs=[SMEM] + [VMEM] * (1 + TABLES),
+        out_specs=VMEM,
+        scratch_shapes=[
+            pltpu.VMEM((2, 2, DEVICES, OWN), f32),
+            pltpu.VMEM((2, DEVICES, GRID_Y), bf16),
+            pltpu.VMEM((2, DEVICES, GRID_Y), bf16),
+            pltpu.VMEM((M_X, M_Y), f32),
+        ],
+        compiler_params=params(),
+        name="plane",
+    )(lengths, received, *tables)
 
 
 def on_device(solution, residual, direction, offsets, noise, bin_cells, lengths):
@@ -388,24 +427,7 @@
     )(*operands)
     received = lax.all_to_all(blocks.reshape(DEVICES, 4, 128), ("px", "py"), 0, 0, tiled=True)
 
-    filtered = pl.pallas_call(
-        plane_kernel,
-        out_shape=block,
-        in_specs=[SMEM] + [VMEM] * 6,
-        out_specs=VMEM,
-        scratch_shapes=[
-            pltpu.VMEM((DEVICES, 512), bf16),
-            pltpu.VMEM((DEVICES, 512), bf16),
-            pltpu.VMEM((CHUNKS, 2 * CHUNK, 512), f32),
-            pltpu.VMEM((CHUNKS, 2 * CHUNK, 512), bf16),
-            pltpu.VMEM((CHUNKS, 2 * CHUNK, 512), bf16),
-            pltpu.VMEM((CHUNKS, 2 * CHUNK, 256), f32),
-            pltpu.VMEM((CHUNKS, 2 * CHUNK, 256), bf16),
-            pltpu.VMEM((CHUNKS, 2 * CHUNK, 256), bf16),
-        ],
-        compiler_params=params(),
-        name="plane",
-    )(lengths, received.reshape(4 * DEVICES, 128), *tables)
+    filtered = filter_plane(lengths, received.reshape(4 * DEVICES, 128), tables)
     returned = lax.all_to_all(filtered.reshape(DEVICES, 4, 128), ("px", "py"), 0, 0, tiled=True)
 
     image, sums = pl.pallas_call(

time: 93 us -> 92.5 us (level)
  Pallas kernels: 11.8 us -> 10.6 us
    pallas_call x1, Pallas kernels: 4.59 us -> 3.4 us  [filter_plane(): pl.pallas_call(plane_kernel, out_shape=jax.ShapeDtypeStruct((4 * DEVICES,...]
where the time goes in v6:
time: 92.5 us; the launch traced here: 92.3 us
  blocking collectives  80.3 us (87%)
  Pallas kernels  10.6 us (11%)
    all_to_all x1, blocking collectives, on_device(): lax.all_to_all(blocks.reshape(DEVICES, 4, 128), ('px', 'py'), 0, 0, tiled...  36 us
    all_to_all x1, blocking collectives, on_device(): lax.all_to_all(filtered.reshape(DEVICES, 4, 128), ('px', 'py'), 0, 0, til...  26 us
    all_to_all x1, blocking collectives, on_device(): lax.all_to_all(sums.reshape(DEVICES, 1, BIN), ('px', 'py'), 0, 0, tiled=T...  18.3 us
    pallas_call x1, Pallas kernels, on_device(): pl.pallas_call(spread_kernel, out_shape=(block, jax.ShapeDtypeStruct((3,...  3.83 us
    pallas_call x1, Pallas kernels, filter_plane(): pl.pallas_call(plane_kernel, out_shape=jax.ShapeDtypeStruct((4 * DEVICES,...  3.4 us
    pallas_call x1, Pallas kernels, on_device(): pl.pallas_call(gather_kernel, out_shape=(point, jax.ShapeDtypeStruct((DEV...  2.5 us

profile of v6, /device:TPU:1, one launch (start us, length us, event | category | flops | bytes accessed | tf_op | source)
XLA Modules:
  0.0 92.3 jit_solution(4486305080912106936)
XLA Ops:
  0.6 3.8 %spread.1 = (f32[1024,128]{1,0:T(8,128)S(1)}, f32[3,256,128]{2,1,0:T(8,128)S(1)}, s32[256,128]{1,0:T(8,128)S(1)}, s32[256,128]{1,0:T(8,128)S(1)}, bf16[256,512]{...) custom-call(f32[256,128]{1,0:T(8,128)} %bitcast.21, ...), custom_call_target="tpu_custom_call" | custom-call | tf_op jit(solution)/shard_map/spread/pallas_call | solution.py:409
  4.5 36.0 %all_to_all.15 = f32[256,4,128]{2,1,0:T(4,128)S(1)} all-to-all(f32[256,4,128]{2,1,0:T(4,128)S(1)} %bitcast.27), channel_id=1, replica_groups=mesh['px'=32,'py'=8] {'px','py'}, dimensions={0} | all-to-all | bytes 1048576 | tf_op jit(solution)/shard_map/all_to_all | solution.py:428
  40.4 0.0 copy-start.5
  40.4 0.7 copy-done.5
  41.1 3.4 %plane.1 = f32[1024,128]{1,0:T(8,128)S(1)} custom-call(f32[3]{0:T(128)S(1)} %copy-done.5, f32[1024,128]{1,0:T(8,128)S(1)} %bitcast.18, bf16[256,512]{1,0:T(8,128)(2,1)S(1)} %get-tuple-element.20.along_x, bf16[256,512]{1,0:T(8,128)(2,1)S(1)} %get-tuple-element.21.back_x, bf16[256,1024]{1,0:T(8,128)(2,1)S(1)} %get-tuple-element.22.along_y, ...), custom_call_target="tpu_custom_call" | custom-call | tf_op jit(solution)/shard_map/plane/pallas_call | solution.py:382
  44.5 0.0 copy-start
  44.5 0.0 copy-start.1
  44.5 0.0 copy-start.2
  44.5 0.0 copy-start.3
  44.5 26.0 %all_to_all.16 = f32[256,4,128]{2,1,0:T(4,128)S(1)} all-to-all(f32[256,4,128]{2,1,0:T(4,128)S(1)} %bitcast.19), channel_id=1, replica_groups=mesh['px'=32,'py'=8] {'px','py'}, dimensions={0} | all-to-all | bytes 1048576 | tf_op jit(solution)/shard_map/all_to_all | solution.py:431
  70.5 0.0 copy-done
  70.5 0.0 copy-done.1
  70.6 0.0 copy-done.2
  70.6 0.0 copy-done.3
  70.6 2.5 %interpolate.1 = (f32[256,128]{1,0:T(8,128)S(1)}, f32[256,128]{1,0:T(8,128)S(1)}) custom-call(f32[1024,128]{1,0:T(8,128)S(1)} %bitcast.20, f32[256,128]{1,0:T(8,128)S(1)} %bitcast.22, f32[256,128]{1,0:T(8,128)S(1)} %bitcast.24, f32[256,128]{1,0:T(8,128)S(1)} %bitcast.28, f32[3,256,128]{2,1,0:T(8,128)S(1)} %get-tuple-element.27.offsets, ...), custom_call_target="tpu_custom_call" | custom-call | tf_op jit(solution)/shard_map/interpolate/pallas_call | solution.py:433
  73.1 0.0 copy-start.4
  73.1 18.3 %all_to_all.17 = f32[256,1,128]{2,1,0:T(1,128)S(1)} all-to-all(f32[256,1,128]{2,1,0:T(1,128)S(1)} %bitcast.30), channel_id=1, replica_groups=mesh['px'=32,'py'=8] {'px','py'}, dimensions={0} | all-to-all | bytes 262144 | tf_op jit(solution)/shard_map/all_to_all | solution.py:443
  91.4 0.0 copy-done.4
  91.4 0.9 step.1
Async XLA Ops:
  40.4 0.7 copy-start.5
  44.5 26.1 %copy-start = (f32[1,32768]{1,0:T(1,128)S(1)}, f32[1,32768]{1,0:T(1,128)}, u32[]{:S(2)}) copy-start(f32[1,32768]{1,0:T(1,128)} %param.18) | copy-start | bytes 393220
  44.5 26.0 %copy-start.1 = (f32[1,32768]{1,0:T(1,128)S(1)}, f32[1,32768]{1,0:T(1,128)}, u32[]{:S(2)}) copy-start(f32[1,32768]{1,0:T(1,128)} %param.17) | copy-start | bytes 393220
  44.5 26.0 %copy-start.2 = (bf16[256,1024]{1,0:T(8,128)(2,1)S(1)}, bf16[256,1024]{1,0:T(8,128)(2,1)}, u32[]{:S(2)}) copy-start(bf16[256,1024]{1,0:T(8,128)(2,1)} %constant.26.clone.inverse) | copy-start | bytes 1572868
  44.5 26.0 %copy-start.3 = (f32[32768]{0:T(1024)S(1)}, f32[32768]{0:T(1024)}, u32[]{:S(2)}) copy-start(f32[32768]{0:T(1024)} %param.20) | copy-start | bytes 393220
  73.1 18.3 %copy-start.4 = (f32[1,32768]{1,0:T(1,128)S(1)}, f32[1,32768]{1,0:T(1,128)}, u32[]{:S(2)}) copy-start(f32[1,32768]{1,0:T(1,128)} %param.16) | copy-start | bytes 393220

commit v7 on v6

--- a/solution.py
+++ b/solution.py
@@ -17,7 +17,7 @@
 M_X, M_Y, M_Z = 2 * GRID_X, 2 * GRID_Y, 2 * GRID_Z - 1
 BINS = 256
 SPREAD_GROUP, READ_GROUP = 32, 32
-TABLES = 7
+TABLES = 8
 SLOTS = (1, 2, 3, 4, 5, 6, 0)
 
 f32, bf16 = jnp.float32, jnp.bfloat16
@@ -234,7 +234,7 @@
 
 
 def plane_kernel(
-    lengths, received, along_x, back_x, along_y, back_y, sine_x, sines, rim, out, tiles, x_hi, x_lo, spectrum
+    received, along_x, back_x, along_y, back_y, sine_x, sines, rim, lengths, out, tiles, x_hi, x_lo, spectrum
 ):
     last_column = (iota((DEVICES, CELLS), 1) & 31) == COLUMNS - 1
     quarter = iota((DEVICES, OWN), 1) >> 5
@@ -242,11 +242,12 @@
 
     def filtering():
         yield
-        scale_x, scale_y = lengths[0] * lengths[0], lengths[1] * lengths[1]
+        length_x, length_y, length_z = (lengths[0:1, j : j + 1] for j in range(3))
+        scale_x, scale_y = length_x * length_x, length_y * length_y
         frequency = lax.axis_index("px") * N_PY + lax.axis_index("py")
         sine = jnp.where(iota((1, GRID_Z), 1) == frequency, sines[1:2, :GRID_Z], 0.0)
-        rest = 1.0 + lengths[2] * lengths[2] * jnp.sum(sine, axis=1, keepdims=True)
-        factor = 2.0 / (M_X * M_Y) * lengths[0] * lengths[1] * lengths[2]
+        rest = 1.0 + length_z * length_z * jnp.sum(sine, axis=1, keepdims=True)
+        factor = 2.0 / (M_X * M_Y) * length_x * length_y * length_z
         rows = rest + scale_x * sine_x[...]
         for j in range(M_Y // 128):
             lanes = slice(128 * j, 128 * (j + 1))
@@ -371,18 +372,17 @@
 
 VMEM = pl.BlockSpec(memory_space=pltpu.VMEM)
 HBM = pl.BlockSpec(memory_space=pltpu.HBM)
-SMEM = pl.BlockSpec(memory_space=pltpu.SMEM)
 
 
 def params():
     return pltpu.CompilerParams(vmem_limit_bytes=16 * 1024 * 1024)
 
 
-def filter_plane(lengths, received, tables):
+def filter_plane(received, tables):
     return pl.pallas_call(
         plane_kernel,
         out_shape=jax.ShapeDtypeStruct((4 * DEVICES, 128), f32),
-        in_specs=[SMEM] + [VMEM] * (1 + TABLES),
+        in_specs=[VMEM] * (1 + TABLES),
         out_specs=VMEM,
         scratch_shapes=[
             pltpu.VMEM((2, 2, DEVICES, OWN), f32),
@@ -392,7 +392,7 @@
         ],
         compiler_params=params(),
         name="plane",
-    )(lengths, received, *tables)
+    )(received, *tables)
 
 
 def on_device(solution, residual, direction, offsets, noise, bin_cells, lengths):
@@ -402,7 +402,7 @@
     index = jax.ShapeDtypeStruct((BINS, BIN), jnp.int32)
     block = jax.ShapeDtypeStruct((4 * DEVICES, 128), f32)
 
-    tables = plane_tables()
+    tables = (*plane_tables(), lengths.reshape(1, 3))
     by_tile = offsets.reshape(3, BINS, BIN).transpose(1, 0, 2)
     operands = [pltpu.with_memory_space_constraint(x, pltpu.HBM) for x in (d, by_tile, bin_cells, forward, *tables)]
 
@@ -427,7 +427,7 @@
     )(*operands)
     received = lax.all_to_all(blocks.reshape(DEVICES, 4, 128), ("px", "py"), 0, 0, tiled=True)
 
-    filtered = filter_plane(lengths, received.reshape(4 * DEVICES, 128), tables)
+    filtered = filter_plane(received.reshape(4 * DEVICES, 128), tables)
     returned = lax.all_to_all(filtered.reshape(DEVICES, 4, 128), ("px", "py"), 0, 0, tiled=True)
 
     image, sums = pl.pallas_call(

time: 92.5 us -> 91.3 us (0.987)
  no operation moved by 1% of the time
where the time goes in v7:
time: 91.3 us; the launch traced here: 91.2 us
  blocking collectives  80.3 us (88%)
  Pallas kernels  10.1 us (11%)
    all_to_all x1, blocking collectives, on_device(): lax.all_to_all(blocks.reshape(DEVICES, 4, 128), ('px', 'py'), 0, 0, tiled...  36 us
    all_to_all x1, blocking collectives, on_device(): lax.all_to_all(filtered.reshape(DEVICES, 4, 128), ('px', 'py'), 0, 0, til...  26 us
    all_to_all x1, blocking collectives, on_device(): lax.all_to_all(sums.reshape(DEVICES, 1, BIN), ('px', 'py'), 0, 0, tiled=T...  18.3 us
    pallas_call x1, Pallas kernels, on_device(): pl.pallas_call(spread_kernel, out_shape=(block, jax.ShapeDtypeStruct((3,...  3.85 us
    pallas_call x1, Pallas kernels, filter_plane(): pl.pallas_call(plane_kernel, out_shape=jax.ShapeDtypeStruct((4 * DEVICES,...  2.88 us
    pallas_call x1, Pallas kernels, on_device(): pl.pallas_call(gather_kernel, out_shape=(point, jax.ShapeDtypeStruct((DEV...  2.51 us

profile of v7, /device:TPU:1, one launch (start us, length us, event | category | flops | bytes accessed | tf_op | source)
XLA Modules:
  0.0 91.2 jit_solution(11246635986688585729)
XLA Ops:
  0.6 3.8 %spread.1 = (f32[1024,128]{1,0:T(8,128)S(1)}, f32[3,256,128]{2,1,0:T(8,128)S(1)}, s32[256,128]{1,0:T(8,128)S(1)}, s32[256,128]{1,0:T(8,128)S(1)}, bf16[256,512]{...) custom-call(f32[256,128]{1,0:T(8,128)} %bitcast.22, ...), custom_call_target="tpu_custom_call" | custom-call | tf_op jit(solution)/shard_map/spread/pallas_call | solution.py:409
  4.5 36.0 %all_to_all.15 = f32[256,4,128]{2,1,0:T(4,128)S(1)} all-to-all(f32[256,4,128]{2,1,0:T(4,128)S(1)} %bitcast.28), channel_id=1, replica_groups=mesh['px'=32,'py'=8] {'px','py'}, dimensions={0} | all-to-all | bytes 1048576 | tf_op jit(solution)/shard_map/all_to_all | solution.py:428
  40.5 2.9 %plane.1 = f32[1024,128]{1,0:T(8,128)S(1)} custom-call(f32[1024,128]{1,0:T(8,128)S(1)} %bitcast.19, bf16[256,512]{1,0:T(8,128)(2,1)S(1)} %get-tuple-element.21.along_x, bf16[256,512]{1,0:T(8,128)(2,1)S(1)} %get-tuple-element.22.back_x, bf16[256,1024]{1,0:T(8,128)(2,1)S(1)} %get-tuple-element.23.along_y, bf16[512,512]{1,0:T(8,128)(2,1)S(1)} %get-tuple-element.24.back_y, ...), custom_call_target="tpu_custom_call" | custom-call | tf_op jit(solution)/shard_map/plane/pallas_call | solution.py:382
  43.3 0.0 copy-start
  43.3 0.0 copy-start.1
  43.4 0.0 copy-start.2
  43.4 0.0 copy-start.3
  43.4 26.0 %all_to_all.16 = f32[256,4,128]{2,1,0:T(4,128)S(1)} all-to-all(f32[256,4,128]{2,1,0:T(4,128)S(1)} %bitcast.20), channel_id=1, replica_groups=mesh['px'=32,'py'=8] {'px','py'}, dimensions={0} | all-to-all | bytes 1048576 | tf_op jit(solution)/shard_map/all_to_all | solution.py:431
  69.4 0.0 copy-done
  69.4 0.0 copy-done.1
  69.4 0.0 copy-done.2
  69.4 0.0 copy-done.3
  69.4 2.5 %interpolate.1 = (f32[256,128]{1,0:T(8,128)S(1)}, f32[256,128]{1,0:T(8,128)S(1)}) custom-call(f32[1024,128]{1,0:T(8,128)S(1)} %bitcast.21, f32[256,128]{1,0:T(8,128)S(1)} %bitcast.23, f32[256,128]{1,0:T(8,128)S(1)} %bitcast.25, f32[256,128]{1,0:T(8,128)S(1)} %bitcast.29, f32[3,256,128]{2,1,0:T(8,128)S(1)} %get-tuple-element.29.offsets, ...), custom_call_target="tpu_custom_call" | custom-call | tf_op jit(solution)/shard_map/interpolate/pallas_call | solution.py:433
  71.9 0.0 copy-start.4
  71.9 18.3 %all_to_all.17 = f32[256,1,128]{2,1,0:T(1,128)S(1)} all-to-all(f32[256,1,128]{2,1,0:T(1,128)S(1)} %bitcast.31), channel_id=1, replica_groups=mesh['px'=32,'py'=8] {'px','py'}, dimensions={0} | all-to-all | bytes 262144 | tf_op jit(solution)/shard_map/all_to_all | solution.py:443
  90.2 0.0 copy-done.4
  90.2 0.9 %step.1 = (f32[256,128]{1,0:T(8,128)}, f32[256,128]{1,0:T(8,128)}, f32[256,128]{1,0:T(8,128)}) custom-call(f32[256,128]{1,0:T(8,128)S(1)} %bitcast.27, f32[256,128]{1,0:T(8,128)S(1)} %bitcast.30, f32[256,128]{1,0:T(8,128)S(1)} %bitcast.26, f32[256,128]{1,0:T(8,128)S(1)} %bitcast.24, f32[256,128]{1,0:T(8,128)S(1)} %get-tuple-element.33.image), custom_call_target="tpu_custom_call" | custom-call | tf_op jit(solution)/shard_map/step/pallas_call | solution.py:444
Async XLA Ops:
  43.3 26.0 %copy-start = (f32[1,32768]{1,0:T(1,128)S(1)}, f32[1,32768]{1,0:T(1,128)}, u32[]{:S(2)}) copy-start(f32[1,32768]{1,0:T(1,128)} %param.18) | copy-start | bytes 393220
  43.3 26.0 %copy-start.1 = (f32[1,32768]{1,0:T(1,128)S(1)}, f32[1,32768]{1,0:T(1,128)}, u32[]{:S(2)}) copy-start(f32[1,32768]{1,0:T(1,128)} %param.17) | copy-start | bytes 393220
  43.4 26.0 %copy-start.2 = (bf16[256,1024]{1,0:T(8,128)(2,1)S(1)}, bf16[256,1024]{1,0:T(8,128)(2,1)}, u32[]{:S(2)}) copy-start(bf16[256,1024]{1,0:T(8,128)(2,1)} %constant.26.clone.inverse) | copy-start | bytes 1572868
  43.4 26.0 %copy-start.3 = (f32[32768]{0:T(1024)S(1)}, f32[32768]{0:T(1024)}, u32[]{:S(2)}) copy-start(f32[32768]{0:T(1024)} %param.20) | copy-start | bytes 393220
  71.9 18.3 %copy-start.4 = (f32[1,32768]{1,0:T(1,128)S(1)}, f32[1,32768]{1,0:T(1,128)}, u32[]{:S(2)}) copy-start(f32[1,32768]{1,0:T(1,128)} %param.16) | copy-start | bytes 393220

commit v8 on v7

--- a/solution.py
+++ b/solution.py
@@ -16,7 +16,7 @@
 CELLS, OWN, RIM = 256, 128, 64
 M_X, M_Y, M_Z = 2 * GRID_X, 2 * GRID_Y, 2 * GRID_Z - 1
 BINS = 256
-SPREAD_GROUP, READ_GROUP = 32, 32
+SPREAD_GROUP, READ_GROUP = 16, 32
 TABLES = 8
 SLOTS = (1, 2, 3, 4, 5, 6, 0)
 
@@ -145,7 +145,7 @@
 ):
     tables_hbm, (out, offsets, base, depth), tables = refs[:TABLES], refs[TABLES : TABLES + 4], refs[TABLES + 4 : 2 * TABLES + 4]
     direction, cells, forward, q_hi, q_lo, sems = refs[2 * TABLES + 4 :]
-    group = SPREAD_GROUP
+    group, beside = SPREAD_GROUP, 64 // SPREAD_GROUP
     copies = [
         pltpu.make_async_copy(cells_hbm, cells, sems.at[0]),
         pltpu.make_async_copy(direction_hbm, direction, sems.at[1]),
@@ -185,25 +185,30 @@
         yield
         placed = split(placed[: 4 * group] + placed[4 * group :])
         for f in range(4):
-            rows = slice((4 * (g // 2) + f) * 2 * group + g % 2 * group, (4 * (g // 2) + f) * 2 * group + (g % 2 + 1) * group)
-            q_hi[rows, :] = placed[0][f * group : (f + 1) * group]
-            q_lo[rows, :] = placed[1][f * group : (f + 1) * group]
-
-    def pair(p, found):
-        parts = [multiplied(2 * p), multiplied(2 * p + 1)]
+            start = (4 * (g // beside) + f) * beside * group + g % beside * group
+            q_hi[start : start + group, :] = placed[0][f * group : (f + 1) * group]
+            q_lo[start : start + group, :] = placed[1][f * group : (f + 1) * group]
+
+    def several(p, found):
+        parts = [multiplied(beside * p + j) for j in range(beside)]
         while parts:
             parts = [part for part in parts if next(part, 0) is None]
             yield
-        own = cells[2:3, 2 * p * group : 2 * (p + 1) * group]
+        own = cells[2:3, beside * p * group : beside * (p + 1) * group]
         own = jnp.concatenate([own + f - 1 for f in range(4)], 1)
-        at_depth = one_hot(iota((GRID_Z, 8 * group), 0) == own)
-        yield
-        rows = slice(8 * p * group, 8 * (p + 1) * group)
+        at_depth = one_hot(iota((GRID_Z, 4 * beside * group), 0) == own)
+        yield
+        rows = slice(4 * beside * p * group, 4 * beside * (p + 1) * group)
         found.append(dot(twice(at_depth), jnp.concatenate([q_hi[rows, :], q_lo[rows, :]], 0)))
         yield
 
     found = []
-    interleave([pair(p, found) for p in range(BINS // group // 2)])
+    running = [several(p, found) for p in range(BINS // group // beside)]
+    for turn in range(16):
+        for p, part in enumerate(running):
+            if turn >= p:
+                next(part, 0)
+
     gridded = split(sum(found))
     copies[5].wait()
     transformed = dot3((forward[:, :GRID_Z], forward[:, GRID_Z:]), gridded)
@@ -273,20 +278,31 @@
         x_hi[part, empty, :] = jnp.zeros((N_PX, GRID_Y), bf16)
         x_lo[part, empty, :] = jnp.zeros((N_PX, GRID_Y), bf16)
         yield
-        values = dot3((along_x[:, :DEVICES], along_x[:, DEVICES:]), (x_hi[part], x_lo[part]))
-        yield
-        values = split(values)
-        yield
-        values = dot3(values, (along_y[:, :M_Y], along_y[:, M_Y:]))
-        yield
-        values = split(values * spectrum[...])
-        yield
-        values = dot3(values, (back_y[:, :GRID_Y], back_y[:, GRID_Y:]))
-        yield
-        values = split(values)
-        yield
-        values = dot3((back_x[:, :M_X], back_x[:, M_X:]), values)
-        yield
+        found = []
+
+        def half(h):
+            rows = slice(h * M_X // 2, (h + 1) * M_X // 2)
+            values = dot3((along_x[rows, :DEVICES], along_x[rows, DEVICES:]), (x_hi[part], x_lo[part]))
+            yield
+            values = split(values)
+            yield
+            values = dot3(values, (along_y[:, :M_Y], along_y[:, M_Y:]))
+            yield
+            values = split(values * spectrum[rows, :])
+            yield
+            values = dot3(values, (back_y[:, :GRID_Y], back_y[:, GRID_Y:]))
+            yield
+            values = split(values)
+            yield
+            left = slice(rows.start + M_X, rows.stop + M_X)
+            found.append(dot3((back_x[:, rows], back_x[:, left]), values))
+            yield
+
+        parts = [half(0), half(1)]
+        while parts:
+            parts = [p for p in parts if next(p, 0) is None]
+            yield
+        values = sum(found)
         for py in range(N_PY):
             lanes = slice(128 * (py // 4), 128 * (py // 4 + 1))
             pieces = [[None] * 4, [None] * 4]

time: 91.3 us -> 91 us (level)
  no operation moved by 1% of the time
where the time goes in v8:
time: 91 us; the launch traced here: 90.8 us
  blocking collectives  80.3 us (88%)
  Pallas kernels  9.79 us (11%)
    all_to_all x1, blocking collectives, on_device(): lax.all_to_all(blocks.reshape(DEVICES, 4, 128), ('px', 'py'), 0, 0, tiled...  36 us
    all_to_all x1, blocking collectives, on_device(): lax.all_to_all(filtered.reshape(DEVICES, 4, 128), ('px', 'py'), 0, 0, til...  26 us
    all_to_all x1, blocking collectives, on_device(): lax.all_to_all(sums.reshape(DEVICES, 1, BIN), ('px', 'py'), 0, 0, tiled=T...  18.3 us
    pallas_call x1, Pallas kernels, on_device(): pl.pallas_call(spread_kernel, out_shape=(block, jax.ShapeDtypeStruct((3,...  3.56 us
    pallas_call x1, Pallas kernels, filter_plane(): pl.pallas_call(plane_kernel, out_shape=jax.ShapeDtypeStruct((4 * DEVICES,...  2.81 us
    pallas_call x1, Pallas kernels, on_device(): pl.pallas_call(gather_kernel, out_shape=(point, jax.ShapeDtypeStruct((DEV...  2.51 us

profile of v8, /device:TPU:1, one launch (start us, length us, event | category | flops | bytes accessed | tf_op | source)
XLA Modules:
  0.0 90.8 jit_solution(15760830366111941739)
XLA Ops:
  0.6 3.6 %spread.1 = (f32[1024,128]{1,0:T(8,128)S(1)}, f32[3,256,128]{2,1,0:T(8,128)S(1)}, s32[256,128]{1,0:T(8,128)S(1)}, s32[256,128]{1,0:T(8,128)S(1)}, bf16[256,512]{...) custom-call(f32[256,128]{1,0:T(8,128)} %bitcast.22, ...), custom_call_target="tpu_custom_call" | custom-call | tf_op jit(solution)/shard_map/spread/pallas_call | solution.py:425
  4.2 36.0 %all_to_all.15 = f32[256,4,128]{2,1,0:T(4,128)S(1)} all-to-all(f32[256,4,128]{2,1,0:T(4,128)S(1)} %bitcast.28), channel_id=1, replica_groups=mesh['px'=32,'py'=8] {'px','py'}, dimensions={0} | all-to-all | bytes 1048576 | tf_op jit(solution)/shard_map/all_to_all | solution.py:444
  40.2 2.8 %plane.1 = f32[1024,128]{1,0:T(8,128)S(1)} custom-call(f32[1024,128]{1,0:T(8,128)S(1)} %bitcast.19, bf16[256,512]{1,0:T(8,128)(2,1)S(1)} %get-tuple-element.21.along_x, bf16[256,512]{1,0:T(8,128)(2,1)S(1)} %get-tuple-element.22.back_x, bf16[256,1024]{1,0:T(8,128)(2,1)S(1)} %get-tuple-element.23.along_y, bf16[512,512]{1,0:T(8,128)(2,1)S(1)} %get-tuple-element.24.back_y, ...), custom_call_target="tpu_custom_call" | custom-call | tf_op jit(solution)/shard_map/plane/pallas_call | solution.py:398
  43.0 0.0 copy-start
  43.0 0.0 copy-start.1
  43.0 0.0 copy-start.2
  43.0 0.0 copy-start.3
  43.0 26.0 %all_to_all.16 = f32[256,4,128]{2,1,0:T(4,128)S(1)} all-to-all(f32[256,4,128]{2,1,0:T(4,128)S(1)} %bitcast.20), channel_id=1, replica_groups=mesh['px'=32,'py'=8] {'px','py'}, dimensions={0} | all-to-all | bytes 1048576 | tf_op jit(solution)/shard_map/all_to_all | solution.py:447
  69.0 0.0 copy-done
  69.0 0.0 copy-done.1
  69.0 0.0 copy-done.2
  69.0 0.0 copy-done.3
  69.0 2.5 %interpolate.1 = (f32[256,128]{1,0:T(8,128)S(1)}, f32[256,128]{1,0:T(8,128)S(1)}) custom-call(f32[1024,128]{1,0:T(8,128)S(1)} %bitcast.21, f32[256,128]{1,0:T(8,128)S(1)} %bitcast.23, f32[256,128]{1,0:T(8,128)S(1)} %bitcast.25, f32[256,128]{1,0:T(8,128)S(1)} %bitcast.29, f32[3,256,128]{2,1,0:T(8,128)S(1)} %get-tuple-element.29.offsets, ...), custom_call_target="tpu_custom_call" | custom-call | tf_op jit(solution)/shard_map/interpolate/pallas_call | solution.py:449
  71.6 0.0 copy-start.4
  71.6 18.3 %all_to_all.17 = f32[256,1,128]{2,1,0:T(1,128)S(1)} all-to-all(f32[256,1,128]{2,1,0:T(1,128)S(1)} %bitcast.31), channel_id=1, replica_groups=mesh['px'=32,'py'=8] {'px','py'}, dimensions={0} | all-to-all | bytes 262144 | tf_op jit(solution)/shard_map/all_to_all | solution.py:459
  89.9 0.0 copy-done.4
  89.9 0.9 %step.1 = (f32[256,128]{1,0:T(8,128)}, f32[256,128]{1,0:T(8,128)}, f32[256,128]{1,0:T(8,128)}) custom-call(f32[256,128]{1,0:T(8,128)S(1)} %bitcast.27, f32[256,128]{1,0:T(8,128)S(1)} %bitcast.30, f32[256,128]{1,0:T(8,128)S(1)} %bitcast.26, f32[256,128]{1,0:T(8,128)S(1)} %bitcast.24, f32[256,128]{1,0:T(8,128)S(1)} %get-tuple-element.33.image), custom_call_target="tpu_custom_call" | custom-call | tf_op jit(solution)/shard_map/step/pallas_call | solution.py:460
Async XLA Ops:
  43.0 26.0 %copy-start = (f32[1,32768]{1,0:T(1,128)S(1)}, f32[1,32768]{1,0:T(1,128)}, u32[]{:S(2)}) copy-start(f32[1,32768]{1,0:T(1,128)} %param.18) | copy-start | bytes 393220
  43.0 26.0 %copy-start.1 = (f32[1,32768]{1,0:T(1,128)S(1)}, f32[1,32768]{1,0:T(1,128)}, u32[]{:S(2)}) copy-start(f32[1,32768]{1,0:T(1,128)} %param.17) | copy-start | bytes 393220
  43.0 26.0 %copy-start.2 = (bf16[256,1024]{1,0:T(8,128)(2,1)S(1)}, bf16[256,1024]{1,0:T(8,128)(2,1)}, u32[]{:S(2)}) copy-start(bf16[256,1024]{1,0:T(8,128)(2,1)} %constant.26.clone.inverse) | copy-start | bytes 1572868
  43.0 26.0 %copy-start.3 = (f32[32768]{0:T(1024)S(1)}, f32[32768]{0:T(1024)}, u32[]{:S(2)}) copy-start(f32[32768]{0:T(1024)} %param.20) | copy-start | bytes 393220
  71.6 18.3 %copy-start.4 = (f32[1,32768]{1,0:T(1,128)S(1)}, f32[1,32768]{1,0:T(1,128)}, u32[]{:S(2)}) copy-start(f32[1,32768]{1,0:T(1,128)} %param.16) | copy-start | bytes 393220

commit v9 on v8

--- a/solution.py
+++ b/solution.py
@@ -183,7 +183,8 @@
         yield
         placed = dot(patches, cells)
         yield
-        placed = split(placed[: 4 * group] + placed[4 * group :])
+        placed = placed.astype(bf16)
+        placed = placed[: 4 * group], placed[4 * group :]
         for f in range(4):
             start = (4 * (g // beside) + f) * beside * group + g % beside * group
             q_hi[start : start + group, :] = placed[0][f * group : (f + 1) * group]
@@ -211,12 +212,11 @@
 
     gridded = split(sum(found))
     copies[5].wait()
-    transformed = dot3((forward[:, :GRID_Z], forward[:, GRID_Z:]), gridded)
     for part in range(2):
+        rows = slice(part * GRID_Z, (part + 1) * GRID_Z)
+        transformed = dot3((forward[rows, :GRID_Z], forward[rows, GRID_Z:]), gridded)
         for half in range(2):
-            out[pl.ds(2 * part + half, GRID_Z, stride=4), :] = transformed[
-                part * GRID_Z : (part + 1) * GRID_Z, half * 128 : (half + 1) * 128
-            ]
+            out[pl.ds(2 * part + half, GRID_Z, stride=4), :] = transformed[:, half * 128 : (half + 1) * 128]
     for copy in copies[6:]:
         copy.wait()
 
@@ -241,8 +241,8 @@
 def plane_kernel(
     received, along_x, back_x, along_y, back_y, sine_x, sines, rim, lengths, out, tiles, x_hi, x_lo, spectrum
 ):
-    last_column = (iota((DEVICES, CELLS), 1) & 31) == COLUMNS - 1
-    quarter = iota((DEVICES, OWN), 1) >> 5
+    rim_lane = iota((DEVICES, OWN), 1) & 31
+    before = rim_lane == 3 * ((rim_lane * 11) >> 5)
     place = ((0, 0), (0, 1), (0, 2), (0, 3), (1, 0), (1, 1), (1, 3))
 
     def filtering():
@@ -261,12 +261,12 @@
 
     def plane(part):
         own, rest = (received[pl.ds(2 * part + half, DEVICES, stride=4), :] for half in range(2))
-        rims = dot(jnp.concatenate(split(rest), 0), rim[...])
+        to_owner = jnp.where(before, moved(rest, -1), moved(rest, 1))
+        rims = dot(jnp.concatenate(split(to_owner), 0), rim[...])
         yield
         columns = rims[:DEVICES] + rims[DEVICES:]
-        columns = jnp.where(last_column, moved(columns, -1), moved(columns, 1))
         tiles[part, 0] = own + columns[:, :OWN]
-        tiles[part, 1] = jnp.where(quarter == 2, 0.0, rest) + columns[:, OWN:]
+        tiles[part, 1] = rest + columns[:, OWN:]
         loaded = [[tiles[part, tile, pl.ds(py, N_PX, stride=N_PY), :] for py in range(N_PY)] for tile in range(2)]
         for slot, (tile, q) in enumerate(place):
             rows = slice(slot * N_PX, (slot + 1) * N_PX)
@@ -293,7 +293,6 @@
             values = dot3(values, (back_y[:, :GRID_Y], back_y[:, GRID_Y:]))
             yield
             values = split(values)
-            yield
             left = slice(rows.start + M_X, rows.stop + M_X)
             found.append(dot3((back_x[:, rows], back_x[:, left]), values))
             yield
@@ -312,12 +311,13 @@
                 tiles[part, tile, pl.ds(py, N_PX, stride=N_PY), :] = by_quarter(pieces[tile])
         own, rest = tiles[part, 0], tiles[part, 1]
         out[pl.ds(2 * part, DEVICES, stride=4), :] = own
-        region = jnp.concatenate([own, rest], 1)
-        region = jnp.concatenate(split(jnp.where(last_column, moved(region, 1), moved(region, -1))), 0)
+        region = jnp.concatenate(split(jnp.concatenate([own, rest], 1)), 0)
         yield
         rims = dot_nt(region, rim[...])
         yield
-        out[pl.ds(2 * part + 1, DEVICES, stride=4), :] = rest + rims[:DEVICES] + rims[DEVICES:]
+        rims = rims[:DEVICES] + rims[DEVICES:]
+        rims = jnp.where(before, moved(rims, 1), moved(rims, -1))
+        out[pl.ds(2 * part + 1, DEVICES, stride=4), :] = rest + rims
 
     interleave([plane(0), plane(1), filtering()])
 

time: 91 us -> 90.9 us (level)
  no operation moved by 1% of the time
where the time goes in v9:
time: 90.9 us; the launch traced here: 90.7 us
  blocking collectives  80.3 us (88%)
  Pallas kernels  9.67 us (11%)
    all_to_all x1, blocking collectives, on_device(): lax.all_to_all(blocks.reshape(DEVICES, 4, 128), ('px', 'py'), 0, 0, tiled...  36 us
    all_to_all x1, blocking collectives, on_device(): lax.all_to_all(filtered.reshape(DEVICES, 4, 128), ('px', 'py'), 0, 0, til...  26 us
    all_to_all x1, blocking collectives, on_device(): lax.all_to_all(sums.reshape(DEVICES, 1, BIN), ('px', 'py'), 0, 0, tiled=T...  18.3 us
    pallas_call x1, Pallas kernels, on_device(): pl.pallas_call(spread_kernel, out_shape=(block, jax.ShapeDtypeStruct((3,...  3.51 us
    pallas_call x1, Pallas kernels, filter_plane(): pl.pallas_call(plane_kernel, out_shape=jax.ShapeDtypeStruct((4 * DEVICES,...  2.74 us
    pallas_call x1, Pallas kernels, on_device(): pl.pallas_call(gather_kernel, out_shape=(point, jax.ShapeDtypeStruct((DEV...  2.51 us

profile of v9, /device:TPU:1, one launch (start us, length us, event | category | flops | bytes accessed | tf_op | source)
XLA Modules:
  0.0 90.7 jit_solution(5964341767402281196)
XLA Ops:
  0.6 3.5 %spread.1 = (f32[1024,128]{1,0:T(8,128)S(1)}, f32[3,256,128]{2,1,0:T(8,128)S(1)}, s32[256,128]{1,0:T(8,128)S(1)}, s32[256,128]{1,0:T(8,128)S(1)}, bf16[256,512]{...) custom-call(f32[256,128]{1,0:T(8,128)} %bitcast.22, ...), custom_call_target="tpu_custom_call" | custom-call | tf_op jit(solution)/shard_map/spread/pallas_call | solution.py:425
  4.1 36.0 %all_to_all.15 = f32[256,4,128]{2,1,0:T(4,128)S(1)} all-to-all(f32[256,4,128]{2,1,0:T(4,128)S(1)} %bitcast.28), channel_id=1, replica_groups=mesh['px'=32,'py'=8] {'px','py'}, dimensions={0} | all-to-all | bytes 1048576 | tf_op jit(solution)/shard_map/all_to_all | solution.py:444
  40.1 2.7 %plane.1 = f32[1024,128]{1,0:T(8,128)S(1)} custom-call(f32[1024,128]{1,0:T(8,128)S(1)} %bitcast.19, bf16[256,512]{1,0:T(8,128)(2,1)S(1)} %get-tuple-element.21.along_x, bf16[256,512]{1,0:T(8,128)(2,1)S(1)} %get-tuple-element.22.back_x, bf16[256,1024]{1,0:T(8,128)(2,1)S(1)} %get-tuple-element.23.along_y, bf16[512,512]{1,0:T(8,128)(2,1)S(1)} %get-tuple-element.24.back_y, ...), custom_call_target="tpu_custom_call" | custom-call | tf_op jit(solution)/shard_map/plane/pallas_call | solution.py:398
  42.9 0.0 copy-start
  42.9 0.0 copy-start.1
  42.9 0.0 copy-start.2
  42.9 0.0 copy-start.3
  42.9 26.0 %all_to_all.16 = f32[256,4,128]{2,1,0:T(4,128)S(1)} all-to-all(f32[256,4,128]{2,1,0:T(4,128)S(1)} %bitcast.20), channel_id=1, replica_groups=mesh['px'=32,'py'=8] {'px','py'}, dimensions={0} | all-to-all | bytes 1048576 | tf_op jit(solution)/shard_map/all_to_all | solution.py:447
  68.9 0.0 copy-done
  68.9 0.0 copy-done.1
  68.9 0.0 copy-done.2
  68.9 0.0 copy-done.3
  68.9 2.5 %interpolate.1 = (f32[256,128]{1,0:T(8,128)S(1)}, f32[256,128]{1,0:T(8,128)S(1)}) custom-call(f32[1024,128]{1,0:T(8,128)S(1)} %bitcast.21, f32[256,128]{1,0:T(8,128)S(1)} %bitcast.23, f32[256,128]{1,0:T(8,128)S(1)} %bitcast.25, f32[256,128]{1,0:T(8,128)S(1)} %bitcast.29, f32[3,256,128]{2,1,0:T(8,128)S(1)} %get-tuple-element.29.offsets, ...), custom_call_target="tpu_custom_call" | custom-call | tf_op jit(solution)/shard_map/interpolate/pallas_call | solution.py:449
  71.4 0.0 copy-start.4
  71.5 18.3 %all_to_all.17 = f32[256,1,128]{2,1,0:T(1,128)S(1)} all-to-all(f32[256,1,128]{2,1,0:T(1,128)S(1)} %bitcast.31), channel_id=1, replica_groups=mesh['px'=32,'py'=8] {'px','py'}, dimensions={0} | all-to-all | bytes 262144 | tf_op jit(solution)/shard_map/all_to_all | solution.py:459
  89.8 0.0 copy-done.4
  89.8 0.9 %step.1 = (f32[256,128]{1,0:T(8,128)}, f32[256,128]{1,0:T(8,128)}, f32[256,128]{1,0:T(8,128)}) custom-call(f32[256,128]{1,0:T(8,128)S(1)} %bitcast.27, f32[256,128]{1,0:T(8,128)S(1)} %bitcast.30, f32[256,128]{1,0:T(8,128)S(1)} %bitcast.26, f32[256,128]{1,0:T(8,128)S(1)} %bitcast.24, f32[256,128]{1,0:T(8,128)S(1)} %get-tuple-element.33.image), custom_call_target="tpu_custom_call" | custom-call | tf_op jit(solution)/shard_map/step/pallas_call | solution.py:460
Async XLA Ops:
  42.9 26.0 %copy-start = (f32[1,32768]{1,0:T(1,128)S(1)}, f32[1,32768]{1,0:T(1,128)}, u32[]{:S(2)}) copy-start(f32[1,32768]{1,0:T(1,128)} %param.18) | copy-start | bytes 393220
  42.9 26.0 %copy-start.1 = (f32[1,32768]{1,0:T(1,128)S(1)}, f32[1,32768]{1,0:T(1,128)}, u32[]{:S(2)}) copy-start(f32[1,32768]{1,0:T(1,128)} %param.17) | copy-start | bytes 393220
  42.9 26.0 %copy-start.2 = (bf16[256,1024]{1,0:T(8,128)(2,1)S(1)}, bf16[256,1024]{1,0:T(8,128)(2,1)}, u32[]{:S(2)}) copy-start(bf16[256,1024]{1,0:T(8,128)(2,1)} %constant.26.clone.inverse) | copy-start | bytes 1572868
  42.9 26.0 %copy-start.3 = (f32[32768]{0:T(1024)S(1)}, f32[32768]{0:T(1024)}, u32[]{:S(2)}) copy-start(f32[32768]{0:T(1024)} %param.20) | copy-start | bytes 393220
  71.4 18.3 %copy-start.4 = (f32[1,32768]{1,0:T(1,128)S(1)}, f32[1,32768]{1,0:T(1,128)}, u32[]{:S(2)}) copy-start(f32[1,32768]{1,0:T(1,128)} %param.16) | copy-start | bytes 393220

commit v10 on v9

--- a/solution.py
+++ b/solution.py
@@ -246,7 +246,6 @@
     place = ((0, 0), (0, 1), (0, 2), (0, 3), (1, 0), (1, 1), (1, 3))
 
     def filtering():
-        yield
         length_x, length_y, length_z = (lengths[0:1, j : j + 1] for j in range(3))
         scale_x, scale_y = length_x * length_x, length_y * length_y
         frequency = lax.axis_index("px") * N_PY + lax.axis_index("py")
@@ -258,6 +257,7 @@
             lanes = slice(128 * j, 128 * (j + 1))
             denominator = rows + scale_y * sines[0:1, lanes]
             spectrum[:, lanes] = factor / (denominator * denominator)
+        yield
 
     def plane(part):
         own, rest = (received[pl.ds(2 * part + half, DEVICES, stride=4), :] for half in range(2))
@@ -319,7 +319,7 @@
         rims = jnp.where(before, moved(rims, 1), moved(rims, -1))
         out[pl.ds(2 * part + 1, DEVICES, stride=4), :] = rest + rims
 
-    interleave([plane(0), plane(1), filtering()])
+    interleave([filtering(), plane(0), plane(1)])
 
 
 def gather_kernel(received, direction, residual, noise, offsets, base, depth, inverse, image, sums, v_hi, v_lo):

time: 90.9 us -> 90.9 us (level)
  no operation moved by 1% of the time
where the time goes in v10:
time: 90.9 us; the launch traced here: 90.7 us
  blocking collectives  80.3 us (88%)
  Pallas kernels  9.66 us (11%)
    all_to_all x1, blocking collectives, on_device(): lax.all_to_all(blocks.reshape(DEVICES, 4, 128), ('px', 'py'), 0, 0, tiled...  36 us
    all_to_all x1, blocking collectives, on_device(): lax.all_to_all(filtered.reshape(DEVICES, 4, 128), ('px', 'py'), 0, 0, til...  26 us
    all_to_all x1, blocking collectives, on_device(): lax.all_to_all(sums.reshape(DEVICES, 1, BIN), ('px', 'py'), 0, 0, tiled=T...  18.3 us
    pallas_call x1, Pallas kernels, on_device(): pl.pallas_call(spread_kernel, out_shape=(block, jax.ShapeDtypeStruct((3,...  3.51 us
    pallas_call x1, Pallas kernels, filter_plane(): pl.pallas_call(plane_kernel, out_shape=jax.ShapeDtypeStruct((4 * DEVICES,...  2.73 us
    pallas_call x1, Pallas kernels, on_device(): pl.pallas_call(gather_kernel, out_shape=(point, jax.ShapeDtypeStruct((DEV...  2.51 us

profile of v10, /device:TPU:1, one launch (start us, length us, event | category | flops | bytes accessed | tf_op | source)
XLA Modules:
  0.0 90.7 jit_solution(7669578737839111751)
XLA Ops:
  0.6 3.5 %spread.1 = (f32[1024,128]{1,0:T(8,128)S(1)}, f32[3,256,128]{2,1,0:T(8,128)S(1)}, s32[256,128]{1,0:T(8,128)S(1)}, s32[256,128]{1,0:T(8,128)S(1)}, bf16[256,512]{...) custom-call(f32[256,128]{1,0:T(8,128)} %bitcast.22, ...), custom_call_target="tpu_custom_call" | custom-call | tf_op jit(solution)/shard_map/spread/pallas_call | solution.py:425
  4.1 36.0 %all_to_all.15 = f32[256,4,128]{2,1,0:T(4,128)S(1)} all-to-all(f32[256,4,128]{2,1,0:T(4,128)S(1)} %bitcast.28), channel_id=1, replica_groups=mesh['px'=32,'py'=8] {'px','py'}, dimensions={0} | all-to-all | bytes 1048576 | tf_op jit(solution)/shard_map/all_to_all | solution.py:444
  40.1 2.7 %plane.1 = f32[1024,128]{1,0:T(8,128)S(1)} custom-call(f32[1024,128]{1,0:T(8,128)S(1)} %bitcast.19, bf16[256,512]{1,0:T(8,128)(2,1)S(1)} %get-tuple-element.21.along_x, bf16[256,512]{1,0:T(8,128)(2,1)S(1)} %get-tuple-element.22.back_x, bf16[256,1024]{1,0:T(8,128)(2,1)S(1)} %get-tuple-element.23.along_y, bf16[512,512]{1,0:T(8,128)(2,1)S(1)} %get-tuple-element.24.back_y, ...), custom_call_target="tpu_custom_call" | custom-call | tf_op jit(solution)/shard_map/plane/pallas_call | solution.py:398
  42.9 0.0 copy-start
  42.9 0.0 copy-start.1
  42.9 0.0 copy-start.2
  42.9 0.0 copy-start.3
  42.9 26.0 %all_to_all.16 = f32[256,4,128]{2,1,0:T(4,128)S(1)} all-to-all(f32[256,4,128]{2,1,0:T(4,128)S(1)} %bitcast.20), channel_id=1, replica_groups=mesh['px'=32,'py'=8] {'px','py'}, dimensions={0} | all-to-all | bytes 1048576 | tf_op jit(solution)/shard_map/all_to_all | solution.py:447
  68.9 0.0 copy-done
  68.9 0.0 copy-done.1
  68.9 0.0 copy-done.2
  68.9 0.0 copy-done.3
  68.9 2.5 %interpolate.1 = (f32[256,128]{1,0:T(8,128)S(1)}, f32[256,128]{1,0:T(8,128)S(1)}) custom-call(f32[1024,128]{1,0:T(8,128)S(1)} %bitcast.21, f32[256,128]{1,0:T(8,128)S(1)} %bitcast.23, f32[256,128]{1,0:T(8,128)S(1)} %bitcast.25, f32[256,128]{1,0:T(8,128)S(1)} %bitcast.29, f32[3,256,128]{2,1,0:T(8,128)S(1)} %get-tuple-element.29.offsets, ...), custom_call_target="tpu_custom_call" | custom-call | tf_op jit(solution)/shard_map/interpolate/pallas_call | solution.py:449
  71.4 0.0 copy-start.4
  71.4 18.3 %all_to_all.17 = f32[256,1,128]{2,1,0:T(1,128)S(1)} all-to-all(f32[256,1,128]{2,1,0:T(1,128)S(1)} %bitcast.31), channel_id=1, replica_groups=mesh['px'=32,'py'=8] {'px','py'}, dimensions={0} | all-to-all | bytes 262144 | tf_op jit(solution)/shard_map/all_to_all | solution.py:459
  89.7 0.0 copy-done.4
  89.8 0.9 %step.1 = (f32[256,128]{1,0:T(8,128)}, f32[256,128]{1,0:T(8,128)}, f32[256,128]{1,0:T(8,128)}) custom-call(f32[256,128]{1,0:T(8,128)S(1)} %bitcast.27, f32[256,128]{1,0:T(8,128)S(1)} %bitcast.30, f32[256,128]{1,0:T(8,128)S(1)} %bitcast.26, f32[256,128]{1,0:T(8,128)S(1)} %bitcast.24, f32[256,128]{1,0:T(8,128)S(1)} %get-tuple-element.33.image), custom_call_target="tpu_custom_call" | custom-call | tf_op jit(solution)/shard_map/step/pallas_call | solution.py:460
Async XLA Ops:
  42.9 26.0 %copy-start = (f32[1,32768]{1,0:T(1,128)S(1)}, f32[1,32768]{1,0:T(1,128)}, u32[]{:S(2)}) copy-start(f32[1,32768]{1,0:T(1,128)} %param.18) | copy-start | bytes 393220
  42.9 26.0 %copy-start.1 = (f32[1,32768]{1,0:T(1,128)S(1)}, f32[1,32768]{1,0:T(1,128)}, u32[]{:S(2)}) copy-start(f32[1,32768]{1,0:T(1,128)} %param.17) | copy-start | bytes 393220
  42.9 26.0 %copy-start.2 = (bf16[256,1024]{1,0:T(8,128)(2,1)S(1)}, bf16[256,1024]{1,0:T(8,128)(2,1)}, u32[]{:S(2)}) copy-start(bf16[256,1024]{1,0:T(8,128)(2,1)} %constant.26.clone.inverse) | copy-start | bytes 1572868
  42.9 26.0 %copy-start.3 = (f32[32768]{0:T(1024)S(1)}, f32[32768]{0:T(1024)}, u32[]{:S(2)}) copy-start(f32[32768]{0:T(1024)} %param.20) | copy-start | bytes 393220
  71.4 18.3 %copy-start.4 = (f32[1,32768]{1,0:T(1,128)S(1)}, f32[1,32768]{1,0:T(1,128)}, u32[]{:S(2)}) copy-start(f32[1,32768]{1,0:T(1,128)} %param.16) | copy-start | bytes 393220
